TPU v7x, 32 devices: a whole 2x2x4 slice. The times are simulated.
32 devices in a mesh: grp: 8 (over z, x), dp: 4 (over y, core).
Axes of the slice: x: 2, y: 2, z: 4, core: 2. Of those that a mesh axis runs over, the one named last changes fastest.
Arguments:
- queries: bfloat16 [4096, 4096], P(('grp', 'dp')), may hold values from -1.25 to 1.25
- documents: bfloat16 [4096, 4096], P(('grp', 'dp')), may hold values from -0.75 to 0.75
- positives: int32 [4096], P(('grp', 'dp')), may hold values from 0 to 127, as said below
- inner_owner: int32 [8, 512, 1], P('grp'), may hold values from 0 to 3; in each aligned block of 128 rows (0 to 127, 128 to 255, ..., all dimensions but the last counted through in order) at most 64 rows name the same one
- inner_row: int32 [8, 512, 1], P('grp'), may hold values from 0 to 127
- outer_owner: int32 [4, 8, 128, 1], P('dp'), may hold values from 0 to 6; in each aligned block of 128 rows (0 to 127, 128 to 255, ..., all dimensions but the last counted through in order) at most 36 rows name the same one
- outer_row: int32 [4, 8, 128, 1], P('dp'), may hold values from 0 to 127
Outputs:
- losses: float32 [4096], P(('grp', 'dp'))
- query_grads: bfloat16 [4096, 4096], P(('grp', 'dp'))
- doc_grads: bfloat16 [4096, 4096], P(('grp', 'dp'))
Inputs may be any that keep to these rules, and one draw needn't show every extreme that they name: `positives`: within each device's 128 queries every row of that device's documents is the positive of exactly one query. `inner_owner`: among the 128 queries of one device, no dp index is named by more than 64 of them, a bound that some block reaches. `outer_owner`: among the 128 queries of one device, no value is named by more than 36 of them, a bound that some block reaches.
All inputs are finite; a program needn't handle non-finite values.
Results may differ from a plain program's by a relative error of at most 0.0041.
Values may be sent and summed in bfloat16 or wider, within the bound.
No kernel may reach another device: no remote copies, remote signals or barrier semaphores. Data moves between devices by JAX's collectives and lax.ppermute only.
A program may use at most 64 MiB of HBM per device.

v0:
```python
import jax
import jax.numpy as jnp
from jax import lax
from jax.sharding import PartitionSpec as P


def slot_table(wanted, row_ids, capacity, doc_count):
    slot_rank = jnp.cumsum(wanted.astype(jnp.int32), axis=1) - 1
    slot_ids = jnp.arange(capacity, dtype=jnp.int32)
    chosen = wanted[:, None, :] & (slot_rank[:, None, :] == slot_ids[None, :, None])
    row_at = jnp.sum(jnp.where(chosen, row_ids[:, None, :], 0), axis=2)
    filled = jnp.any(chosen, axis=2)
    doc_ids = jnp.arange(doc_count, dtype=jnp.int32)
    indicator_matrix = (row_at[:, :, None] == doc_ids[None, None, :]) & filled[:, :, None]
    return (indicator_matrix, row_at, filled)


def slot_filled(owners, peer_count, capacity):
    peer_ids = jnp.arange(peer_count, dtype=jnp.int32)
    counts = jnp.sum((owners[None, :] == peer_ids[:, None]).astype(jnp.int32), axis=1)
    return (jnp.arange(capacity, dtype=jnp.int32)[None, :] < counts[:, None]).reshape(-1)


def collect_slot_index(documents, row_at, filled):
    picked = jnp.take(documents, row_at.reshape(-1), axis=0)
    picked = jnp.where(filled.reshape(-1, 1), picked, jnp.zeros_like(picked))
    return picked.reshape(row_at.shape + (documents.shape[1],))


def add_returned(indicator_matrix, sent_back_rows):
    return jnp.einsum(
        "mna,mnu->au",
        indicator_matrix.astype(jnp.bfloat16),
        sent_back_rows,
        preferred_element_type=jnp.float32,
    )


def against(left, right):
    return lax.dot_general(
        left, right, (((1,), (1,)), ((), ())), preferred_element_type=jnp.float32
    )


def across(left, right):
    return lax.dot_general(
        left, right, (((0,), (0,)), ((), ())), preferred_element_type=jnp.float32
    )


def per_device(queries, documents, positives, inner_owner, inner_row, outer_owner, outer_row):
    tok_rows, embedding_width = queries.shape
    dp_count = lax.axis_size("dp")
    grp_count = lax.axis_size("grp")
    cap_inner = max(2, 2 * tok_rows // dp_count)
    cap_outer = max(2, 2 * tok_rows // (grp_count - 1))
    my_column = lax.axis_index("dp")
    my_group = lax.axis_index("grp")
    inner_owners = inner_owner.reshape(dp_count, tok_rows)
    inner_rows = inner_row.reshape(dp_count, tok_rows)
    group_ids = jnp.arange(grp_count, dtype=jnp.int32)
    outer_groups = (group_ids[:, None] + 1 + outer_owner.reshape(grp_count, tok_rows)) % grp_count
    outer_rows = outer_row.reshape(grp_count, tok_rows)
    inner_onehot, inner_at, inner_full = slot_table(
        inner_owners == my_column, inner_rows, cap_inner, tok_rows
    )
    outer_onehot, outer_at, outer_full = slot_table(
        outer_groups == my_group, outer_rows, cap_outer, tok_rows
    )
    send_inner = collect_slot_index(documents, inner_at, inner_full)
    send_outer = collect_slot_index(documents, outer_at, outer_full)
    received_inner_rows = lax.all_to_all(send_inner, "dp", split_axis=0, concat_axis=0, tiled=True)
    fetched_outer = lax.all_to_all(send_outer, "grp", split_axis=0, concat_axis=0, tiled=True)
    inner_live = slot_filled(
        lax.dynamic_index_in_dim(inner_owners, my_column, 0, keepdims=False), dp_count, cap_inner
    )
    outer_live = slot_filled(
        lax.dynamic_index_in_dim(outer_groups, my_group, 0, keepdims=False), grp_count, cap_outer
    )
    flat_inner = received_inner_rows.reshape(-1, embedding_width)
    flat_outer = fetched_outer.reshape(-1, embedding_width)
    scores = 3.0 * jnp.concatenate(
        [against(queries, documents), against(queries, flat_inner), against(queries, flat_outer)],
        axis=1,
    )
    live_cols = jnp.concatenate([jnp.ones((tok_rows,), jnp.bool_), inner_live, outer_live])
    masked = jnp.where(live_cols[None, :], scores, -jnp.inf)
    row_max = jnp.max(masked, axis=1, keepdims=True)
    exp_scores = jnp.exp(masked - row_max)
    row_total = jnp.sum(exp_scores, axis=1, keepdims=True)
    column_ids = jnp.arange(scores.shape[1], dtype=jnp.int32)
    target = (column_ids[None, :] == positives[:, None]).astype(jnp.float32)
    losses = row_max[:, 0] + jnp.log(row_total[:, 0]) - jnp.sum(target * scores, axis=1)
    weights = (3.0 * (exp_scores / row_total - target)).astype(jnp.bfloat16)
    inner_count = dp_count * cap_inner
    local_w = weights[:, :tok_rows]
    inner_w = weights[:, tok_rows : tok_rows + inner_count]
    outer_w = weights[:, tok_rows + inner_count :]
    query_grads = jnp.dot(local_w, documents, preferred_element_type=jnp.float32)
    query_grads = query_grads + jnp.dot(inner_w, flat_inner, preferred_element_type=jnp.float32)
    query_grads = query_grads + jnp.dot(outer_w, flat_outer, preferred_element_type=jnp.float32)
    inner_slots = (
        across(inner_w, queries).astype(jnp.bfloat16).reshape(dp_count, cap_inner, embedding_width)
    )
    outer_slots = (
        across(outer_w, queries).astype(jnp.bfloat16).reshape(grp_count, cap_outer, embedding_width)
    )
    returned_inner = lax.all_to_all(inner_slots, "dp", split_axis=0, concat_axis=0, tiled=True)
    returned_outer = lax.all_to_all(outer_slots, "grp", split_axis=0, concat_axis=0, tiled=True)
    doc_grads = across(local_w, queries)
    doc_grads = doc_grads + add_returned(inner_onehot, returned_inner)
    doc_grads = doc_grads + add_returned(outer_onehot, returned_outer)
    return (losses, query_grads.astype(jnp.bfloat16), doc_grads.astype(jnp.bfloat16))


def solution(mesh):
    return jax.shard_map(
        per_device,
        mesh=mesh,
        in_specs=(
            P(("grp", "dp"), None),
            P(("grp", "dp"), None),
            P(("grp", "dp")),
            P("grp", None, None),
            P("grp", None, None),
            P("dp", None, None, None),
            P("dp", None, None, None),
        ),
        out_specs=(P(("grp", "dp")), P(("grp", "dp"), None), P(("grp", "dp"), None)),
        check_vma=False,
    )
```

profile of v0, /device:TPU:3, one launch (start us, length us, event | category | flops | bytes accessed | tf_op | source)
XLA Modules:
  0.0 215.0 jit_solution(12194662466521258576)
XLA Ops:
  2.8 6.6 %gather_fusion = bf16[256,4096]{1,0:T(8,128)(2,1)} fusion(bf16[128,4096]{1,0:T(8,128)(2,1)} %param.8, s32[1024]{0:T(1024)S(1)} %pad_clamp_fusion.1), kind=kCustom, calls=%fused_computation | custom fusion | bytes 4195328 | tf_op jit(solution)/shard_map/jit(_take)/gather | solution.py:25
  9.4 3.2 %select_select_fusion.1 = bf16[4,64,4096]{2,1,0:T(8,128)(2,1)} fusion(bf16[4,64,4096]{2,1,0:T(8,128)(2,1)} %bitcast.34, pred[4,64]{1,0:T(4,128)(4,1)S(1)} %compare_and_fusion.1, pred[4,64]{1,0:T(4,128)(4,1)S(1)} %fusion.9), kind=kLoop, calls=%fused_computation.13 | loop fusion | flops 2097152 | bytes 4194816 | tf_op jit(solution)/shard_map/jit(_where)/select_n | solution.py:26
  12.7 5.2 %all-to-all-start = ((bf16[4,64,4096]{2,1,0:T(8,128)(2,1)}), bf16[4,64,4096]{2,1,0:T(8,128)(2,1)}, u32[]{:S(2)}, u32[]{:S(2)}) async-start(bf16[4,64,4096]{2,1,0:T(8,128)(2,1)} %select_select_fusion.1), calls=%async_computation | async-start | bytes 4194304 | tf_op jit(solution)/shard_map/all_to_all | solution.py:72
  19.1 3.8 %gather_fusion.1 = bf16[288,4096]{1,0:T(8,128)(2,1)} fusion(bf16[128,4096]{1,0:T(8,128)(2,1)S(1)} %copy-done.1, s32[1024]{0:T(1024)S(1)} %pad_clamp_fusion), kind=kCustom, calls=%fused_computation.1 | custom fusion | bytes 4719744 | tf_op jit(solution)/shard_map/jit(_take)/gather | solution.py:25
  22.9 4.1 %gather.15 = bf16[8,36,4096]{2,1,0:T(8,128)(2,1)} reshape(bf16[288,4096]{1,0:T(8,128)(2,1)} %gather_fusion.1) | data formatting | bytes 4718592 | tf_op jit(solution)/shard_map/jit(_take)/gather | solution.py:25
  27.9 3.7 %select_select_fusion = bf16[8,36,4096]{2,1,0:T(8,128)(2,1)} fusion(bf16[8,36,4096]{2,1,0:T(8,128)(2,1)} %gather.15, pred[8,36]{1,0:T(8,128)(4,1)S(1)} %copy.15, pred[8,36]{1,0:T(8,128)(4,1)S(1)} %copy.14), kind=kLoop, calls=%fused_computation.12 | loop fusion | flops 2359296 | bytes 4719168 | tf_op jit(solution)/shard_map/jit(_where)/select_n | solution.py:26
  31.6 11.2 %all-to-all-done = bf16[4,64,4096]{2,1,0:T(8,128)(2,1)} async-done(((bf16[4,64,4096]{2,1,0:T(8,128)(2,1)}), bf16[4,64,4096]{2,1,0:T(8,128)(2,1)}, u32[]{:S(2)}, u32[]{:S(2)}) %all-to-all-start) | async-done | bytes 2097184 | tf_op jit(solution)/shard_map/all_to_all | solution.py:72
  42.8 5.8 %all-to-all-start.1 = ((bf16[8,36,4096]{2,1,0:T(8,128)(2,1)}), bf16[8,36,4096]{2,1,0:T(8,128)(2,1)}, u32[]{:S(2)}, u32[]{:S(2)}) async-start(bf16[8,36,4096]{2,1,0:T(8,128)(2,1)} %select_select_fusion), calls=%async_computation.1 | async-start | bytes 5242880 | tf_op jit(solution)/shard_map/all_to_all | solution.py:73
  50.3 2.3 %convolution_bitcast_fusion.3 = f32[128,256]{0,1:T(8,128)S(1)} fusion(bf16[256,4096]{1,0:T(8,128)(2,1)} %bitcast.7, bf16[128,4096]{1,0:T(8,128)(2,1)S(1)} %copy-done), kind=kOutput, calls=%fused_computation.15 | convolution fusion | flops 268435456 | bytes 3276800 | tf_op jit(solution)/shard_map/dot_general | solution.py:40
  52.6 54.8 %all-to-all-done.1 = bf16[8,36,4096]{2,1,0:T(8,128)(2,1)} async-done(((bf16[8,36,4096]{2,1,0:T(8,128)(2,1)}), bf16[8,36,4096]{2,1,0:T(8,128)(2,1)}, u32[]{:S(2)}, u32[]{:S(2)}) %all-to-all-start.1) | async-done | bytes 2359328 | tf_op jit(solution)/shard_map/all_to_all | solution.py:73
  107.4 4.1 %reshape.232 = bf16[288,4096]{1,0:T(8,128)(2,1)} reshape(bf16[8,36,4096]{2,1,0:T(8,128)(2,1)} %all-to-all-done.1) | data formatting | bytes 4718592 | tf_op jit(solution)/shard_map/reshape | solution.py:81
  111.5 2.4 %convolution_bitcast_fusion.2 = f32[128,288]{0,1:T(8,128)S(1)} fusion(bf16[288,4096]{1,0:T(8,128)(2,1)} %reshape.232, bf16[128,4096]{1,0:T(8,128)(2,1)S(1)} %copy-done), kind=kOutput, calls=%fused_computation.14 | convolution fusion | flops 301989888 | bytes 3555328 | tf_op jit(solution)/shard_map/dot_general | solution.py:40
  114.5 2.0 convolution_convert_fusion.1
  116.5 5.9 %all-to-all-start.2 = ((bf16[4,64,4096]{2,1,0:T(8,128)(2,1)}), bf16[4,64,4096]{2,1,0:T(8,128)(2,1)}, u32[]{:S(2)}, u32[]{:S(2)}) async-start(bf16[4,64,4096]{2,1,0:T(8,128)(2,1)} %bitcast.35), calls=%async_computation.2 | async-start | bytes 4194304 | tf_op jit(solution)/shard_map/all_to_all | solution.py:108
  122.4 2.3 %convolution_convert_fusion = bf16[288,4096]{1,0:T(8,128)(2,1)} fusion(bf16[128,4096]{1,0:T(8,128)(2,1)S(1)} %copy-done, bf16[128,672]{0,1:T(8,128)(2,1)S(1)} %multiply_convert_fusion), kind=kOutput, calls=%fused_computation.2 | convolution fusion | flops 303169536 | bytes 3481600 | tf_op jit(solution)/shard_map/dot_general | solution.py:46
  124.7 4.1 %reshape.234 = bf16[8,36,4096]{2,1,0:T(8,128)(2,1)} reshape(bf16[288,4096]{1,0:T(8,128)(2,1)} %convolution_convert_fusion) | data formatting | bytes 4718592 | tf_op jit(solution)/shard_map/reshape | solution.py:106
  128.8 18.5 %all-to-all-done.2 = bf16[4,64,4096]{2,1,0:T(8,128)(2,1)} async-done(((bf16[4,64,4096]{2,1,0:T(8,128)(2,1)}), bf16[4,64,4096]{2,1,0:T(8,128)(2,1)}, u32[]{:S(2)}, u32[]{:S(2)}) %all-to-all-start.2) | async-done | bytes 2097184 | tf_op jit(solution)/shard_map/all_to_all | solution.py:108
  147.3 4.6 %all-to-all-start.3 = ((bf16[8,36,4096]{2,1,0:T(8,128)(2,1)}), bf16[8,36,4096]{2,1,0:T(8,128)(2,1)}, u32[]{:S(2)}, u32[]{:S(2)}) async-start(bf16[8,36,4096]{2,1,0:T(8,128)(2,1)} %reshape.234), calls=%async_computation.3 | async-start | bytes 5242880 | tf_op jit(solution)/shard_map/all_to_all | solution.py:109
  152.9 2.3 %convolution_add_fusion.2 = f32[128,4096]{1,0:T(8,128)S(1)} fusion(f32[128,4096]{1,0:T(8,128)S(1)} %fusion.21, bf16[256,4096]{1,0:T(8,128)(2,1)} %bitcast.7, bf16[128,672]{0,1:T(8,128)(2,1)S(1)} %multiply_convert_fusion), kind=kOutput, calls=%fused_computation.9 | convolution fusion | flops 268959744 | bytes 6356992 | tf_op jit(solution)/shard_map/dot_general | solution.py:100
  155.2 1.7 fusion.1
  156.9 3.5 %convolution_bitcast_fusion.1 = f32[128,4096]{1,0:T(8,128)} fusion(bf16[4,64,4096]{2,1,0:T(8,128)(2,1)} %all-to-all-done.2, s32[4,64]{1,0:T(4,128)S(1)} %select_reduce_fusion.3, pred[4,64]{1,0:T(4,128)(4,1)S(1)} %fusion.9), kind=kOutput, calls=%fused_computation.5 | convolution fusion | flops 268500992 | bytes 4195584 | tf_op jit(solution)/shard_map/mna,mnu->au/dot_general | solution.py:31
  160.4 50.3 %all-to-all-done.3 = bf16[8,36,4096]{2,1,0:T(8,128)(2,1)} async-done(((bf16[8,36,4096]{2,1,0:T(8,128)(2,1)}), bf16[8,36,4096]{2,1,0:T(8,128)(2,1)}, u32[]{:S(2)}, u32[]{:S(2)}) %all-to-all-start.3) | async-done | bytes 2359328 | tf_op jit(solution)/shard_map/all_to_all | solution.py:109
  210.7 2.8 %convolution_bitcast_fusion = f32[128,4096]{1,0:T(8,128)S(1)} fusion(bf16[8,36,4096]{2,1,0:T(8,128)(2,1)} %all-to-all-done.3, s32[8,36]{1,0:T(8,128)S(1)} %copy.16, pred[8,36]{1,0:T(8,128)(4,1)S(1)} %copy.14), kind=kOutput, calls=%fused_computation.4 | convolution fusion | flops 302063616 | bytes 4457888 | tf_op jit(solution)/shard_map/mna,mnu->au/dot_general | solution.py:31
  213.5 1.5 fusion.2
  (52 shorter events, 7.6 us)
Async XLA Ops:
  0.6 49.2 %copy-start = (bf16[128,4096]{1,0:T(8,128)(2,1)S(1)}, bf16[128,4096]{1,0:T(8,128)(2,1)}, u32[]{:S(2)}) copy-start(bf16[128,4096]{1,0:T(8,128)(2,1)} %param.7) | copy-start | bytes 3145732
  12.7 5.2 %copy-start.4 = (s32[1,8,128,1]{2,3,1,0:T(1,128)S(1)}, s32[1,8,128,1]{2,3,1,0:T(1,128)}, u32[]{:S(2)}) copy-start(s32[1,8,128,1]{2,3,1,0:T(1,128)} %param.12) | copy-start | bytes 12292
  12.7 5.6 %copy-start.5 = (s32[1,8,128,1]{2,3,1,0:T(1,128)S(1)}, s32[1,8,128,1]{2,3,1,0:T(1,128)}, u32[]{:S(2)}) copy-start(s32[1,8,128,1]{2,3,1,0:T(1,128)} %param.13) | copy-start | bytes 12292
  12.7 6.5 %copy-start.1 = (bf16[128,4096]{1,0:T(8,128)(2,1)S(1)}, bf16[128,4096]{1,0:T(8,128)(2,1)}, u32[]{:S(2)}) copy-start(bf16[128,4096]{1,0:T(8,128)(2,1)} %param.8) | copy-start | bytes 3145732
  12.7 30.1 %all-to-all-start = ((bf16[4,64,4096]{2,1,0:T(8,128)(2,1)}), bf16[4,64,4096]{2,1,0:T(8,128)(2,1)}, u32[]{:S(2)}, u32[]{:S(2)}) async-start(bf16[4,64,4096]{2,1,0:T(8,128)(2,1)} %select_select_fusion.1), calls=%async_computation | async-start | bytes 4194304 | tf_op jit(solution)/shard_map/all_to_all | solution.py:72
  42.8 64.6 %all-to-all-start.1 = ((bf16[8,36,4096]{2,1,0:T(8,128)(2,1)}), bf16[8,36,4096]{2,1,0:T(8,128)(2,1)}, u32[]{:S(2)}, u32[]{:S(2)}) async-start(bf16[8,36,4096]{2,1,0:T(8,128)(2,1)} %select_select_fusion), calls=%async_computation.1 | async-start | bytes 5242880 | tf_op jit(solution)/shard_map/all_to_all | solution.py:73
  111.5 2.6 %copy-start.6 = (s32[128]{0:T(128)S(1)}, s32[128]{0:T(128)}, u32[]{:S(2)}) copy-start(s32[128]{0:T(128)} %param.9) | copy-start | bytes 1540
  116.5 30.8 %all-to-all-start.2 = ((bf16[4,64,4096]{2,1,0:T(8,128)(2,1)}), bf16[4,64,4096]{2,1,0:T(8,128)(2,1)}, u32[]{:S(2)}, u32[]{:S(2)}) async-start(bf16[4,64,4096]{2,1,0:T(8,128)(2,1)} %bitcast.35), calls=%async_computation.2 | async-start | bytes 4194304 | tf_op jit(solution)/shard_map/all_to_all | solution.py:108
  147.3 63.4 %all-to-all-start.3 = ((bf16[8,36,4096]{2,1,0:T(8,128)(2,1)}), bf16[8,36,4096]{2,1,0:T(8,128)(2,1)}, u32[]{:S(2)}, u32[]{:S(2)}) async-start(bf16[8,36,4096]{2,1,0:T(8,128)(2,1)} %reshape.234), calls=%async_computation.3 | async-start | bytes 5242880 | tf_op jit(solution)/shard_map/all_to_all | solution.py:109
  152.9 2.3 %copy-start.2 = (bf16[288,4096]{1,0:T(8,128)(2,1)S(1)}, bf16[288,4096]{1,0:T(8,128)(2,1)}, u32[]{:S(2)}) copy-start(bf16[288,4096]{1,0:T(8,128)(2,1)} %reshape.232) | copy-start | bytes 7077892
  210.7 2.8 %copy-start.3 = (f32[128,4096]{1,0:T(8,128)S(1)}, f32[128,4096]{1,0:T(8,128)}, u32[]{:S(2)}) copy-start(f32[128,4096]{1,0:T(8,128)} %convolution_bitcast_fusion.1) | copy-start | bytes 6291460
where the time goes:
time: 218 us; the launch traced here: 215 us
  waiting for transfers between devices  135 us (62%)
  local copies, waits for them, and re-layouts  24.1 us (11%)
  matrix products  21.6 us (10%)
  starting transfers between devices  21.4 us (10%)
  other arithmetic  12.3 us (6%)
    all_to_all x1, waiting for transfers between devices, per_device(): lax.all_to_all(send_outer, 'grp', split_axis=0, concat_axis=0, tiled=True)  54.8 us
    all_to_all x1, waiting for transfers between devices, per_device(): lax.all_to_all(outer_slots, 'grp', split_axis=0, concat_axis=0, tiled=True)  50.3 us
    all_to_all x1, waiting for transfers between devices, per_device(): lax.all_to_all(inner_slots, 'dp', split_axis=0, concat_axis=0, tiled=True)  18.5 us
    gather x3, local copies, waits for them, and re-layouts, collect_slot_index(): picked = jnp.take(documents, row_at.reshape(-1), axis=0)  14.5 us
    all_to_all x1, waiting for transfers between devices, per_device(): lax.all_to_all(send_inner, 'dp', split_axis=0, concat_axis=0, tiled=True)  11.2 us
    select_n x2, other arithmetic, collect_slot_index(): picked = jnp.where(filled.reshape(-1, 1), picked, jnp.zeros_like(picked))  6.9 us
    dot_general x2, matrix products, add_returned(): jnp.einsum('mna,mnu->au', indicator_matrix.astype(jnp.bfloat16), sent_bac...  6.3 us
    all_to_all x1, starting transfers between devices, per_device(): lax.all_to_all(inner_slots, 'dp', split_axis=0, concat_axis=0, tiled=True)  5.87 us
  transfers between devices with their start and end apart: 4, of which 4 were waited for; matrix products, arithmetic and copies ran while one was open for 15% of the time, Pallas kernels for 0%

commit v1 on v0

v1 whole, which is shorter than its diff:
```python
import functools

import jax
import jax.numpy as jnp
from jax import lax
from jax.experimental import pallas as pl
from jax.experimental.pallas import tpu as pltpu
from jax.sharding import PartitionSpec as P

SPLIT = 4
SCALE = 3.0
VMEM = pl.BlockSpec(memory_space=pltpu.VMEM)
f32, bf16, i32 = jnp.float32, jnp.bfloat16, jnp.int32


def call(kernel, out_shape, *args, scratch=(), flops=0):
    nbytes = sum(a.size * a.dtype.itemsize for a in (*args, *jax.tree.leaves(out_shape)))
    return pl.pallas_call(
        kernel,
        out_shape=out_shape,
        in_specs=[VMEM] * len(args),
        out_specs=jax.tree.map(lambda _: VMEM, out_shape),
        scratch_shapes=list(scratch),
        compiler_params=pltpu.CompilerParams(vmem_limit_bytes=32 * 2**20),
        cost_estimate=pl.CostEstimate(flops=flops, bytes_accessed=nbytes, transcendentals=0),
    )(*args)


def dot(a, b, dims=((1,), (0,))):
    return lax.dot_general(a, b, (dims, ((), ())), preferred_element_type=f32)


NT = ((1,), (1,))
TN = ((0,), (0,))


def row_plan(count, split):
    t = lax.broadcasted_iota(i32, (count * split, 128), 0)
    chunk = jnp.zeros_like(t)
    for c in range(1, split):
        chunk = chunk + (t >= c * count).astype(i32)
    return t - count * chunk, chunk


def stacked(ref, split):
    width = ref.shape[1] // split
    return jnp.concatenate([ref[:, c * width : (c + 1) * width] for c in range(split)], axis=0)


def spread(values, chunk, split):
    return jnp.concatenate([jnp.where(chunk == c, values, 0.0).astype(bf16) for c in range(split)], axis=1)


def slot_codes(owner_ref, codes, axis, relative):
    peers, rows = owner_ref.shape
    me = lax.axis_index(axis)
    if relative:
        name = lax.rem(me - lax.broadcasted_iota(i32, (peers, rows), 0) - 1 + 2 * peers, peers)
    else:
        name = me
    wanted = owner_ref[...] == name
    earlier = lax.broadcasted_iota(i32, (rows, rows), 0) < lax.broadcasted_iota(i32, (rows, rows), 1)
    rank = dot(wanted.astype(f32).astype(bf16), earlier.astype(f32).astype(bf16))
    codes[...] = jnp.where(wanted, rank, -1.0).astype(i32)


def slot_onehot(codes, row_ref, axis, shift, slot):
    peers = codes.shape[0]
    r = lax.rem(lax.axis_index(axis) + shift, peers)
    chosen = codes[pl.ds(r, 1), :] == slot
    at = jnp.sum(jnp.where(chosen, row_ref[pl.ds(r, 1), :] + 1, 0).astype(f32), axis=1, keepdims=True)
    ids = lax.broadcasted_iota(i32, slot.shape, 1) + 1
    return jnp.where(ids.astype(f32) == at, 1.0, 0.0)


def send_kernel(axis, relative, shifts, count, split, owner_ref, row_ref, docs_ref, *refs):
    *outs, codes = refs
    slot_codes(owner_ref, codes, axis, relative)
    slot, chunk = row_plan(count, split)
    docs = stacked(docs_ref, split)
    for shift, out in zip(shifts, outs):
        onehot = slot_onehot(codes, row_ref, axis, shift, slot)
        out[...] = dot(spread(onehot, chunk, split), docs).astype(bf16)


def live_count(owner_ref, me, name):
    hit = (owner_ref[pl.ds(me, 1), :] == name).astype(f32)
    return jnp.sum(hit, axis=1, keepdims=True).astype(i32)


def near_kernel(shifts, q_ref, docs_ref, owner_ref, row_ref, *refs):
    *blocks, own_out, mult_out, inner_out = refs
    peers = owner_ref.shape[0]
    me = lax.axis_index("dp")
    q = q_ref[...]
    own_out[...] = SCALE * dot(docs_ref[...], q, NT)
    rows = docs_ref.shape[0]
    named = (owner_ref[pl.ds(me, 1), :] == me) & (
        row_ref[pl.ds(me, 1), :] == lax.broadcasted_iota(i32, (rows, rows), 0)
    )
    mult = jnp.sum(named.astype(f32), axis=1, keepdims=True)
    mult_out[...] = jnp.broadcast_to(mult, (rows, rows))
    count = blocks[0].shape[0]
    for n, (shift, block) in enumerate(zip(shifts, blocks)):
        live = live_count(owner_ref, me, lax.rem(me - shift + peers, peers))
        scores = SCALE * dot(block[...], q, NT)
        slot = lax.broadcasted_iota(i32, scores.shape, 0)
        inner_out[n * count : (n + 1) * count, :] = jnp.where(slot < live, scores, -jnp.inf)


def main_kernel(shifts, count, split, q_ref, own_ref, mult_ref, inner_ref, pos_ref, owner_ref, *refs):
    nseg = len(shifts)
    blocks, refs = refs[:nseg], refs[nseg:]
    loss_out, own_w, inner_w, outer_w = refs[:4]
    grads = refs[4 : 4 + nseg]
    acc = refs[-1]
    peers = owner_ref.shape[0]
    me = lax.axis_index("grp")
    slot, chunk = row_plan(count, split)
    width = q_ref.shape[1] // split
    own, inner = own_ref[...], inner_ref[...]
    top = jnp.maximum(jnp.max(own, axis=0, keepdims=True), jnp.max(inner, axis=0, keepdims=True))
    size = count * split
    for n, (shift, block) in enumerate(zip(shifts, blocks)):
        part = jnp.zeros(slot.shape, f32)
        for c in range(split):
            part = jnp.where(chunk == c, dot(block[...], q_ref[:, c * width : (c + 1) * width], NT), part)
        scores = part
        for c in range(1, split):
            scores = scores + pltpu.roll(part, c * count, 0)
        live = live_count(owner_ref, me, peers - 1 - shift)
        scores = jnp.where(slot < live, SCALE * scores, -jnp.inf)
        acc[n * size : (n + 1) * size, :] = scores
        top = jnp.maximum(top, jnp.max(scores, axis=0, keepdims=True))
    own_e = (1.0 + mult_ref[...]) * jnp.exp(own - top)
    inner_e = jnp.exp(inner - top)
    total = jnp.sum(own_e, axis=0, keepdims=True) + jnp.sum(inner_e, axis=0, keepdims=True)
    for n in range(nseg):
        e = jnp.exp(acc[n * size : (n + 1) * size, :] - top)
        acc[n * size : (n + 1) * size, :] = e
        total = total + jnp.sum(jnp.where(chunk == 0, e, 0.0), axis=0, keepdims=True)
    factor = SCALE / total
    q = stacked(q_ref, split)
    for n in range(nseg):
        w = acc[n * size : (n + 1) * size, :] * factor
        outer_w[n * size : (n + 1) * size, :] = w.astype(bf16)
        grads[n][...] = dot(spread(w, chunk, split), q).astype(bf16)
    positive = (lax.broadcasted_iota(i32, own.shape, 0) == pos_ref[...]).astype(f32)
    loss_out[...] = top + jnp.log(total) - jnp.sum(positive * own, axis=0, keepdims=True)
    own_w[...] = (own_e * factor - SCALE * positive).astype(bf16)
    inner_w[...] = (inner_e * factor).astype(bf16)


def inner_grad_kernel(w_ref, q_ref, *outs):
    count = outs[0].shape[0]
    for n, out in enumerate(outs):
        out[...] = dot(w_ref[n * count : (n + 1) * count, :], q_ref[...]).astype(bf16)


def query_grad_kernel(n_inner, count, split, own_w, inner_w, outer_w, docs_ref, *refs):
    *blocks, out = refs
    inner, outer = blocks[:n_inner], blocks[n_inner:]
    _, chunk = row_plan(count, split)
    width = docs_ref.shape[1] // split
    size = count * split
    cap = inner[0].shape[0]
    for c in range(split):
        cols = slice(c * width, (c + 1) * width)
        acc = dot(own_w[...], docs_ref[:, cols], TN)
        for n, block in enumerate(inner):
            acc = acc + dot(inner_w[n * cap : (n + 1) * cap, :], block[:, cols], TN)
        for n, block in enumerate(outer):
            w = outer_w[n * size : (n + 1) * size, :].astype(f32)
            acc = acc + dot(jnp.where(chunk == c, w, 0.0).astype(bf16), block[...], TN)
        out[:, cols] = acc.astype(bf16)


def near_grad_kernel(shifts, own_w, q_ref, owner_ref, row_ref, *refs):
    *blocks, out, codes = refs
    slot_codes(owner_ref, codes, "dp", False)
    slot = lax.broadcasted_iota(i32, (blocks[0].shape[0], 128), 0)
    onehots = [slot_onehot(codes, row_ref, "dp", shift, slot).astype(bf16) for shift in shifts]
    width = q_ref.shape[1] // SPLIT
    for c in range(SPLIT):
        cols = slice(c * width, (c + 1) * width)
        acc = dot(own_w[...], q_ref[:, cols])
        for onehot, block in zip(onehots, blocks):
            acc = acc + dot(onehot, block[:, cols], TN)
        out[:, cols] = acc


def far_grad_kernel(shifts, count, split, near_ref, owner_ref, row_ref, *refs):
    *blocks, out, codes = refs
    slot_codes(owner_ref, codes, "grp", True)
    slot, chunk = row_plan(count, split)
    onehots = [slot_onehot(codes, row_ref, "grp", shift, slot) for shift in shifts]
    width = near_ref.shape[1] // split
    for c in range(split):
        cols = slice(c * width, (c + 1) * width)
        acc = near_ref[:, cols]
        for onehot, block in zip(onehots, blocks):
            acc = acc + dot(jnp.where(chunk == c, onehot, 0.0).astype(bf16), block[...], TN)
        out[:, cols] = acc.astype(bf16)


def shifted(block, axis, shift):
    size = lax.axis_size(axis)
    return lax.ppermute(block, axis, [(g, (g + shift) % size) for g in range(size)])


def per_device(queries, documents, positives, inner_owner, inner_row, outer_owner, outer_row):
    rows, width = queries.shape
    dp, grp = lax.axis_size("dp"), lax.axis_size("grp")
    cap_inner = -(-max(2, 2 * rows // dp) // 16) * 16
    cap_outer = -(-max(2, 2 * rows // (grp - 1)) // 4) * 4
    shape = jax.ShapeDtypeStruct
    in_shifts = list(range(1, dp))
    out_shifts = sorted(range(1, grp), key=lambda k: (abs(2 * k - grp), k))
    inner_owner, inner_row = inner_owner.reshape(dp, rows), inner_row.reshape(dp, rows)
    outer_owner, outer_row = outer_owner.reshape(grp, rows), outer_row.reshape(grp, rows)
    outer_block = shape((cap_outer * SPLIT, width // SPLIT), bf16)
    inner_block = shape((cap_inner, width), bf16)
    n_in, n_out = len(in_shifts), len(out_shifts)

    send_outer = call(
        functools.partial(send_kernel, "grp", True, out_shifts, cap_outer, SPLIT),
        [outer_block] * n_out,
        outer_owner, outer_row, documents,
        scratch=[pltpu.VMEM((grp, rows), i32)],
        flops=2 * n_out * cap_outer * SPLIT * rows * width,
    )
    got_outer = [shifted(b, "grp", k) for b, k in zip(send_outer, out_shifts)]
    send_inner = call(
        functools.partial(send_kernel, "dp", False, in_shifts, cap_inner, 1),
        [inner_block] * n_in,
        inner_owner, inner_row, documents,
        scratch=[pltpu.VMEM((dp, rows), i32)],
        flops=2 * n_in * cap_inner * rows * width,
    )
    got_inner = [shifted(b, "dp", k) for b, k in zip(send_inner, in_shifts)]
    own_scores, mult, inner_scores = call(
        functools.partial(near_kernel, in_shifts),
        [shape((rows, rows), f32), shape((rows, rows), f32), shape((n_in * cap_inner, rows), f32)],
        queries, documents, inner_owner, inner_row, *got_inner,
        flops=2 * (n_in * cap_inner + rows) * rows * width,
    )
    losses, own_w, inner_w, outer_w, *grads_outer = call(
        functools.partial(main_kernel, out_shifts, cap_outer, SPLIT),
        [
            shape((1, rows), f32),
            shape((rows, rows), bf16),
            shape((n_in * cap_inner, rows), bf16),
            shape((n_out * cap_outer * SPLIT, rows), bf16),
        ]
        + [outer_block] * n_out,
        queries, own_scores, mult, inner_scores, positives.reshape(1, rows), outer_owner, *got_outer,
        scratch=[pltpu.VMEM((n_out * cap_outer * SPLIT, rows), f32)],
        flops=4 * n_out * cap_outer * SPLIT * rows * width,
    )
    back_outer = [shifted(b, "grp", -k) for b, k in zip(grads_outer, out_shifts)]
    grads_inner = call(
        inner_grad_kernel, [inner_block] * n_in, inner_w, queries, flops=2 * n_in * cap_inner * rows * width
    )
    back_inner = [shifted(b, "dp", -k) for b, k in zip(grads_inner, in_shifts)]
    query_grads = call(
        functools.partial(query_grad_kernel, n_in, cap_outer, SPLIT),
        shape((rows, width), bf16),
        own_w, inner_w, outer_w, documents, *got_inner, *got_outer,
        flops=2 * (n_out * cap_outer * SPLIT + n_in * cap_inner + rows) * rows * width,
    )
    near_grads = call(
        functools.partial(near_grad_kernel, in_shifts),
        shape((rows, width), f32),
        own_w, queries, inner_owner, inner_row, *back_inner,
        scratch=[pltpu.VMEM((dp, rows), i32)],
        flops=2 * (n_in * cap_inner + rows) * rows * width,
    )
    doc_grads = call(
        functools.partial(far_grad_kernel, out_shifts, cap_outer, SPLIT),
        shape((rows, width), bf16),
        near_grads, outer_owner, outer_row, *back_outer,
        scratch=[pltpu.VMEM((grp, rows), i32)],
        flops=2 * n_out * cap_outer * SPLIT * rows * width,
    )
    return losses.reshape(rows), query_grads, doc_grads


def solution(mesh):
    return jax.shard_map(
        per_device,
        mesh=mesh,
        in_specs=(
            P(("grp", "dp"), None),
            P(("grp", "dp"), None),
            P(("grp", "dp")),
            P("grp", None, None),
            P("grp", None, None),
            P("dp", None, None, None),
            P("dp", None, None, None),
        ),
        out_specs=(P(("grp", "dp")), P(("grp", "dp"), None), P(("grp", "dp"), None)),
        check_vma=False,
    )
```

time: 218 us -> 135 us (0.62); the launches traced: 215 us -> 135 us
  waiting for transfers between devices: 135 us -> 70.8 us
  matrix products: 21.6 us -> 0 us
  starting transfers between devices: 21.4 us -> 41.1 us
  local copies, waits for them, and re-layouts: 24.1 us -> 5.22 us
  Pallas kernels: 0 us -> 17 us
  other arithmetic: 12.3 us -> 0 us
    all_to_all x4 -> x0, waiting for transfers between devices: 135 us -> none  [the longest x1 54.8 us: per_device(): lax.all_to_all(send_outer, 'grp', split_axis=0, concat_axis=0, tiled=True)]
    ppermute x0 -> x20, waiting for transfers between devices: none -> 70.8 us  [shifted(): lax.ppermute(block, axis, [(g, (g + shift) % size) for g in range(size)])]
    ppermute x0 -> x20, starting transfers between devices: none -> 41.1 us  [shifted(): lax.ppermute(block, axis, [(g, (g + shift) % size) for g in range(size)])]
    dot_general x11 -> x0, matrix products: 21.6 us -> none  [the longest x2 6.3 us: add_returned(): jnp.einsum('mna,mnu->au', indicator_matrix.astype(jnp.bfloat16), sent_bac...]
    all_to_all x4 -> x0, starting transfers between devices: 21.4 us -> none  [the longest x1 5.87 us: per_device(): lax.all_to_all(inner_slots, 'dp', split_axis=0, concat_axis=0, tiled=True)]
    pallas_call x0 -> x8, Pallas kernels: none -> 17 us  [call(): pl.pallas_call(kernel, out_shape=out_shape, in_specs=[VMEM] * len(args),...]
    gather x3 -> x0, local copies, waits for them, and re-layouts: 14.5 us -> none  [collect_slot_index(): picked = jnp.take(documents, row_at.reshape(-1), axis=0)]
    reshape x4 -> x0, local copies, waits for them, and re-layouts: 8.41 us -> none  [the longest x1 4.14 us: per_device(): across(outer_w, queries).astype(jnp.bfloat16)]
  transfers between devices with their start and end apart: 4 -> 20, of which waited for: 4 -> 6; matrix products, arithmetic and copies ran while one was open for 15% -> 0% of each run, Pallas kernels for 0% -> 6%
where the time goes in v1:
time: 135 us
  waiting for transfers between devices  70.8 us (52%)
  starting transfers between devices  41.1 us (30%)
  Pallas kernels  17 us (13%)
  local copies, waits for them, and re-layouts  5.22 us (4%)
    ppermute x20, waiting for transfers between devices, shifted(): lax.ppermute(block, axis, [(g, (g + shift) % size) for g in range(size)])  70.8 us
    ppermute x20, starting transfers between devices, shifted(): lax.ppermute(block, axis, [(g, (g + shift) % size) for g in range(size)])  41.1 us
    pallas_call x8, Pallas kernels, call(): pl.pallas_call(kernel, out_shape=out_shape, in_specs=[VMEM] * len(args),...  17 us
    unnamed x26, local copies, waits for them, and re-layouts  5.22 us
  transfers between devices with their start and end apart: 20, of which 6 were waited for; matrix products, arithmetic and copies ran while one was open for 0% of the time, Pallas kernels for 6%

profile of v1, /device:TPU:3, one launch (start us, length us, event | category | flops | bytes accessed | tf_op | source)
XLA Modules:
  0.0 134.8 jit_solution(10475533148417718796)
XLA Ops:
  0.6 1.2 copy-done
  4.0 1.9 %collective-permute-start = (bf16[64,4096]{1,0:T(8,128)(2,1)S(1)}, bf16[64,4096]{1,0:T(8,128)(2,1)S(1)}, u32[]{:S(2)}, u32[]{:S(2)}) collective-permute-start(bf16[64,4096]{1,0:T(8,128)(2,1)S(1)} %get-tuple-element.30), channel_id=1, source_target_pairs={{0,1},{1,2},{2,3},{3,0},{4,5},{5,6},{6,7},{7,4},{8,9},{9,10},{10,1... | collective-permute-start | bytes 1572872 | tf_op jit(solution)/shard_map/ppermute | solution.py:208
  6.4 1.2 copy-done.1
  9.0 1.4 %shard_map.96 = (bf16[144,1024]{1,0:T(8,128)(2,1)S(1)}, bf16[144,1024]{1,0:T(8,128)(2,1)S(1)}, bf16[144,1024]{1,0:T(8,128)(2,1)S(1)}, bf16[144,1024]{1,0:T(8,128...) custom-call(s32[8,128]{1,0:T(8,128)S(1)} %bitcast.12, ...), custom_call_target="tpu_custom_call" | custom-call | flops 1056964608 | bytes 3121152 | tf_op jit(solution)/shard_map/pallas_call | solution.py:18
  10.4 2.4 %collective-permute-start.3 = (bf16[144,1024]{1,0:T(8,128)(2,1)S(1)}, bf16[144,1024]{1,0:T(8,128)(2,1)S(1)}, u32[]{:S(2)}, u32[]{:S(2)}) collective-permute-start(bf16[144,1024]{1,0:T(8,128)(2,1)S(1)} %get-tuple-element.36), channel_id=1, source_target_pairs={{0,16},{4,20},{8,24},{12,28},{16,0},{20,4},{24,8},{28,12},{1,17},{... | collective-permute-start | bytes 884744 | tf_op jit(solution)/shard_map/ppermute | solution.py:208
  12.8 19.0 %collective-permute-done.3.refs_0_.refs_3_ = bf16[144,1024]{1,0:T(8,128)(2,1)S(1)} collective-permute-done((bf16[144,1024]{1,0:T(8,128)(2,1)S(1)}, bf16[144,1024]{1,0:T(8,128)(2,1)S(1)}, u32[]{:S(2)}, u32[]{:S(2)}) %collective-permute-start.3) | collective-permute-done | bytes 294944 | tf_op jit(solution)/shard_map/ppermute | solution.py:208
  31.9 14.1 %collective-permute-start.6 = (bf16[144,1024]{1,0:T(8,128)(2,1)S(1)}, bf16[144,1024]{1,0:T(8,128)(2,1)S(1)}, u32[]{:S(2)}, u32[]{:S(2)}) collective-permute-start(bf16[144,1024]{1,0:T(8,128)(2,1)S(1)} %get-tuple-element.39), channel_id=1, source_target_pairs={{0,8},{4,12},{8,16},{12,20},{16,24},{20,28},{24,0},{28,4},{1,9},{5... | collective-permute-start | bytes 884744 | tf_op jit(solution)/shard_map/ppermute | solution.py:208
  46.1 4.0 %collective-permute-start.9 = (bf16[144,1024]{1,0:T(8,128)(2,1)S(1)}, bf16[144,1024]{1,0:T(8,128)(2,1)S(1)}, u32[]{:S(2)}, u32[]{:S(2)}) collective-permute-start(bf16[144,1024]{1,0:T(8,128)(2,1)S(1)} %get-tuple-element.42), channel_id=1, source_target_pairs={{0,28},{4,0},{8,4},{12,8},{16,12},{20,16},{24,20},{28,24},{1,29},{... | collective-permute-start | bytes 884744 | tf_op jit(solution)/shard_map/ppermute | solution.py:208
  50.1 1.5 %shard_map.95 = (f32[128,128]{1,0:T(8,128)S(1)}, f32[128,128]{1,0:T(8,128)S(1)}, f32[192,128]{1,0:T(8,128)S(1)}) custom-call(bf16[128,4096]{1,0:T(8,128)(2,1)S(1)} %copy-done.3, bf16[128,4096]{1,0:T(8,128)(2,1)S(1)} %copy-done.2, s32[4,128]{1,0:T(4,128)S(1)} %bitcast.7, s32[4,128]{1,0:T(4,128)S(1)} %bitcast.10, ...), custom_call_target="tpu_custom_call" | custom-call | flops 335544320 | bytes 3903488 | tf_op jit(solution)/shard_map/pallas_call | solution.py:18
  51.9 12.6 %collective-permute-done.7.refs_4_.refs_7_ = bf16[144,1024]{1,0:T(8,128)(2,1)S(1)} collective-permute-done((bf16[144,1024]{1,0:T(8,128)(2,1)S(1)}, bf16[144,1024]{1,0:T(8,128)(2,1)S(1)}, u32[]{:S(2)}, u32[]{:S(2)}) %collective-permute-start.7) | collective-permute-done | bytes 294944 | tf_op jit(solution)/shard_map/ppermute | solution.py:208
  64.6 3.7 %shard_map.97 = (f32[1,128]{1,0:T(1,128)}, bf16[128,128]{1,0:T(8,128)(2,1)S(1)}, bf16[192,128]{1,0:T(8,128)(2,1)S(1)}, bf16[1008,128]{1,0:T(8,128)(2,1)S(1)}, bf...) custom-call(bf16[128,4096]{1,0:T(8,128)(2,1)S(1)} %copy-done.3, ...), custom_call_target="tpu_custom_call" | custom-call | flops 2113929216 | bytes 5751808 | tf_op jit(solution)/shard_map/pallas_call | solution.py:18
  69.0 1.7 %collective-permute-start.10 = (bf16[64,4096]{1,0:T(8,128)(2,1)S(1)}, bf16[64,4096]{1,0:T(8,128)(2,1)S(1)}, u32[]{:S(2)}, u32[]{:S(2)}) collective-permute-start(bf16[64,4096]{1,0:T(8,128)(2,1)S(1)} %get-tuple-element.47), channel_id=1, source_target_pairs={{0,3},{1,0},{2,1},{3,2},{4,7},{5,4},{6,5},{7,6},{8,11},{9,8},{10,9... | collective-permute-start | bytes 1572872 | tf_op jit(solution)/shard_map/ppermute | solution.py:208
  70.6 1.2 collective-permute-start.11
  72.4 4.6 %collective-permute-start.13 = (bf16[144,1024]{1,0:T(8,128)(2,1)S(1)}, bf16[144,1024]{1,0:T(8,128)(2,1)S(1)}, u32[]{:S(2)}, u32[]{:S(2)}) collective-permute-start(bf16[144,1024]{1,0:T(8,128)(2,1)S(1)} %get-tuple-element.50), channel_id=1, source_target_pairs={{0,16},{4,20},{8,24},{12,28},{16,0},{20,4},{24,8},{28,12},{1,17},{... | collective-permute-start | bytes 884744 | tf_op jit(solution)/shard_map/ppermute | solution.py:208
  77.0 1.0 collective-permute-start.14
  78.0 12.6 %collective-permute-done.13.refs_0_ = bf16[144,1024]{1,0:T(8,128)(2,1)S(1)} collective-permute-done((bf16[144,1024]{1,0:T(8,128)(2,1)S(1)}, bf16[144,1024]{1,0:T(8,128)(2,1)S(1)}, u32[]{:S(2)}, u32[]{:S(2)}) %collective-permute-start.13) | collective-permute-done | bytes 294944 | tf_op jit(solution)/shard_map/ppermute | solution.py:208
  90.6 5.3 %collective-permute-start.15 = (bf16[144,1024]{1,0:T(8,128)(2,1)S(1)}, bf16[144,1024]{1,0:T(8,128)(2,1)S(1)}, u32[]{:S(2)}, u32[]{:S(2)}) collective-permute-start(bf16[144,1024]{1,0:T(8,128)(2,1)S(1)} %get-tuple-element.52), channel_id=1, source_target_pairs={{0,12},{4,16},{8,20},{12,24},{16,28},{20,0},{24,4},{28,8},{1,13},{... | collective-permute-start | bytes 884744 | tf_op jit(solution)/shard_map/ppermute | solution.py:208
  95.9 12.7 %collective-permute-done.14.refs_1_ = bf16[144,1024]{1,0:T(8,128)(2,1)S(1)} collective-permute-done((bf16[144,1024]{1,0:T(8,128)(2,1)S(1)}, bf16[144,1024]{1,0:T(8,128)(2,1)S(1)}, u32[]{:S(2)}, u32[]{:S(2)}) %collective-permute-start.14) | collective-permute-done | bytes 294944 | tf_op jit(solution)/shard_map/ppermute | solution.py:208
  108.7 1.5 %collective-permute-start.17 = (bf16[144,1024]{1,0:T(8,128)(2,1)S(1)}, bf16[144,1024]{1,0:T(8,128)(2,1)S(1)}, u32[]{:S(2)}, u32[]{:S(2)}) collective-permute-start(bf16[144,1024]{1,0:T(8,128)(2,1)S(1)} %get-tuple-element.54), channel_id=1, source_target_pairs={{0,8},{4,12},{8,16},{12,20},{16,24},{20,28},{24,0},{28,4},{1,9},{5... | collective-permute-start | bytes 884744 | tf_op jit(solution)/shard_map/ppermute | solution.py:208
  110.2 2.4 %collective-permute-start.19 = (bf16[144,1024]{1,0:T(8,128)(2,1)S(1)}, bf16[144,1024]{1,0:T(8,128)(2,1)S(1)}, u32[]{:S(2)}, u32[]{:S(2)}) collective-permute-start(bf16[144,1024]{1,0:T(8,128)(2,1)S(1)} %get-tuple-element.56), channel_id=1, source_target_pairs={{0,4},{4,8},{8,12},{12,16},{16,20},{20,24},{24,28},{28,0},{1,5},{5... | collective-permute-start | bytes 884744 | tf_op jit(solution)/shard_map/ppermute | solution.py:208
  112.5 4.2 %shard_map.98 = bf16[128,4096]{1,0:T(8,128)(2,1)} custom-call(bf16[128,128]{1,0:T(8,128)(2,1)S(1)} %get-tuple-element.44.own_w, bf16[192,128]{1,0:T(8,128)(2,1)S(1)} %get-tuple-element.45.inner_w.w_ref, bf16[1008,128]{1,0:T(8,128)(2,1)S(1)} %get-tuple-element.46.outer_w, bf16[128,4096]{1,0:T(8,128)(2,1)S(1)} %copy-done.2, ...), custom_call_target="tpu_custom_call" | custom-call | flops 1392508928 | bytes 6074368 | tf_op jit(solution)/shard_map/pallas_call | solution.py:18
  116.7 1.5 %shard_map.100.near_ref = f32[128,4096]{1,0:T(8,128)S(1)} custom-call(bf16[128,128]{1,0:T(8,128)(2,1)S(1)} %get-tuple-element.44.own_w, bf16[128,4096]{1,0:T(8,128)(2,1)S(1)} %copy-done.3, s32[4,128]{1,0:T(4,128)S(1)} %bitcast.8, s32[4,128]{1,0:T(4,128)S(1)} %bitcast.11, bf16[64,4096]{1,0:T(8,128)(2,1)S(1)} %collective-permute-done.10.refs_0_, ...), custom_call_target="tpu_custom_call" | custom-call | flops 335544320 | bytes 4755456 | tf_op jit(solution)/shard_map/pallas_call | solution.py:18
  118.2 13.3 %collective-permute-done.16.refs_3_ = bf16[144,1024]{1,0:T(8,128)(2,1)S(1)} collective-permute-done((bf16[144,1024]{1,0:T(8,128)(2,1)S(1)}, bf16[144,1024]{1,0:T(8,128)(2,1)S(1)}, u32[]{:S(2)}, u32[]{:S(2)}) %collective-permute-start.16) | collective-permute-done | bytes 294944 | tf_op jit(solution)/shard_map/ppermute | solution.py:208
  131.5 3.3 %shard_map.101 = bf16[128,4096]{1,0:T(8,128)(2,1)} custom-call(f32[128,4096]{1,0:T(8,128)S(1)} %shard_map.100.near_ref, s32[8,128]{1,0:T(8,128)S(1)} %bitcast.14, s32[8,128]{1,0:T(8,128)S(1)} %bitcast.16, bf16[144,1024]{1,0:T(8,128)(2,1)S(1)} %collective-permute-done.13.refs_0_, bf16[144,1024]{1,0:T(8,128)(2,1)S(1)} %collective-permute-done.14.refs_1_, ...), custom_call_target="tpu_custom_call" | custom-call | flops 1056964608 | bytes 5218304 | tf_op jit(solution)/shard_map/pallas_call | solution.py:18
  (50 shorter events, 5.6 us)
Async XLA Ops:
  3.2 46.9 %copy-start.2 = (bf16[128,4096]{1,0:T(8,128)(2,1)S(1)}, bf16[128,4096]{1,0:T(8,128)(2,1)}, u32[]{:S(2)}) copy-start(bf16[128,4096]{1,0:T(8,128)(2,1)} %docs_ref.7) | copy-start | bytes 3145732
  4.0 46.1 %copy-start.5 = (s32[1,512,1]{1,2,0:T(1,128)S(1)}, s32[1,512,1]{1,2,0:T(1,128)}, u32[]{:S(2)}) copy-start(s32[1,512,1]{1,2,0:T(1,128)} %param.10) | copy-start | bytes 6148
  4.0 42.0 %collective-permute-start = (bf16[64,4096]{1,0:T(8,128)(2,1)S(1)}, bf16[64,4096]{1,0:T(8,128)(2,1)S(1)}, u32[]{:S(2)}, u32[]{:S(2)}) collective-permute-start(bf16[64,4096]{1,0:T(8,128)(2,1)S(1)} %get-tuple-element.30), channel_id=1, source_target_pairs={{0,1},{1,2},{2,3},{3,0},{4,5},{5,6},{6,7},{7,4},{8,9},{9,10},{10,1... | collective-permute-start | bytes 1572872 | tf_op jit(solution)/shard_map/ppermute | solution.py:208
  5.9 40.2 %collective-permute-start.1 = (bf16[64,4096]{1,0:T(8,128)(2,1)S(1)}, bf16[64,4096]{1,0:T(8,128)(2,1)S(1)}, u32[]{:S(2)}, u32[]{:S(2)}) collective-permute-start(bf16[64,4096]{1,0:T(8,128)(2,1)S(1)} %get-tuple-element.31), channel_id=1, source_target_pairs={{0,2},{1,3},{2,0},{3,1},{4,6},{5,7},{6,4},{7,5},{8,10},{9,11},{10,... | collective-permute-start | bytes 1572872 | tf_op jit(solution)/shard_map/ppermute | solution.py:208
  6.1 40.0 %collective-permute-start.2 = (bf16[64,4096]{1,0:T(8,128)(2,1)S(1)}, bf16[64,4096]{1,0:T(8,128)(2,1)S(1)}, u32[]{:S(2)}, u32[]{:S(2)}) collective-permute-start(bf16[64,4096]{1,0:T(8,128)(2,1)S(1)} %get-tuple-element.32), channel_id=1, source_target_pairs={{0,3},{1,0},{2,1},{3,2},{4,7},{5,4},{6,5},{7,6},{8,11},{9,8},{10,9... | collective-permute-start | bytes 1572872 | tf_op jit(solution)/shard_map/ppermute | solution.py:208
  10.4 54.2 %copy-start.9 = (s32[1,8,128,1]{2,3,1,0:T(1,128)S(1)}, s32[1,8,128,1]{2,3,1,0:T(1,128)}, u32[]{:S(2)}) copy-start(s32[1,8,128,1]{2,3,1,0:T(1,128)} %param.12) | copy-start | bytes 12292
  10.4 54.2 %copy-start.12 = (s32[128]{0:T(128)S(1)}, s32[128]{0:T(128)}, u32[]{:S(2)}) copy-start(s32[128]{0:T(128)} %param.9) | copy-start | bytes 1540
  10.4 21.5 %collective-permute-start.3 = (bf16[144,1024]{1,0:T(8,128)(2,1)S(1)}, bf16[144,1024]{1,0:T(8,128)(2,1)S(1)}, u32[]{:S(2)}, u32[]{:S(2)}) collective-permute-start(bf16[144,1024]{1,0:T(8,128)(2,1)S(1)} %get-tuple-element.36), channel_id=1, source_target_pairs={{0,16},{4,20},{8,24},{12,28},{16,0},{20,4},{24,8},{28,12},{1,17},{... | collective-permute-start | bytes 884744 | tf_op jit(solution)/shard_map/ppermute | solution.py:208
  12.8 19.1 %collective-permute-start.4 = (bf16[144,1024]{1,0:T(8,128)(2,1)S(1)}, bf16[144,1024]{1,0:T(8,128)(2,1)S(1)}, u32[]{:S(2)}, u32[]{:S(2)}) collective-permute-start(bf16[144,1024]{1,0:T(8,128)(2,1)S(1)} %get-tuple-element.37), channel_id=1, source_target_pairs={{0,12},{4,16},{8,20},{12,24},{16,28},{20,0},{24,4},{28,8},{1,13},{... | collective-permute-start | bytes 884744 | tf_op jit(solution)/shard_map/ppermute | solution.py:208
  31.9 19.7 %collective-permute-start.5 = (bf16[144,1024]{1,0:T(8,128)(2,1)S(1)}, bf16[144,1024]{1,0:T(8,128)(2,1)S(1)}, u32[]{:S(2)}, u32[]{:S(2)}) collective-permute-start(bf16[144,1024]{1,0:T(8,128)(2,1)S(1)} %get-tuple-element.38), channel_id=1, source_target_pairs={{0,20},{4,24},{8,28},{12,0},{16,4},{20,8},{24,12},{28,16},{1,21},{... | collective-permute-start | bytes 884744 | tf_op jit(solution)/shard_map/ppermute | solution.py:208
  31.9 20.0 %collective-permute-start.6 = (bf16[144,1024]{1,0:T(8,128)(2,1)S(1)}, bf16[144,1024]{1,0:T(8,128)(2,1)S(1)}, u32[]{:S(2)}, u32[]{:S(2)}) collective-permute-start(bf16[144,1024]{1,0:T(8,128)(2,1)S(1)} %get-tuple-element.39), channel_id=1, source_target_pairs={{0,8},{4,12},{8,16},{12,20},{16,24},{20,28},{24,0},{28,4},{1,9},{5... | collective-permute-start | bytes 884744 | tf_op jit(solution)/shard_map/ppermute | solution.py:208
  46.0 18.5 %collective-permute-start.7 = (bf16[144,1024]{1,0:T(8,128)(2,1)S(1)}, bf16[144,1024]{1,0:T(8,128)(2,1)S(1)}, u32[]{:S(2)}, u32[]{:S(2)}) collective-permute-start(bf16[144,1024]{1,0:T(8,128)(2,1)S(1)} %get-tuple-element.40), channel_id=1, source_target_pairs={{0,24},{4,28},{8,0},{12,4},{16,8},{20,12},{24,16},{28,20},{1,25},{... | collective-permute-start | bytes 884744 | tf_op jit(solution)/shard_map/ppermute | solution.py:208
  46.0 18.6 %collective-permute-start.8 = (bf16[144,1024]{1,0:T(8,128)(2,1)S(1)}, bf16[144,1024]{1,0:T(8,128)(2,1)S(1)}, u32[]{:S(2)}, u32[]{:S(2)}) collective-permute-start(bf16[144,1024]{1,0:T(8,128)(2,1)S(1)} %get-tuple-element.41), channel_id=1, source_target_pairs={{0,4},{4,8},{8,12},{12,16},{16,20},{20,24},{24,28},{28,0},{1,5},{5... | collective-permute-start | bytes 884744 | tf_op jit(solution)/shard_map/ppermute | solution.py:208
  46.1 18.5 %collective-permute-start.9 = (bf16[144,1024]{1,0:T(8,128)(2,1)S(1)}, bf16[144,1024]{1,0:T(8,128)(2,1)S(1)}, u32[]{:S(2)}, u32[]{:S(2)}) collective-permute-start(bf16[144,1024]{1,0:T(8,128)(2,1)S(1)} %get-tuple-element.42), channel_id=1, source_target_pairs={{0,28},{4,0},{8,4},{12,8},{16,12},{20,16},{24,20},{28,24},{1,29},{... | collective-permute-start | bytes 884744 | tf_op jit(solution)/shard_map/ppermute | solution.py:208
  69.0 39.7 %collective-permute-start.10 = (bf16[64,4096]{1,0:T(8,128)(2,1)S(1)}, bf16[64,4096]{1,0:T(8,128)(2,1)S(1)}, u32[]{:S(2)}, u32[]{:S(2)}) collective-permute-start(bf16[64,4096]{1,0:T(8,128)(2,1)S(1)} %get-tuple-element.47), channel_id=1, source_target_pairs={{0,3},{1,0},{2,1},{3,2},{4,7},{5,4},{6,5},{7,6},{8,11},{9,8},{10,9... | collective-permute-start | bytes 1572872 | tf_op jit(solution)/shard_map/ppermute | solution.py:208
  70.6 39.5 %collective-permute-start.11 = (bf16[64,4096]{1,0:T(8,128)(2,1)S(1)}, bf16[64,4096]{1,0:T(8,128)(2,1)S(1)}, u32[]{:S(2)}, u32[]{:S(2)}) collective-permute-start(bf16[64,4096]{1,0:T(8,128)(2,1)S(1)} %get-tuple-element.48), channel_id=1, source_target_pairs={{0,2},{1,3},{2,0},{3,1},{4,6},{5,7},{6,4},{7,5},{8,10},{9,11},{10,... | collective-permute-start | bytes 1572872 | tf_op jit(solution)/shard_map/ppermute | solution.py:208
  71.9 38.3 %collective-permute-start.12 = (bf16[64,4096]{1,0:T(8,128)(2,1)S(1)}, bf16[64,4096]{1,0:T(8,128)(2,1)S(1)}, u32[]{:S(2)}, u32[]{:S(2)}) collective-permute-start(bf16[64,4096]{1,0:T(8,128)(2,1)S(1)} %get-tuple-element.49), channel_id=1, source_target_pairs={{0,1},{1,2},{2,3},{3,0},{4,5},{5,6},{6,7},{7,4},{8,9},{9,10},{10,1... | collective-permute-start | bytes 1572872 | tf_op jit(solution)/shard_map/ppermute | solution.py:208
  72.4 18.2 %collective-permute-start.13 = (bf16[144,1024]{1,0:T(8,128)(2,1)S(1)}, bf16[144,1024]{1,0:T(8,128)(2,1)S(1)}, u32[]{:S(2)}, u32[]{:S(2)}) collective-permute-start(bf16[144,1024]{1,0:T(8,128)(2,1)S(1)} %get-tuple-element.50), channel_id=1, source_target_pairs={{0,16},{4,20},{8,24},{12,28},{16,0},{20,4},{24,8},{28,12},{1,17},{... | collective-permute-start | bytes 884744 | tf_op jit(solution)/shard_map/ppermute | solution.py:208
  77.0 31.7 %collective-permute-start.14 = (bf16[144,1024]{1,0:T(8,128)(2,1)S(1)}, bf16[144,1024]{1,0:T(8,128)(2,1)S(1)}, u32[]{:S(2)}, u32[]{:S(2)}) collective-permute-start(bf16[144,1024]{1,0:T(8,128)(2,1)S(1)} %get-tuple-element.51), channel_id=1, source_target_pairs={{0,20},{4,24},{8,28},{12,0},{16,4},{20,8},{24,12},{28,16},{1,21},{... | collective-permute-start | bytes 884744 | tf_op jit(solution)/shard_map/ppermute | solution.py:208
  90.6 27.6 %collective-permute-start.15 = (bf16[144,1024]{1,0:T(8,128)(2,1)S(1)}, bf16[144,1024]{1,0:T(8,128)(2,1)S(1)}, u32[]{:S(2)}, u32[]{:S(2)}) collective-permute-start(bf16[144,1024]{1,0:T(8,128)(2,1)S(1)} %get-tuple-element.52), channel_id=1, source_target_pairs={{0,12},{4,16},{8,20},{12,24},{16,28},{20,0},{24,4},{28,8},{1,13},{... | collective-permute-start | bytes 884744 | tf_op jit(solution)/shard_map/ppermute | solution.py:208
  108.7 22.8 %collective-permute-start.16 = (bf16[144,1024]{1,0:T(8,128)(2,1)S(1)}, bf16[144,1024]{1,0:T(8,128)(2,1)S(1)}, u32[]{:S(2)}, u32[]{:S(2)}) collective-permute-start(bf16[144,1024]{1,0:T(8,128)(2,1)S(1)} %get-tuple-element.53), channel_id=1, source_target_pairs={{0,24},{4,28},{8,0},{12,4},{16,8},{20,12},{24,16},{28,20},{1,25},{... | collective-permute-start | bytes 884744 | tf_op jit(solution)/shard_map/ppermute | solution.py:208
  108.7 22.8 %collective-permute-start.17 = (bf16[144,1024]{1,0:T(8,128)(2,1)S(1)}, bf16[144,1024]{1,0:T(8,128)(2,1)S(1)}, u32[]{:S(2)}, u32[]{:S(2)}) collective-permute-start(bf16[144,1024]{1,0:T(8,128)(2,1)S(1)} %get-tuple-element.54), channel_id=1, source_target_pairs={{0,8},{4,12},{8,16},{12,20},{16,24},{20,28},{24,0},{28,4},{1,9},{5... | collective-permute-start | bytes 884744 | tf_op jit(solution)/shard_map/ppermute | solution.py:208
  110.2 21.4 %collective-permute-start.18 = (bf16[144,1024]{1,0:T(8,128)(2,1)S(1)}, bf16[144,1024]{1,0:T(8,128)(2,1)S(1)}, u32[]{:S(2)}, u32[]{:S(2)}) collective-permute-start(bf16[144,1024]{1,0:T(8,128)(2,1)S(1)} %get-tuple-element.55), channel_id=1, source_target_pairs={{0,28},{4,0},{8,4},{12,8},{16,12},{20,16},{24,20},{28,24},{1,29},{... | collective-permute-start | bytes 884744 | tf_op jit(solution)/shard_map/ppermute | solution.py:208
  110.2 21.4 %collective-permute-start.19 = (bf16[144,1024]{1,0:T(8,128)(2,1)S(1)}, bf16[144,1024]{1,0:T(8,128)(2,1)S(1)}, u32[]{:S(2)}, u32[]{:S(2)}) collective-permute-start(bf16[144,1024]{1,0:T(8,128)(2,1)S(1)} %get-tuple-element.56), channel_id=1, source_target_pairs={{0,4},{4,8},{8,12},{12,16},{16,20},{20,24},{24,28},{28,0},{1,5},{5... | collective-permute-start | bytes 884744 | tf_op jit(solution)/shard_map/ppermute | solution.py:208
  (9 other events, 107.3 us)

commit v2 on v0

v2 whole, which is shorter than its diff:
```python
import functools
from typing import NamedTuple

import jax
import jax.numpy as jnp
from jax import lax
from jax.experimental import pallas as pl
from jax.experimental.pallas import tpu as pltpu
from jax.sharding import PartitionSpec as P

COLUMNS = 4
SCALE = 3.0
VMEM = pl.BlockSpec(memory_space=pltpu.VMEM)
ANY = pl.BlockSpec(memory_space=pl.ANY)
f32, bf16, i32 = jnp.float32, jnp.bfloat16, jnp.int32


class Blocks(NamedTuple):
    axis: str
    shifts: tuple
    count: int
    split: int

    @property
    def rows(self):
        return self.count * self.split

    @property
    def total(self):
        return self.rows * len(self.shifts)

    def part(self, n):
        return slice(n * self.rows, (n + 1) * self.rows)


def call(kernel, out_shape, *args, scratch=(), flops=0, unread=0, vmem=24):
    nbytes = sum(a.size * a.dtype.itemsize for a in (*args, *jax.tree.leaves(out_shape)))
    read = len(args) - unread

    def body(*refs):
        kernel(*refs[:read], *refs[len(args) :])

    return pl.pallas_call(
        body,
        out_shape=out_shape,
        in_specs=[VMEM] * read + [ANY] * unread,
        out_specs=jax.tree.map(lambda _: VMEM, out_shape),
        scratch_shapes=list(scratch),
        compiler_params=pltpu.CompilerParams(vmem_limit_bytes=vmem * 2**20),
        cost_estimate=pl.CostEstimate(flops=flops, bytes_accessed=nbytes, transcendentals=0),
    )(*args)


def dot(a, b, dims=((1,), (0,))):
    return lax.dot_general(a, b, (dims, ((), ())), preferred_element_type=f32)


NT = ((1,), (1,))
TN = ((0,), (0,))


def row_plan(plan):
    t = lax.broadcasted_iota(i32, (plan.rows, 128), 0)
    chunk = jnp.zeros_like(t)
    for c in range(1, plan.split):
        chunk = chunk + (t >= c * plan.count).astype(i32)
    slot = t - plan.count * chunk
    return jnp.concatenate([slot] * len(plan.shifts), axis=0), jnp.concatenate([chunk] * len(plan.shifts), axis=0)


def stacked(ref, split):
    width = ref.shape[1] // split
    return jnp.concatenate([ref[:, c * width : (c + 1) * width] for c in range(split)], axis=0)


def spread(values, chunk, split):
    if split == 1:
        return values.astype(bf16)
    return jnp.concatenate([jnp.where(chunk == c, values, 0.0).astype(bf16) for c in range(split)], axis=1)


def slot_codes(axis, owner_ref, codes):
    peers, rows = owner_ref.shape
    name = me = lax.axis_index(axis)
    if axis == "grp":
        name = lax.rem(me - lax.broadcasted_iota(i32, (peers, rows), 0) - 1 + 2 * peers, peers)
    wanted = owner_ref[...] == name
    earlier = lax.broadcasted_iota(i32, (rows, rows), 0) < lax.broadcasted_iota(i32, (rows, rows), 1)
    rank = dot(wanted.astype(f32).astype(bf16), earlier.astype(f32).astype(bf16))
    codes[...] = jnp.where(wanted, rank, -1.0).astype(i32)


def slot_onehot(plan, codes, row_ref):
    slot, chunk = row_plan(plan)
    asked = []
    for n, shift in enumerate(plan.shifts):
        r = lax.rem(lax.axis_index(plan.axis) + shift, codes.shape[0])
        chosen = codes[pl.ds(r, 1), :] == slot[plan.part(n)]
        asked.append(jnp.where(chosen, row_ref[pl.ds(r, 1), :] + 1, 0).astype(f32))
    at = jnp.sum(jnp.concatenate(asked, axis=0), axis=1, keepdims=True)
    ids = lax.broadcasted_iota(i32, slot.shape, 1) + 1
    return jnp.where(ids.astype(f32) == at, 1.0, 0.0), chunk


def live_slots(plan, owner_ref):
    slot, _ = row_plan(plan)
    peers = owner_ref.shape[0]
    me = lax.axis_index(plan.axis)
    live = []
    for n, shift in enumerate(plan.shifts):
        name = peers - 1 - shift if plan.axis == "grp" else lax.rem(me - shift + peers, peers)
        used = jnp.sum((owner_ref[pl.ds(me, 1), :] == name).astype(f32), axis=1, keepdims=True)
        live.append(slot[plan.part(n)].astype(f32) < used)
    return jnp.concatenate(live, axis=0)


def send_kernel(plan, owner_ref, row_ref, docs_ref, *refs):
    *outs, codes = refs
    slot_codes(plan.axis, owner_ref, codes)
    onehot, chunk = slot_onehot(plan, codes, row_ref)
    rows = dot(spread(onehot, chunk, plan.split), stacked(docs_ref, plan.split))
    for n, out in enumerate(outs):
        out[...] = rows[plan.part(n)].astype(bf16)


def near_kernel(plan, q_ref, docs_ref, owner_ref, row_ref, *refs):
    *blocks, scores_out, times_out, inner_out = refs
    me = lax.axis_index("dp")
    rows = q_ref.shape[0]
    named = (owner_ref[pl.ds(me, 1), :] == me) & (row_ref[pl.ds(me, 1), :] == lax.broadcasted_iota(i32, (rows, rows), 0))
    times = 1.0 + jnp.sum(named.astype(f32), axis=1, keepdims=True)
    times_out[:rows, :] = jnp.broadcast_to(times, (rows, rows))
    times_out[rows:, :] = jnp.ones((plan.total, rows), f32)
    scores_out[:rows, :] = SCALE * dot(docs_ref[...], q_ref[...], NT)
    inner_out[...] = jnp.concatenate([block[...] for block in blocks], axis=0)
    scores = SCALE * dot(inner_out[...], q_ref[...], NT)
    scores_out[rows:, :] = jnp.where(live_slots(plan, owner_ref), scores, -jnp.inf)


def main_kernel(plan, q_ref, near_ref, times_ref, pos_ref, owner_ref, *refs):
    blocks, refs = refs[: len(plan.shifts)], refs[len(plan.shifts) :]
    loss_out, near_w, far_w, far, *grads = refs
    rows = q_ref.shape[0]
    _, chunk = row_plan(plan)
    far[...] = jnp.concatenate([block[...] for block in blocks], axis=0)
    width = far.shape[1]
    part = dot(far[...], q_ref[:, :width], NT)
    for c in range(1, plan.split):
        part = jnp.where(chunk == c, dot(far[...], q_ref[:, c * width : (c + 1) * width], NT), part)
    scores = []
    for n in range(len(blocks)):
        total = part[plan.part(n)]
        for c in range(1, plan.split):
            total = total + pltpu.roll(part[plan.part(n)], c * plan.count, 0)
        scores.append(total)
    scores = jnp.where(live_slots(plan, owner_ref), SCALE * jnp.concatenate(scores, axis=0), -jnp.inf)
    near = near_ref[...]
    top = jnp.maximum(jnp.max(near, axis=0, keepdims=True), jnp.max(scores, axis=0, keepdims=True))
    near_e = times_ref[...] * jnp.exp(near - top)
    far_e = jnp.exp(scores - top)
    total = jnp.sum(near_e, axis=0, keepdims=True)
    total = total + jnp.sum(jnp.where(chunk == 0, far_e, 0.0), axis=0, keepdims=True)
    factor = SCALE / total
    w = far_e * factor
    far_w[...] = w.astype(bf16)
    sums = dot(spread(w, chunk, plan.split), stacked(q_ref, plan.split))
    for n, out in enumerate(grads):
        out[...] = sums[plan.part(n)].astype(bf16)
    positive = (lax.broadcasted_iota(i32, near.shape, 0) == pos_ref[...]).astype(f32)
    loss_out[...] = top + jnp.log(total) - jnp.sum(jnp.where(positive > 0.0, near, 0.0), axis=0, keepdims=True)
    near_w[...] = (near_e * factor - SCALE * positive).astype(bf16)


def inner_grad_kernel(plan, near_w, q_ref, *outs):
    sums = dot(near_w[q_ref.shape[0] :, :], q_ref[...])
    for n, out in enumerate(outs):
        out[...] = sums[plan.part(n)].astype(bf16)


def add_far(plan, select, block, acc, cols):
    width = block.shape[1]
    chunk = cols.start // width
    if plan.split > 1:
        select = jnp.where(row_plan(plan)[1] == chunk, select, 0.0)
    return acc + dot(select.astype(bf16), block[:, cols.start - chunk * width : cols.stop - chunk * width], TN)


def query_grad_kernel(plan, near_w, docs_ref, inner_ref, far_w, far_ref, out):
    rows = docs_ref.shape[0]
    width = out.shape[1] // COLUMNS
    far_w = far_w[...].astype(f32)
    for c in range(COLUMNS):
        cols = slice(c * width, (c + 1) * width)
        acc = dot(near_w[:rows, :], docs_ref[:, cols], TN) + dot(near_w[rows:, :], inner_ref[:, cols], TN)
        out[:, cols] = add_far(plan, far_w, far_ref, acc, cols).astype(bf16)


def near_grad_kernel(plan, near_w, q_ref, owner_ref, row_ref, *refs):
    *blocks, out, codes = refs
    slot_codes(plan.axis, owner_ref, codes)
    onehot, _ = slot_onehot(plan, codes, row_ref)
    block = jnp.concatenate([block[...] for block in blocks], axis=0)
    out[...] = dot(near_w[: q_ref.shape[0], :], q_ref[...]) + dot(onehot.astype(bf16), block, TN)


def doc_grad_kernel(plan, near_ref, owner_ref, row_ref, *refs):
    *blocks, out, codes = refs
    slot_codes(plan.axis, owner_ref, codes)
    onehot, _ = slot_onehot(plan, codes, row_ref)
    block = jnp.concatenate([block[...] for block in blocks], axis=0)
    width = out.shape[1] // COLUMNS
    for c in range(COLUMNS):
        cols = slice(c * width, (c + 1) * width)
        out[:, cols] = add_far(plan, onehot, block, near_ref[:, cols], cols).astype(bf16)


def exchange(plan, blocks, sign):
    size = lax.axis_size(plan.axis)
    return [
        lax.ppermute(block, plan.axis, [(g, (g + sign * shift) % size) for g in range(size)])
        for shift, block in zip(plan.shifts, blocks)
    ]


def per_device(queries, documents, positives, inner_owner, inner_row, outer_owner, outer_row):
    rows, width = queries.shape
    dp, grp = lax.axis_size("dp"), lax.axis_size("grp")
    cap_inner = -(-max(2, 2 * rows // dp) // 16) * 16
    cap_outer = -(-max(2, 2 * rows // (grp - 1)) // 4) * 4
    inner = Blocks("dp", tuple(range(1, dp)), cap_inner, 1)
    outer_shifts = tuple(sorted(range(1, grp), key=lambda k: (abs(2 * k - grp), k)))
    outer = Blocks("grp", outer_shifts, cap_outer, 1 if cap_outer % 8 == 0 else 2)
    inner_owner, inner_row = inner_owner.reshape(dp, rows), inner_row.reshape(dp, rows)
    outer_owner, outer_row = outer_owner.reshape(grp, rows), outer_row.reshape(grp, rows)
    shape = jax.ShapeDtypeStruct
    outer_blocks = [shape((outer.rows, width // outer.split), bf16)] * len(outer.shifts)
    inner_blocks = [shape((inner.rows, width), bf16)] * len(inner.shifts)
    outer_codes, inner_codes = [pltpu.VMEM((grp, rows), i32)], [pltpu.VMEM((dp, rows), i32)]
    far_flops, inner_flops, own_flops = 2 * outer.total * rows * width, 2 * inner.total * rows * width, 2 * rows * rows * width

    send = call(
        functools.partial(send_kernel, outer),
        outer_blocks,
        outer_owner, outer_row, documents,
        scratch=outer_codes, flops=far_flops,
    )
    got = exchange(outer, send, 1)
    send_inner = call(
        functools.partial(send_kernel, inner),
        inner_blocks,
        inner_owner, inner_row, documents,
        scratch=inner_codes, flops=inner_flops, unread=0,
    )
    got_inner = exchange(inner, send_inner, 1)
    scores, times, inner_rows = call(
        functools.partial(near_kernel, inner),
        [shape((rows + inner.total, rows), f32)] * 2 + [shape((inner.total, width), bf16)],
        queries, documents, inner_owner, inner_row, *got_inner, got[0], got[1], got[2],
        flops=inner_flops + own_flops, unread=3,
    )
    losses, near_w, far_w, far_rows, *grads = call(
        functools.partial(main_kernel, outer),
        [
            shape((1, rows), f32),
            shape((rows + inner.total, rows), bf16),
            shape((outer.total, rows), bf16),
            shape((outer.total, width // outer.split), bf16),
            *outer_blocks,
        ],
        queries, scores, times, positives.reshape(1, rows), outer_owner, *got,
        flops=2 * far_flops,
    )
    back = exchange(outer, grads, -1)
    query_grads = call(
        functools.partial(query_grad_kernel, outer),
        shape((rows, width), bf16),
        near_w, documents, inner_rows, far_w, far_rows,
        flops=far_flops + inner_flops + own_flops,
    )
    grads_inner = call(
        functools.partial(inner_grad_kernel, inner),
        inner_blocks,
        near_w, queries,
        flops=inner_flops, unread=0,
    )
    back_inner = exchange(inner, grads_inner, -1)
    near_grads = call(
        functools.partial(near_grad_kernel, inner),
        shape((rows, width), f32),
        near_w, queries, inner_owner, inner_row, *back_inner, back[0], back[1], back[2],
        scratch=inner_codes, flops=inner_flops + own_flops, unread=3,
    )
    doc_grads = call(
        functools.partial(doc_grad_kernel, outer),
        shape((rows, width), bf16),
        near_grads, outer_owner, outer_row, *back,
        scratch=outer_codes, flops=far_flops,
    )
    return losses.reshape(rows), query_grads, doc_grads


def solution(mesh):
    return jax.shard_map(
        per_device,
        mesh=mesh,
        in_specs=(
            P(("grp", "dp"), None),
            P(("grp", "dp"), None),
            P(("grp", "dp")),
            P("grp", None, None),
            P("grp", None, None),
            P("dp", None, None, None),
            P("dp", None, None, None),
        ),
        out_specs=(P(("grp", "dp")), P(("grp", "dp"), None), P(("grp", "dp"), None)),
        check_vma=False,
    )
```

time: 218 us -> 123 us (0.56)
  waiting for transfers between devices: 135 us -> 59.7 us
  starting transfers between devices: 21.4 us -> 44.9 us
  matrix products: 21.6 us -> 0 us
  local copies, waits for them, and re-layouts: 24.1 us -> 5.29 us
  other arithmetic: 12.3 us -> 0 us
  Pallas kernels: 0 us -> 10.4 us
    all_to_all x4 -> x0, waiting for transfers between devices: 135 us -> none  [the longest x1 54.8 us: per_device(): lax.all_to_all(send_outer, 'grp', split_axis=0, concat_axis=0, tiled=True)]
    ppermute x0 -> x20, waiting for transfers between devices: none -> 59.7 us  [exchange(): lax.ppermute(block, plan.axis, [(g, (g + sign * shift) % size) for g in r...]
    ppermute x0 -> x20, starting transfers between devices: none -> 44.9 us  [exchange(): lax.ppermute(block, plan.axis, [(g, (g + sign * shift) % size) for g in r...]
    dot_general x11 -> x0, matrix products: 21.6 us -> none  [the longest x2 6.3 us: add_returned(): jnp.einsum('mna,mnu->au', indicator_matrix.astype(jnp.bfloat16), sent_bac...]
    all_to_all x4 -> x0, starting transfers between devices: 21.4 us -> none  [the longest x1 5.87 us: per_device(): lax.all_to_all(inner_slots, 'dp', split_axis=0, concat_axis=0, tiled=True)]
    gather x3 -> x0, local copies, waits for them, and re-layouts: 14.5 us -> none  [collect_slot_index(): picked = jnp.take(documents, row_at.reshape(-1), axis=0)]
    pallas_call x0 -> x8, Pallas kernels: none -> 10.4 us  [call(): pl.pallas_call(body, out_shape=out_shape, in_specs=[VMEM] * read + [ANY]...]
    reshape x4 -> x0, local copies, waits for them, and re-layouts: 8.41 us -> none  [the longest x1 4.14 us: per_device(): across(outer_w, queries).astype(jnp.bfloat16)]
  transfers between devices with their start and end apart: 4 -> 20, of which waited for: 4 -> 7; matrix products, arithmetic and copies ran while one was open for 15% -> 0% of each run, Pallas kernels for 0% -> 4%
where the time goes in v2:
time: 123 us; the launch traced here: 121 us
  waiting for transfers between devices  59.7 us (49%)
  starting transfers between devices  44.9 us (37%)
  Pallas kernels  10.4 us (8%)
  local copies, waits for them, and re-layouts  5.29 us (4%)
    ppermute x20, waiting for transfers between devices, exchange(): lax.ppermute(block, plan.axis, [(g, (g + sign * shift) % size) for g in r...  59.7 us
    ppermute x20, starting transfers between devices, exchange(): lax.ppermute(block, plan.axis, [(g, (g + sign * shift) % size) for g in r...  44.9 us
    pallas_call x8, Pallas kernels, call(): pl.pallas_call(body, out_shape=out_shape, in_specs=[VMEM] * read + [ANY]...  10.4 us
    unnamed x24, local copies, waits for them, and re-layouts  5.29 us
  transfers between devices with their start and end apart: 20, of which 7 were waited for; matrix products, arithmetic and copies ran while one was open for 0% of the time, Pallas kernels for 4%

profile of v2, /device:TPU:3, one launch (start us, length us, event | category | flops | bytes accessed | tf_op | source)
XLA Modules:
  0.0 121.1 jit_solution(14519176462005822889)
XLA Ops:
  0.7 1.3 %copy-done.1 = bf16[128,4096]{1,0:T(8,128)(2,1)S(1)} copy-done((bf16[128,4096]{1,0:T(8,128)(2,1)S(1)}, bf16[128,4096]{1,0:T(8,128)(2,1)}, u32[]{:S(2)}) %copy-start.1) | copy-done | bytes 1048600
  4.2 2.4 %collective-permute-start.3 = (bf16[72,2048]{1,0:T(8,128)(2,1)S(1)}, bf16[72,2048]{1,0:T(8,128)(2,1)S(1)}, u32[]{:S(2)}, u32[]{:S(2)}) collective-permute-start(bf16[72,2048]{1,0:T(8,128)(2,1)S(1)} %get-tuple-element.33), channel_id=1, source_target_pairs={{0,16},{4,20},{8,24},{12,28},{16,0},{20,4},{24,8},{28,12},{1,17},{... | collective-permute-start | bytes 884744 | tf_op jit(solution)/shard_map/ppermute | solution.py:220
  6.6 1.2 %copy-done.2 = bf16[128,4096]{1,0:T(8,128)(2,1)S(1)} copy-done((bf16[128,4096]{1,0:T(8,128)(2,1)S(1)}, bf16[128,4096]{1,0:T(8,128)(2,1)}, u32[]{:S(2)}) %copy-start.2) | copy-done | bytes 1048600
  10.0 2.1 %collective-permute-start = (bf16[64,4096]{1,0:T(8,128)(2,1)S(1)}, bf16[64,4096]{1,0:T(8,128)(2,1)S(1)}, u32[]{:S(2)}, u32[]{:S(2)}) collective-permute-start(bf16[64,4096]{1,0:T(8,128)(2,1)S(1)} %get-tuple-element.30), channel_id=1, source_target_pairs={{0,1},{1,2},{2,3},{3,0},{4,5},{5,6},{6,7},{7,4},{8,9},{9,10},{10,1... | collective-permute-start | bytes 1572872 | tf_op jit(solution)/shard_map/ppermute | solution.py:220
  12.3 4.2 %collective-permute-start.5 = (bf16[72,2048]{1,0:T(8,128)(2,1)S(1)}, bf16[72,2048]{1,0:T(8,128)(2,1)S(1)}, u32[]{:S(2)}, u32[]{:S(2)}) collective-permute-start(bf16[72,2048]{1,0:T(8,128)(2,1)S(1)} %get-tuple-element.35), channel_id=1, source_target_pairs={{0,20},{4,24},{8,28},{12,0},{16,4},{20,8},{24,12},{28,16},{1,21},{... | collective-permute-start | bytes 884744 | tf_op jit(solution)/shard_map/ppermute | solution.py:220
  16.5 9.3 %collective-permute-done.3.refs_7_.refs_5_ = bf16[72,2048]{1,0:T(8,128)(2,1)S(1)} collective-permute-done((bf16[72,2048]{1,0:T(8,128)(2,1)S(1)}, bf16[72,2048]{1,0:T(8,128)(2,1)S(1)}, u32[]{:S(2)}, u32[]{:S(2)}) %collective-permute-start.3) | collective-permute-done | bytes 294944 | tf_op jit(solution)/shard_map/ppermute | solution.py:220
  25.8 2.7 %collective-permute-start.2 = (bf16[64,4096]{1,0:T(8,128)(2,1)S(1)}, bf16[64,4096]{1,0:T(8,128)(2,1)S(1)}, u32[]{:S(2)}, u32[]{:S(2)}) collective-permute-start(bf16[64,4096]{1,0:T(8,128)(2,1)S(1)} %get-tuple-element.32), channel_id=1, source_target_pairs={{0,3},{1,0},{2,1},{3,2},{4,7},{5,4},{6,5},{7,6},{8,11},{9,8},{10,9... | collective-permute-start | bytes 1572872 | tf_op jit(solution)/shard_map/ppermute | solution.py:220
  28.5 11.3 %collective-permute-start.6 = (bf16[72,2048]{1,0:T(8,128)(2,1)S(1)}, bf16[72,2048]{1,0:T(8,128)(2,1)S(1)}, u32[]{:S(2)}, u32[]{:S(2)}) collective-permute-start(bf16[72,2048]{1,0:T(8,128)(2,1)S(1)} %get-tuple-element.38), channel_id=1, source_target_pairs={{0,8},{4,12},{8,16},{12,20},{16,24},{20,28},{24,0},{28,4},{1,9},{5... | collective-permute-start | bytes 884744 | tf_op jit(solution)/shard_map/ppermute | solution.py:220
  39.9 2.8 %collective-permute-start.7 = (bf16[72,2048]{1,0:T(8,128)(2,1)S(1)}, bf16[72,2048]{1,0:T(8,128)(2,1)S(1)}, u32[]{:S(2)}, u32[]{:S(2)}) collective-permute-start(bf16[72,2048]{1,0:T(8,128)(2,1)S(1)} %get-tuple-element.39), channel_id=1, source_target_pairs={{0,24},{4,28},{8,0},{12,4},{16,8},{20,12},{24,16},{28,20},{1,25},{... | collective-permute-start | bytes 884744 | tf_op jit(solution)/shard_map/ppermute | solution.py:220
  42.6 3.0 %collective-permute-start.8 = (bf16[72,2048]{1,0:T(8,128)(2,1)S(1)}, bf16[72,2048]{1,0:T(8,128)(2,1)S(1)}, u32[]{:S(2)}, u32[]{:S(2)}) collective-permute-start(bf16[72,2048]{1,0:T(8,128)(2,1)S(1)} %get-tuple-element.40), channel_id=1, source_target_pairs={{0,4},{4,8},{8,12},{12,16},{16,20},{20,24},{24,28},{28,0},{1,5},{5... | collective-permute-start | bytes 884744 | tf_op jit(solution)/shard_map/ppermute | solution.py:220
  46.5 7.4 %collective-permute-done.7.refs_9_ = bf16[72,2048]{1,0:T(8,128)(2,1)S(1)} collective-permute-done((bf16[72,2048]{1,0:T(8,128)(2,1)S(1)}, bf16[72,2048]{1,0:T(8,128)(2,1)S(1)}, u32[]{:S(2)}, u32[]{:S(2)}) %collective-permute-start.7) | collective-permute-done | bytes 294944 | tf_op jit(solution)/shard_map/ppermute | solution.py:220
  53.9 4.5 %collective-permute-done.8.refs_10_ = bf16[72,2048]{1,0:T(8,128)(2,1)S(1)} collective-permute-done((bf16[72,2048]{1,0:T(8,128)(2,1)S(1)}, bf16[72,2048]{1,0:T(8,128)(2,1)S(1)}, u32[]{:S(2)}, u32[]{:S(2)}) %collective-permute-start.8) | collective-permute-done | bytes 294944 | tf_op jit(solution)/shard_map/ppermute | solution.py:220
  58.5 5.2 %collective-permute-done.9.refs_11_ = bf16[72,2048]{1,0:T(8,128)(2,1)S(1)} collective-permute-done((bf16[72,2048]{1,0:T(8,128)(2,1)S(1)}, bf16[72,2048]{1,0:T(8,128)(2,1)S(1)}, u32[]{:S(2)}, u32[]{:S(2)}) %collective-permute-start.9) | collective-permute-done | bytes 294944 | tf_op jit(solution)/shard_map/ppermute | solution.py:220
  63.6 2.1 %shard_map.97 = (f32[1,128]{1,0:T(1,128)}, bf16[320,128]{1,0:T(8,128)(2,1)S(1)}, bf16[504,128]{1,0:T(8,128)(2,1)S(1)}, bf16[504,2048]{1,0:T(8,128)(2,1)S(1)}, bf...) custom-call(bf16[128,4096]{1,0:T(8,128)(2,1)S(1)} %copy-done, ...), custom_call_target="tpu_custom_call" | custom-call | flops 1056964608 | bytes 7785472 | tf_op jit(solution)/shard_map/pallas_call | solution.py:43
  66.4 1.2 collective-permute-start.10
  67.6 1.3 %collective-permute-start.11 = (bf16[64,4096]{1,0:T(8,128)(2,1)S(1)}, bf16[64,4096]{1,0:T(8,128)(2,1)S(1)}, u32[]{:S(2)}, u32[]{:S(2)}) collective-permute-start(bf16[64,4096]{1,0:T(8,128)(2,1)S(1)} %get-tuple-element.48), channel_id=1, source_target_pairs={{0,2},{1,3},{2,0},{3,1},{4,6},{5,7},{6,4},{7,5},{8,10},{9,11},{10,... | collective-permute-start | bytes 1572872 | tf_op jit(solution)/shard_map/ppermute | solution.py:220
  69.9 2.3 %collective-permute-start.15 = (bf16[72,2048]{1,0:T(8,128)(2,1)S(1)}, bf16[72,2048]{1,0:T(8,128)(2,1)S(1)}, u32[]{:S(2)}, u32[]{:S(2)}) collective-permute-start(bf16[72,2048]{1,0:T(8,128)(2,1)S(1)} %get-tuple-element.52), channel_id=1, source_target_pairs={{0,12},{4,16},{8,20},{12,24},{16,28},{20,0},{24,4},{28,8},{1,13},{... | collective-permute-start | bytes 884744 | tf_op jit(solution)/shard_map/ppermute | solution.py:220
  72.1 10.9 %collective-permute-done.13.refs_7_.refs_3_ = bf16[72,2048]{1,0:T(8,128)(2,1)S(1)} collective-permute-done((bf16[72,2048]{1,0:T(8,128)(2,1)S(1)}, bf16[72,2048]{1,0:T(8,128)(2,1)S(1)}, u32[]{:S(2)}, u32[]{:S(2)}) %collective-permute-start.13) | collective-permute-done | bytes 294944 | tf_op jit(solution)/shard_map/ppermute | solution.py:220
  83.0 1.8 %collective-permute-start.12 = (bf16[64,4096]{1,0:T(8,128)(2,1)S(1)}, bf16[64,4096]{1,0:T(8,128)(2,1)S(1)}, u32[]{:S(2)}, u32[]{:S(2)}) collective-permute-start(bf16[64,4096]{1,0:T(8,128)(2,1)S(1)} %get-tuple-element.49), channel_id=1, source_target_pairs={{0,1},{1,2},{2,3},{3,0},{4,5},{5,6},{6,7},{7,4},{8,9},{9,10},{10,1... | collective-permute-start | bytes 1572872 | tf_op jit(solution)/shard_map/ppermute | solution.py:220
  84.8 11.1 %collective-permute-done.14.refs_8_.refs_4_ = bf16[72,2048]{1,0:T(8,128)(2,1)S(1)} collective-permute-done((bf16[72,2048]{1,0:T(8,128)(2,1)S(1)}, bf16[72,2048]{1,0:T(8,128)(2,1)S(1)}, u32[]{:S(2)}, u32[]{:S(2)}) %collective-permute-start.14) | collective-permute-done | bytes 294944 | tf_op jit(solution)/shard_map/ppermute | solution.py:220
  97.4 7.1 %collective-permute-start.18 = (bf16[72,2048]{1,0:T(8,128)(2,1)S(1)}, bf16[72,2048]{1,0:T(8,128)(2,1)S(1)}, u32[]{:S(2)}, u32[]{:S(2)}) collective-permute-start(bf16[72,2048]{1,0:T(8,128)(2,1)S(1)} %get-tuple-element.55), channel_id=1, source_target_pairs={{0,28},{4,0},{8,4},{12,8},{16,12},{20,16},{24,20},{28,24},{1,29},{... | collective-permute-start | bytes 884744 | tf_op jit(solution)/shard_map/ppermute | solution.py:220
  104.5 2.2 %shard_map.98 = bf16[128,4096]{1,0:T(8,128)(2,1)} custom-call(bf16[320,128]{1,0:T(8,128)(2,1)S(1)} %get-tuple-element.43.refs_0_, bf16[128,4096]{1,0:T(8,128)(2,1)S(1)} %copy-done.3, bf16[192,4096]{1,0:T(8,128)(2,1)S(1)} %get-tuple-element.44.refs_2_, bf16[504,128]{1,0:T(8,128)(2,1)S(1)} %get-tuple-element.45.refs_3_, ...), custom_call_target="tpu_custom_call" | custom-call | flops 864026624 | bytes 5945344 | tf_op jit(solution)/shard_map/pallas_call | solution.py:43
  107.7 11.4 %collective-permute-done.16.refs_6_ = bf16[72,2048]{1,0:T(8,128)(2,1)S(1)} collective-permute-done((bf16[72,2048]{1,0:T(8,128)(2,1)S(1)}, bf16[72,2048]{1,0:T(8,128)(2,1)S(1)}, u32[]{:S(2)}, u32[]{:S(2)}) %collective-permute-start.16) | collective-permute-done | bytes 294944 | tf_op jit(solution)/shard_map/ppermute | solution.py:220
  119.1 2.0 %shard_map.101 = bf16[128,4096]{1,0:T(8,128)(2,1)} custom-call(f32[128,4096]{1,0:T(8,128)S(1)} %shard_map.100.refs_0_, s32[8,128]{1,0:T(8,128)S(1)} %bitcast.14, s32[8,128]{1,0:T(8,128)S(1)} %bitcast.16, bf16[72,2048]{1,0:T(8,128)(2,1)S(1)} %collective-permute-done.13.refs_7_.refs_3_, bf16[72,2048]{1,0:T(8,128)(2,1)S(1)} %collective-permute-done.14.refs_8_.refs_4_, ...), custom_call_target="tpu_custom_call" | custom-call | flops 528482304 | bytes 5218304 | tf_op jit(solution)/shard_map/pallas_call | solution.py:43
  (48 shorter events, 9.6 us)
Async XLA Ops:
  0.6 45.0 %copy-start = (bf16[128,4096]{1,0:T(8,128)(2,1)S(1)}, bf16[128,4096]{1,0:T(8,128)(2,1)}, u32[]{:S(2)}) copy-start(bf16[128,4096]{1,0:T(8,128)(2,1)} %refs_1_.7) | copy-start | bytes 3145732
  4.2 21.6 %collective-permute-start.3 = (bf16[72,2048]{1,0:T(8,128)(2,1)S(1)}, bf16[72,2048]{1,0:T(8,128)(2,1)S(1)}, u32[]{:S(2)}, u32[]{:S(2)}) collective-permute-start(bf16[72,2048]{1,0:T(8,128)(2,1)S(1)} %get-tuple-element.33), channel_id=1, source_target_pairs={{0,16},{4,20},{8,24},{12,28},{16,0},{20,4},{24,8},{28,12},{1,17},{... | collective-permute-start | bytes 884744 | tf_op jit(solution)/shard_map/ppermute | solution.py:220
  10.0 32.7 %collective-permute-start = (bf16[64,4096]{1,0:T(8,128)(2,1)S(1)}, bf16[64,4096]{1,0:T(8,128)(2,1)S(1)}, u32[]{:S(2)}, u32[]{:S(2)}) collective-permute-start(bf16[64,4096]{1,0:T(8,128)(2,1)S(1)} %get-tuple-element.30), channel_id=1, source_target_pairs={{0,1},{1,2},{2,3},{3,0},{4,5},{5,6},{6,7},{7,4},{8,9},{9,10},{10,1... | collective-permute-start | bytes 1572872 | tf_op jit(solution)/shard_map/ppermute | solution.py:220
  12.1 33.5 %collective-permute-start.1 = (bf16[64,4096]{1,0:T(8,128)(2,1)S(1)}, bf16[64,4096]{1,0:T(8,128)(2,1)S(1)}, u32[]{:S(2)}, u32[]{:S(2)}) collective-permute-start(bf16[64,4096]{1,0:T(8,128)(2,1)S(1)} %get-tuple-element.31), channel_id=1, source_target_pairs={{0,2},{1,3},{2,0},{3,1},{4,6},{5,7},{6,4},{7,5},{8,10},{9,11},{10,... | collective-permute-start | bytes 1572872 | tf_op jit(solution)/shard_map/ppermute | solution.py:220
  12.3 16.2 %collective-permute-start.4 = (bf16[72,2048]{1,0:T(8,128)(2,1)S(1)}, bf16[72,2048]{1,0:T(8,128)(2,1)S(1)}, u32[]{:S(2)}, u32[]{:S(2)}) collective-permute-start(bf16[72,2048]{1,0:T(8,128)(2,1)S(1)} %get-tuple-element.34), channel_id=1, source_target_pairs={{0,12},{4,16},{8,20},{12,24},{16,28},{20,0},{24,4},{28,8},{1,13},{... | collective-permute-start | bytes 884744 | tf_op jit(solution)/shard_map/ppermute | solution.py:220
  12.3 27.5 %collective-permute-start.5 = (bf16[72,2048]{1,0:T(8,128)(2,1)S(1)}, bf16[72,2048]{1,0:T(8,128)(2,1)S(1)}, u32[]{:S(2)}, u32[]{:S(2)}) collective-permute-start(bf16[72,2048]{1,0:T(8,128)(2,1)S(1)} %get-tuple-element.35), channel_id=1, source_target_pairs={{0,20},{4,24},{8,28},{12,0},{16,4},{20,8},{24,12},{28,16},{1,21},{... | collective-permute-start | bytes 884744 | tf_op jit(solution)/shard_map/ppermute | solution.py:220
  25.8 19.9 %collective-permute-start.2 = (bf16[64,4096]{1,0:T(8,128)(2,1)S(1)}, bf16[64,4096]{1,0:T(8,128)(2,1)S(1)}, u32[]{:S(2)}, u32[]{:S(2)}) collective-permute-start(bf16[64,4096]{1,0:T(8,128)(2,1)S(1)} %get-tuple-element.32), channel_id=1, source_target_pairs={{0,3},{1,0},{2,1},{3,2},{4,7},{5,4},{6,5},{7,6},{8,11},{9,8},{10,9... | collective-permute-start | bytes 1572872 | tf_op jit(solution)/shard_map/ppermute | solution.py:220
  28.5 18.0 %collective-permute-start.6 = (bf16[72,2048]{1,0:T(8,128)(2,1)S(1)}, bf16[72,2048]{1,0:T(8,128)(2,1)S(1)}, u32[]{:S(2)}, u32[]{:S(2)}) collective-permute-start(bf16[72,2048]{1,0:T(8,128)(2,1)S(1)} %get-tuple-element.38), channel_id=1, source_target_pairs={{0,8},{4,12},{8,16},{12,20},{16,24},{20,28},{24,0},{28,4},{1,9},{5... | collective-permute-start | bytes 884744 | tf_op jit(solution)/shard_map/ppermute | solution.py:220
  39.9 14.1 %collective-permute-start.7 = (bf16[72,2048]{1,0:T(8,128)(2,1)S(1)}, bf16[72,2048]{1,0:T(8,128)(2,1)S(1)}, u32[]{:S(2)}, u32[]{:S(2)}) collective-permute-start(bf16[72,2048]{1,0:T(8,128)(2,1)S(1)} %get-tuple-element.39), channel_id=1, source_target_pairs={{0,24},{4,28},{8,0},{12,4},{16,8},{20,12},{24,16},{28,20},{1,25},{... | collective-permute-start | bytes 884744 | tf_op jit(solution)/shard_map/ppermute | solution.py:220
  42.6 15.8 %collective-permute-start.8 = (bf16[72,2048]{1,0:T(8,128)(2,1)S(1)}, bf16[72,2048]{1,0:T(8,128)(2,1)S(1)}, u32[]{:S(2)}, u32[]{:S(2)}) collective-permute-start(bf16[72,2048]{1,0:T(8,128)(2,1)S(1)} %get-tuple-element.40), channel_id=1, source_target_pairs={{0,4},{4,8},{8,12},{12,16},{16,20},{20,24},{24,28},{28,0},{1,5},{5... | collective-permute-start | bytes 884744 | tf_op jit(solution)/shard_map/ppermute | solution.py:220
  45.6 18.0 %copy-start.8 = (s32[1,8,128,1]{2,3,1,0:T(1,128)S(1)}, s32[1,8,128,1]{2,3,1,0:T(1,128)}, u32[]{:S(2)}) copy-start(s32[1,8,128,1]{2,3,1,0:T(1,128)} %param.12) | copy-start | bytes 12292
  45.6 18.0 %copy-start.11 = (s32[128]{0:T(128)S(1)}, s32[128]{0:T(128)}, u32[]{:S(2)}) copy-start(s32[128]{0:T(128)} %param.9) | copy-start | bytes 1540
  45.6 18.0 %collective-permute-start.9 = (bf16[72,2048]{1,0:T(8,128)(2,1)S(1)}, bf16[72,2048]{1,0:T(8,128)(2,1)S(1)}, u32[]{:S(2)}, u32[]{:S(2)}) collective-permute-start(bf16[72,2048]{1,0:T(8,128)(2,1)S(1)} %get-tuple-element.41), channel_id=1, source_target_pairs={{0,28},{4,0},{8,4},{12,8},{16,12},{20,16},{24,20},{28,24},{1,29},{... | collective-permute-start | bytes 884744 | tf_op jit(solution)/shard_map/ppermute | solution.py:220
  63.6 40.8 %copy-start.3 = (bf16[128,4096]{1,0:T(8,128)(2,1)S(1)}, bf16[128,4096]{1,0:T(8,128)(2,1)}, u32[]{:S(2)}) copy-start(bf16[128,4096]{1,0:T(8,128)(2,1)} %refs_1_.5) | copy-start | bytes 3145732
  65.8 17.2 %collective-permute-start.13 = (bf16[72,2048]{1,0:T(8,128)(2,1)S(1)}, bf16[72,2048]{1,0:T(8,128)(2,1)S(1)}, u32[]{:S(2)}, u32[]{:S(2)}) collective-permute-start(bf16[72,2048]{1,0:T(8,128)(2,1)S(1)} %get-tuple-element.50), channel_id=1, source_target_pairs={{0,16},{4,20},{8,24},{12,28},{16,0},{20,4},{24,8},{28,12},{1,17},{... | collective-permute-start | bytes 884744 | tf_op jit(solution)/shard_map/ppermute | solution.py:220
  66.4 31.0 %collective-permute-start.10 = (bf16[64,4096]{1,0:T(8,128)(2,1)S(1)}, bf16[64,4096]{1,0:T(8,128)(2,1)S(1)}, u32[]{:S(2)}, u32[]{:S(2)}) collective-permute-start(bf16[64,4096]{1,0:T(8,128)(2,1)S(1)} %get-tuple-element.47), channel_id=1, source_target_pairs={{0,3},{1,0},{2,1},{3,2},{4,7},{5,4},{6,5},{7,6},{8,11},{9,8},{10,9... | collective-permute-start | bytes 1572872 | tf_op jit(solution)/shard_map/ppermute | solution.py:220
  67.6 36.8 %collective-permute-start.11 = (bf16[64,4096]{1,0:T(8,128)(2,1)S(1)}, bf16[64,4096]{1,0:T(8,128)(2,1)S(1)}, u32[]{:S(2)}, u32[]{:S(2)}) collective-permute-start(bf16[64,4096]{1,0:T(8,128)(2,1)S(1)} %get-tuple-element.48), channel_id=1, source_target_pairs={{0,2},{1,3},{2,0},{3,1},{4,6},{5,7},{6,4},{7,5},{8,10},{9,11},{10,... | collective-permute-start | bytes 1572872 | tf_op jit(solution)/shard_map/ppermute | solution.py:220
  68.9 27.1 %collective-permute-start.14 = (bf16[72,2048]{1,0:T(8,128)(2,1)S(1)}, bf16[72,2048]{1,0:T(8,128)(2,1)S(1)}, u32[]{:S(2)}, u32[]{:S(2)}) collective-permute-start(bf16[72,2048]{1,0:T(8,128)(2,1)S(1)} %get-tuple-element.51), channel_id=1, source_target_pairs={{0,20},{4,24},{8,28},{12,0},{16,4},{20,8},{24,12},{28,16},{1,21},{... | collective-permute-start | bytes 884744 | tf_op jit(solution)/shard_map/ppermute | solution.py:220
  69.9 27.1 %collective-permute-start.15 = (bf16[72,2048]{1,0:T(8,128)(2,1)S(1)}, bf16[72,2048]{1,0:T(8,128)(2,1)S(1)}, u32[]{:S(2)}, u32[]{:S(2)}) collective-permute-start(bf16[72,2048]{1,0:T(8,128)(2,1)S(1)} %get-tuple-element.52), channel_id=1, source_target_pairs={{0,12},{4,16},{8,20},{12,24},{16,28},{20,0},{24,4},{28,8},{1,13},{... | collective-permute-start | bytes 884744 | tf_op jit(solution)/shard_map/ppermute | solution.py:220
  83.0 23.7 %collective-permute-start.12 = (bf16[64,4096]{1,0:T(8,128)(2,1)S(1)}, bf16[64,4096]{1,0:T(8,128)(2,1)S(1)}, u32[]{:S(2)}, u32[]{:S(2)}) collective-permute-start(bf16[64,4096]{1,0:T(8,128)(2,1)S(1)} %get-tuple-element.49), channel_id=1, source_target_pairs={{0,1},{1,2},{2,3},{3,0},{4,5},{5,6},{6,7},{7,4},{8,9},{9,10},{10,1... | collective-permute-start | bytes 1572872 | tf_op jit(solution)/shard_map/ppermute | solution.py:220
  95.9 23.2 %collective-permute-start.16 = (bf16[72,2048]{1,0:T(8,128)(2,1)S(1)}, bf16[72,2048]{1,0:T(8,128)(2,1)S(1)}, u32[]{:S(2)}, u32[]{:S(2)}) collective-permute-start(bf16[72,2048]{1,0:T(8,128)(2,1)S(1)} %get-tuple-element.53), channel_id=1, source_target_pairs={{0,24},{4,28},{8,0},{12,4},{16,8},{20,12},{24,16},{28,20},{1,25},{... | collective-permute-start | bytes 884744 | tf_op jit(solution)/shard_map/ppermute | solution.py:220
  97.0 22.1 %collective-permute-start.17 = (bf16[72,2048]{1,0:T(8,128)(2,1)S(1)}, bf16[72,2048]{1,0:T(8,128)(2,1)S(1)}, u32[]{:S(2)}, u32[]{:S(2)}) collective-permute-start(bf16[72,2048]{1,0:T(8,128)(2,1)S(1)} %get-tuple-element.54), channel_id=1, source_target_pairs={{0,8},{4,12},{8,16},{12,20},{16,24},{20,28},{24,0},{28,4},{1,9},{5... | collective-permute-start | bytes 884744 | tf_op jit(solution)/shard_map/ppermute | solution.py:220
  97.4 21.7 %collective-permute-start.18 = (bf16[72,2048]{1,0:T(8,128)(2,1)S(1)}, bf16[72,2048]{1,0:T(8,128)(2,1)S(1)}, u32[]{:S(2)}, u32[]{:S(2)}) collective-permute-start(bf16[72,2048]{1,0:T(8,128)(2,1)S(1)} %get-tuple-element.55), channel_id=1, source_target_pairs={{0,28},{4,0},{8,4},{12,8},{16,12},{20,16},{24,20},{28,24},{1,29},{... | collective-permute-start | bytes 884744 | tf_op jit(solution)/shard_map/ppermute | solution.py:220
  104.4 14.6 %collective-permute-start.19 = (bf16[72,2048]{1,0:T(8,128)(2,1)S(1)}, bf16[72,2048]{1,0:T(8,128)(2,1)S(1)}, u32[]{:S(2)}, u32[]{:S(2)}) collective-permute-start(bf16[72,2048]{1,0:T(8,128)(2,1)S(1)} %get-tuple-element.56), channel_id=1, source_target_pairs={{0,4},{4,8},{8,12},{12,16},{16,20},{20,24},{24,28},{28,0},{1,5},{5... | collective-permute-start | bytes 884744 | tf_op jit(solution)/shard_map/ppermute | solution.py:220
  (8 other events, 19.9 us)

commit v3 on v2

--- a/solution.py
+++ b/solution.py
@@ -9,10 +9,17 @@
 from jax.sharding import PartitionSpec as P
 
 COLUMNS = 4
+OUTER_ORDER = {8: (4, 5, 3, 2, 7, 6, 1)}
+INNER_ORDER = {4: (3, 2, 1)}
 SCALE = 3.0
 VMEM = pl.BlockSpec(memory_space=pltpu.VMEM)
 ANY = pl.BlockSpec(memory_space=pl.ANY)
 f32, bf16, i32 = jnp.float32, jnp.bfloat16, jnp.int32
+
+
+def peer_at(axis, shift, sign, size, me=None):
+    me = lax.axis_index(axis) if me is None else me
+    return lax.rem(me + sign * shift + size, size) if axis == "grp" else lax.bitwise_xor(me, jnp.int32(shift))
 
 
 class Blocks(NamedTuple):
@@ -94,7 +101,7 @@
     slot, chunk = row_plan(plan)
     asked = []
     for n, shift in enumerate(plan.shifts):
-        r = lax.rem(lax.axis_index(plan.axis) + shift, codes.shape[0])
+        r = peer_at(plan.axis, shift, 1, codes.shape[0])
         chosen = codes[pl.ds(r, 1), :] == slot[plan.part(n)]
         asked.append(jnp.where(chosen, row_ref[pl.ds(r, 1), :] + 1, 0).astype(f32))
     at = jnp.sum(jnp.concatenate(asked, axis=0), axis=1, keepdims=True)
@@ -108,7 +115,7 @@
     me = lax.axis_index(plan.axis)
     live = []
     for n, shift in enumerate(plan.shifts):
-        name = peers - 1 - shift if plan.axis == "grp" else lax.rem(me - shift + peers, peers)
+        name = peers - 1 - shift if plan.axis == "grp" else peer_at("dp", shift, -1, peers)
         used = jnp.sum((owner_ref[pl.ds(me, 1), :] == name).astype(f32), axis=1, keepdims=True)
         live.append(slot[plan.part(n)].astype(f32) < used)
     return jnp.concatenate(live, axis=0)
@@ -216,10 +223,11 @@
 
 def exchange(plan, blocks, sign):
     size = lax.axis_size(plan.axis)
-    return [
-        lax.ppermute(block, plan.axis, [(g, (g + sign * shift) % size) for g in range(size)])
-        for shift, block in zip(plan.shifts, blocks)
-    ]
+    moved = []
+    for shift, block in zip(plan.shifts, blocks):
+        pairs = [(g, (g + sign * shift) % size if plan.axis == "grp" else g ^ shift) for g in range(size)]
+        moved.append(lax.ppermute(block, plan.axis, pairs))
+    return moved
 
 
 def per_device(queries, documents, positives, inner_owner, inner_row, outer_owner, outer_row):
@@ -227,8 +235,8 @@
     dp, grp = lax.axis_size("dp"), lax.axis_size("grp")
     cap_inner = -(-max(2, 2 * rows // dp) // 16) * 16
     cap_outer = -(-max(2, 2 * rows // (grp - 1)) // 4) * 4
-    inner = Blocks("dp", tuple(range(1, dp)), cap_inner, 1)
-    outer_shifts = tuple(sorted(range(1, grp), key=lambda k: (abs(2 * k - grp), k)))
+    inner = Blocks("dp", INNER_ORDER.get(dp, tuple(range(1, dp))), cap_inner, 1)
+    outer_shifts = OUTER_ORDER.get(grp, tuple(range(1, grp)))
     outer = Blocks("grp", outer_shifts, cap_outer, 1 if cap_outer % 8 == 0 else 2)
     inner_owner, inner_row = inner_owner.reshape(dp, rows), inner_row.reshape(dp, rows)
     outer_owner, outer_row = outer_owner.reshape(grp, rows), outer_row.reshape(grp, rows)

time: 123 us -> 117 us (0.951); the launches traced: 121 us -> 117 us
  waiting for transfers between devices: 59.7 us -> 49.8 us
  starting transfers between devices: 44.9 us -> 50.6 us
    ppermute x20, waiting for transfers between devices: 59.7 us -> 49.8 us  [exchange(): moved.append(lax.ppermute(block, plan.axis, pairs))]
    ppermute x20, starting transfers between devices: 44.9 us -> 50.6 us  [exchange(): moved.append(lax.ppermute(block, plan.axis, pairs))]
  transfers between devices with their start and end apart: 20 -> 20, of which waited for: 7 -> 10; matrix products, arithmetic and copies ran while one was open for 0% -> 0% of each run, Pallas kernels for 4% -> 5%
where the time goes in v3:
time: 117 us
  starting transfers between devices  50.6 us (43%)
  waiting for transfers between devices  49.8 us (43%)
  Pallas kernels  10.4 us (9%)
  local copies, waits for them, and re-layouts  5.29 us (5%)
    ppermute x20, starting transfers between devices, exchange(): moved.append(lax.ppermute(block, plan.axis, pairs))  50.6 us
    ppermute x20, waiting for transfers between devices, exchange(): moved.append(lax.ppermute(block, plan.axis, pairs))  49.8 us
    pallas_call x8, Pallas kernels, call(): pl.pallas_call(body, out_shape=out_shape, in_specs=[VMEM] * read + [ANY]...  10.4 us
    unnamed x24, local copies, waits for them, and re-layouts  5.29 us
  transfers between devices with their start and end apart: 20, of which 10 were waited for; matrix products, arithmetic and copies ran while one was open for 0% of the time, Pallas kernels for 5%

profile of v3, /device:TPU:3, one launch (start us, length us, event | category | flops | bytes accessed | tf_op | source)
XLA Modules:
  0.0 116.8 jit_solution(12735744211061253930)
XLA Ops:
  0.7 1.3 %copy-done.1 = bf16[128,4096]{1,0:T(8,128)(2,1)S(1)} copy-done((bf16[128,4096]{1,0:T(8,128)(2,1)S(1)}, bf16[128,4096]{1,0:T(8,128)(2,1)}, u32[]{:S(2)}) %copy-start.1) | copy-done | bytes 1048600
  4.2 2.4 %collective-permute-start.3 = (bf16[72,2048]{1,0:T(8,128)(2,1)S(1)}, bf16[72,2048]{1,0:T(8,128)(2,1)S(1)}, u32[]{:S(2)}, u32[]{:S(2)}) collective-permute-start(bf16[72,2048]{1,0:T(8,128)(2,1)S(1)} %get-tuple-element.33), channel_id=1, source_target_pairs={{0,16},{4,20},{8,24},{12,28},{16,0},{20,4},{24,8},{28,12},{1,17},{... | collective-permute-start | bytes 884744 | tf_op jit(solution)/shard_map/ppermute | solution.py:229
  6.6 1.2 %copy-done.2 = bf16[128,4096]{1,0:T(8,128)(2,1)S(1)} copy-done((bf16[128,4096]{1,0:T(8,128)(2,1)S(1)}, bf16[128,4096]{1,0:T(8,128)(2,1)}, u32[]{:S(2)}) %copy-start.2) | copy-done | bytes 1048600
  10.0 2.2 %collective-permute-start = (bf16[64,4096]{1,0:T(8,128)(2,1)S(1)}, bf16[64,4096]{1,0:T(8,128)(2,1)S(1)}, u32[]{:S(2)}, u32[]{:S(2)}) collective-permute-start(bf16[64,4096]{1,0:T(8,128)(2,1)S(1)} %get-tuple-element.30), channel_id=1, source_target_pairs={{0,3},{1,2},{2,1},{3,0},{4,7},{5,6},{6,5},{7,4},{8,11},{9,10},{10,... | collective-permute-start | bytes 1572872 | tf_op jit(solution)/shard_map/ppermute | solution.py:229
  13.4 2.2 %collective-permute-start.5 = (bf16[72,2048]{1,0:T(8,128)(2,1)S(1)}, bf16[72,2048]{1,0:T(8,128)(2,1)S(1)}, u32[]{:S(2)}, u32[]{:S(2)}) collective-permute-start(bf16[72,2048]{1,0:T(8,128)(2,1)S(1)} %get-tuple-element.35), channel_id=1, source_target_pairs={{0,12},{4,16},{8,20},{12,24},{16,28},{20,0},{24,4},{28,8},{1,13},{... | collective-permute-start | bytes 884744 | tf_op jit(solution)/shard_map/ppermute | solution.py:229
  15.6 3.9 %collective-permute-done.3.refs_7_.refs_5_ = bf16[72,2048]{1,0:T(8,128)(2,1)S(1)} collective-permute-done((bf16[72,2048]{1,0:T(8,128)(2,1)S(1)}, bf16[72,2048]{1,0:T(8,128)(2,1)S(1)}, u32[]{:S(2)}, u32[]{:S(2)}) %collective-permute-start.3) | collective-permute-done | bytes 294944 | tf_op jit(solution)/shard_map/ppermute | solution.py:229
  19.5 9.0 %collective-permute-start.2 = (bf16[64,4096]{1,0:T(8,128)(2,1)S(1)}, bf16[64,4096]{1,0:T(8,128)(2,1)S(1)}, u32[]{:S(2)}, u32[]{:S(2)}) collective-permute-start(bf16[64,4096]{1,0:T(8,128)(2,1)S(1)} %get-tuple-element.32), channel_id=1, source_target_pairs={{0,1},{1,0},{2,3},{3,2},{4,5},{5,4},{6,7},{7,6},{8,9},{9,8},{10,11... | collective-permute-start | bytes 1572872 | tf_op jit(solution)/shard_map/ppermute | solution.py:229
  28.4 10.2 %collective-permute-done.4.refs_8_.refs_6_ = bf16[72,2048]{1,0:T(8,128)(2,1)S(1)} collective-permute-done((bf16[72,2048]{1,0:T(8,128)(2,1)S(1)}, bf16[72,2048]{1,0:T(8,128)(2,1)S(1)}, u32[]{:S(2)}, u32[]{:S(2)}) %collective-permute-start.4) | collective-permute-done | bytes 294944 | tf_op jit(solution)/shard_map/ppermute | solution.py:229
  39.6 4.2 %collective-permute-start.8 = (bf16[72,2048]{1,0:T(8,128)(2,1)S(1)}, bf16[72,2048]{1,0:T(8,128)(2,1)S(1)}, u32[]{:S(2)}, u32[]{:S(2)}) collective-permute-start(bf16[72,2048]{1,0:T(8,128)(2,1)S(1)} %get-tuple-element.40), channel_id=1, source_target_pairs={{0,24},{4,28},{8,0},{12,4},{16,8},{20,12},{24,16},{28,20},{1,25},{... | collective-permute-start | bytes 884744 | tf_op jit(solution)/shard_map/ppermute | solution.py:229
  46.2 2.5 %collective-permute-done.7.refs_9_ = bf16[72,2048]{1,0:T(8,128)(2,1)S(1)} collective-permute-done((bf16[72,2048]{1,0:T(8,128)(2,1)S(1)}, bf16[72,2048]{1,0:T(8,128)(2,1)S(1)}, u32[]{:S(2)}, u32[]{:S(2)}) %collective-permute-start.7) | collective-permute-done | bytes 294944 | tf_op jit(solution)/shard_map/ppermute | solution.py:229
  48.7 5.3 %collective-permute-done.9.refs_11_ = bf16[72,2048]{1,0:T(8,128)(2,1)S(1)} collective-permute-done((bf16[72,2048]{1,0:T(8,128)(2,1)S(1)}, bf16[72,2048]{1,0:T(8,128)(2,1)S(1)}, u32[]{:S(2)}, u32[]{:S(2)}) %collective-permute-start.9) | collective-permute-done | bytes 294944 | tf_op jit(solution)/shard_map/ppermute | solution.py:229
  54.1 2.1 %shard_map.97 = (f32[1,128]{1,0:T(1,128)}, bf16[320,128]{1,0:T(8,128)(2,1)S(1)}, bf16[504,128]{1,0:T(8,128)(2,1)S(1)}, bf16[504,2048]{1,0:T(8,128)(2,1)S(1)}, bf...) custom-call(bf16[128,4096]{1,0:T(8,128)(2,1)S(1)} %copy-done, ...), custom_call_target="tpu_custom_call" | custom-call | flops 1056964608 | bytes 7785472 | tf_op jit(solution)/shard_map/pallas_call | solution.py:50
  56.2 5.7 %collective-permute-start.13 = (bf16[72,2048]{1,0:T(8,128)(2,1)S(1)}, bf16[72,2048]{1,0:T(8,128)(2,1)S(1)}, u32[]{:S(2)}, u32[]{:S(2)}) collective-permute-start(bf16[72,2048]{1,0:T(8,128)(2,1)S(1)} %get-tuple-element.50), channel_id=1, source_target_pairs={{0,16},{4,20},{8,24},{12,28},{16,0},{20,4},{24,8},{28,12},{1,17},{... | collective-permute-start | bytes 884744 | tf_op jit(solution)/shard_map/ppermute | solution.py:229
  62.5 2.3 %collective-permute-start.10 = (bf16[64,4096]{1,0:T(8,128)(2,1)S(1)}, bf16[64,4096]{1,0:T(8,128)(2,1)S(1)}, u32[]{:S(2)}, u32[]{:S(2)}) collective-permute-start(bf16[64,4096]{1,0:T(8,128)(2,1)S(1)} %get-tuple-element.47), channel_id=1, source_target_pairs={{0,3},{1,2},{2,1},{3,0},{4,7},{5,6},{6,5},{7,4},{8,11},{9,10},{10,... | collective-permute-start | bytes 1572872 | tf_op jit(solution)/shard_map/ppermute | solution.py:229
  65.0 6.3 %collective-permute-start.14 = (bf16[72,2048]{1,0:T(8,128)(2,1)S(1)}, bf16[72,2048]{1,0:T(8,128)(2,1)S(1)}, u32[]{:S(2)}, u32[]{:S(2)}) collective-permute-start(bf16[72,2048]{1,0:T(8,128)(2,1)S(1)} %get-tuple-element.51), channel_id=1, source_target_pairs={{0,12},{4,16},{8,20},{12,24},{16,28},{20,0},{24,4},{28,8},{1,13},{... | collective-permute-start | bytes 884744 | tf_op jit(solution)/shard_map/ppermute | solution.py:229
  71.3 8.5 %collective-permute-done.13.refs_7_.refs_3_ = bf16[72,2048]{1,0:T(8,128)(2,1)S(1)} collective-permute-done((bf16[72,2048]{1,0:T(8,128)(2,1)S(1)}, bf16[72,2048]{1,0:T(8,128)(2,1)S(1)}, u32[]{:S(2)}, u32[]{:S(2)}) %collective-permute-start.13) | collective-permute-done | bytes 294944 | tf_op jit(solution)/shard_map/ppermute | solution.py:229
  79.8 3.1 %collective-permute-start.12 = (bf16[64,4096]{1,0:T(8,128)(2,1)S(1)}, bf16[64,4096]{1,0:T(8,128)(2,1)S(1)}, u32[]{:S(2)}, u32[]{:S(2)}) collective-permute-start(bf16[64,4096]{1,0:T(8,128)(2,1)S(1)} %get-tuple-element.49), channel_id=1, source_target_pairs={{0,1},{1,0},{2,3},{3,2},{4,5},{5,4},{6,7},{7,6},{8,9},{9,8},{10,11... | collective-permute-start | bytes 1572872 | tf_op jit(solution)/shard_map/ppermute | solution.py:229
  82.9 8.0 %collective-permute-start.16 = (bf16[72,2048]{1,0:T(8,128)(2,1)S(1)}, bf16[72,2048]{1,0:T(8,128)(2,1)S(1)}, u32[]{:S(2)}, u32[]{:S(2)}) collective-permute-start(bf16[72,2048]{1,0:T(8,128)(2,1)S(1)} %get-tuple-element.53), channel_id=1, source_target_pairs={{0,24},{4,28},{8,0},{12,4},{16,8},{20,12},{24,16},{28,20},{1,25},{... | collective-permute-start | bytes 884744 | tf_op jit(solution)/shard_map/ppermute | solution.py:229
  92.0 1.7 %collective-permute-start.17 = (bf16[72,2048]{1,0:T(8,128)(2,1)S(1)}, bf16[72,2048]{1,0:T(8,128)(2,1)S(1)}, u32[]{:S(2)}, u32[]{:S(2)}) collective-permute-start(bf16[72,2048]{1,0:T(8,128)(2,1)S(1)} %get-tuple-element.54), channel_id=1, source_target_pairs={{0,4},{4,8},{8,12},{12,16},{16,20},{20,24},{24,28},{28,0},{1,5},{5... | collective-permute-start | bytes 884744 | tf_op jit(solution)/shard_map/ppermute | solution.py:229
  94.3 2.2 %shard_map.98 = bf16[128,4096]{1,0:T(8,128)(2,1)} custom-call(bf16[320,128]{1,0:T(8,128)(2,1)S(1)} %get-tuple-element.43.refs_0_, bf16[128,4096]{1,0:T(8,128)(2,1)S(1)} %copy-done.3, bf16[192,4096]{1,0:T(8,128)(2,1)S(1)} %get-tuple-element.44.refs_2_, bf16[504,128]{1,0:T(8,128)(2,1)S(1)} %get-tuple-element.45.refs_3_, ...), custom_call_target="tpu_custom_call" | custom-call | flops 864026624 | bytes 5945344 | tf_op jit(solution)/shard_map/pallas_call | solution.py:50
  97.5 6.1 %collective-permute-done.17.refs_7_ = bf16[72,2048]{1,0:T(8,128)(2,1)S(1)} collective-permute-done((bf16[72,2048]{1,0:T(8,128)(2,1)S(1)}, bf16[72,2048]{1,0:T(8,128)(2,1)S(1)}, u32[]{:S(2)}, u32[]{:S(2)}) %collective-permute-start.17) | collective-permute-done | bytes 294944 | tf_op jit(solution)/shard_map/ppermute | solution.py:229
  103.6 6.3 %collective-permute-done.18.refs_8_ = bf16[72,2048]{1,0:T(8,128)(2,1)S(1)} collective-permute-done((bf16[72,2048]{1,0:T(8,128)(2,1)S(1)}, bf16[72,2048]{1,0:T(8,128)(2,1)S(1)}, u32[]{:S(2)}, u32[]{:S(2)}) %collective-permute-start.18) | collective-permute-done | bytes 294944 | tf_op jit(solution)/shard_map/ppermute | solution.py:229
  110.0 4.9 %collective-permute-done.19.refs_9_ = bf16[72,2048]{1,0:T(8,128)(2,1)S(1)} collective-permute-done((bf16[72,2048]{1,0:T(8,128)(2,1)S(1)}, bf16[72,2048]{1,0:T(8,128)(2,1)S(1)}, u32[]{:S(2)}, u32[]{:S(2)}) %collective-permute-start.19) | collective-permute-done | bytes 294944 | tf_op jit(solution)/shard_map/ppermute | solution.py:229
  114.8 2.0 %shard_map.101 = bf16[128,4096]{1,0:T(8,128)(2,1)} custom-call(f32[128,4096]{1,0:T(8,128)S(1)} %shard_map.100.refs_0_, s32[8,128]{1,0:T(8,128)S(1)} %bitcast.14, s32[8,128]{1,0:T(8,128)S(1)} %bitcast.16, bf16[72,2048]{1,0:T(8,128)(2,1)S(1)} %collective-permute-done.13.refs_7_.refs_3_, bf16[72,2048]{1,0:T(8,128)(2,1)S(1)} %collective-permute-done.14.refs_8_.refs_4_, ...), custom_call_target="tpu_custom_call" | custom-call | flops 528482304 | bytes 5218304 | tf_op jit(solution)/shard_map/pallas_call | solution.py:50
  (48 shorter events, 12.4 us)
Async XLA Ops:
  0.6 43.6 %copy-start = (bf16[128,4096]{1,0:T(8,128)(2,1)S(1)}, bf16[128,4096]{1,0:T(8,128)(2,1)}, u32[]{:S(2)}) copy-start(bf16[128,4096]{1,0:T(8,128)(2,1)} %refs_1_.7) | copy-start | bytes 3145732
  4.2 15.2 %collective-permute-start.3 = (bf16[72,2048]{1,0:T(8,128)(2,1)S(1)}, bf16[72,2048]{1,0:T(8,128)(2,1)S(1)}, u32[]{:S(2)}, u32[]{:S(2)}) collective-permute-start(bf16[72,2048]{1,0:T(8,128)(2,1)S(1)} %get-tuple-element.33), channel_id=1, source_target_pairs={{0,16},{4,20},{8,24},{12,28},{16,0},{20,4},{24,8},{28,12},{1,17},{... | collective-permute-start | bytes 884744 | tf_op jit(solution)/shard_map/ppermute | solution.py:229
  10.0 29.6 %collective-permute-start = (bf16[64,4096]{1,0:T(8,128)(2,1)S(1)}, bf16[64,4096]{1,0:T(8,128)(2,1)S(1)}, u32[]{:S(2)}, u32[]{:S(2)}) collective-permute-start(bf16[64,4096]{1,0:T(8,128)(2,1)S(1)} %get-tuple-element.30), channel_id=1, source_target_pairs={{0,3},{1,2},{2,1},{3,0},{4,7},{5,6},{6,5},{7,4},{8,11},{9,10},{10,... | collective-permute-start | bytes 1572872 | tf_op jit(solution)/shard_map/ppermute | solution.py:229
  12.1 31.7 %collective-permute-start.1 = (bf16[64,4096]{1,0:T(8,128)(2,1)S(1)}, bf16[64,4096]{1,0:T(8,128)(2,1)S(1)}, u32[]{:S(2)}, u32[]{:S(2)}) collective-permute-start(bf16[64,4096]{1,0:T(8,128)(2,1)S(1)} %get-tuple-element.31), channel_id=1, source_target_pairs={{0,2},{1,3},{2,0},{3,1},{4,6},{5,7},{6,4},{7,5},{8,10},{9,11},{10,... | collective-permute-start | bytes 1572872 | tf_op jit(solution)/shard_map/ppermute | solution.py:229
  12.4 26.2 %collective-permute-start.4 = (bf16[72,2048]{1,0:T(8,128)(2,1)S(1)}, bf16[72,2048]{1,0:T(8,128)(2,1)S(1)}, u32[]{:S(2)}, u32[]{:S(2)}) collective-permute-start(bf16[72,2048]{1,0:T(8,128)(2,1)S(1)} %get-tuple-element.34), channel_id=1, source_target_pairs={{0,20},{4,24},{8,28},{12,0},{16,4},{20,8},{24,12},{28,16},{1,21},{... | collective-permute-start | bytes 884744 | tf_op jit(solution)/shard_map/ppermute | solution.py:229
  13.4 25.2 %collective-permute-start.5 = (bf16[72,2048]{1,0:T(8,128)(2,1)S(1)}, bf16[72,2048]{1,0:T(8,128)(2,1)S(1)}, u32[]{:S(2)}, u32[]{:S(2)}) collective-permute-start(bf16[72,2048]{1,0:T(8,128)(2,1)S(1)} %get-tuple-element.35), channel_id=1, source_target_pairs={{0,12},{4,16},{8,20},{12,24},{16,28},{20,0},{24,4},{28,8},{1,13},{... | collective-permute-start | bytes 884744 | tf_op jit(solution)/shard_map/ppermute | solution.py:229
  19.5 24.8 %collective-permute-start.2 = (bf16[64,4096]{1,0:T(8,128)(2,1)S(1)}, bf16[64,4096]{1,0:T(8,128)(2,1)S(1)}, u32[]{:S(2)}, u32[]{:S(2)}) collective-permute-start(bf16[64,4096]{1,0:T(8,128)(2,1)S(1)} %get-tuple-element.32), channel_id=1, source_target_pairs={{0,1},{1,0},{2,3},{3,2},{4,5},{5,4},{6,7},{7,6},{8,9},{9,8},{10,11... | collective-permute-start | bytes 1572872 | tf_op jit(solution)/shard_map/ppermute | solution.py:229
  38.6 7.6 %collective-permute-start.6 = (bf16[72,2048]{1,0:T(8,128)(2,1)S(1)}, bf16[72,2048]{1,0:T(8,128)(2,1)S(1)}, u32[]{:S(2)}, u32[]{:S(2)}) collective-permute-start(bf16[72,2048]{1,0:T(8,128)(2,1)S(1)} %get-tuple-element.38), channel_id=1, source_target_pairs={{0,8},{4,12},{8,16},{12,20},{16,24},{20,28},{24,0},{28,4},{1,9},{5... | collective-permute-start | bytes 884744 | tf_op jit(solution)/shard_map/ppermute | solution.py:229
  38.6 10.1 %collective-permute-start.7 = (bf16[72,2048]{1,0:T(8,128)(2,1)S(1)}, bf16[72,2048]{1,0:T(8,128)(2,1)S(1)}, u32[]{:S(2)}, u32[]{:S(2)}) collective-permute-start(bf16[72,2048]{1,0:T(8,128)(2,1)S(1)} %get-tuple-element.39), channel_id=1, source_target_pairs={{0,28},{4,0},{8,4},{12,8},{16,12},{20,16},{24,20},{28,24},{1,29},{... | collective-permute-start | bytes 884744 | tf_op jit(solution)/shard_map/ppermute | solution.py:229
  39.6 9.1 %collective-permute-start.8 = (bf16[72,2048]{1,0:T(8,128)(2,1)S(1)}, bf16[72,2048]{1,0:T(8,128)(2,1)S(1)}, u32[]{:S(2)}, u32[]{:S(2)}) collective-permute-start(bf16[72,2048]{1,0:T(8,128)(2,1)S(1)} %get-tuple-element.40), channel_id=1, source_target_pairs={{0,24},{4,28},{8,0},{12,4},{16,8},{20,12},{24,16},{28,20},{1,25},{... | collective-permute-start | bytes 884744 | tf_op jit(solution)/shard_map/ppermute | solution.py:229
  43.9 10.2 %copy-start.11 = (s32[128]{0:T(128)S(1)}, s32[128]{0:T(128)}, u32[]{:S(2)}) copy-start(s32[128]{0:T(128)} %param.9) | copy-start | bytes 1540
  43.9 10.2 %collective-permute-start.9 = (bf16[72,2048]{1,0:T(8,128)(2,1)S(1)}, bf16[72,2048]{1,0:T(8,128)(2,1)S(1)}, u32[]{:S(2)}, u32[]{:S(2)}) collective-permute-start(bf16[72,2048]{1,0:T(8,128)(2,1)S(1)} %get-tuple-element.41), channel_id=1, source_target_pairs={{0,4},{4,8},{8,12},{12,16},{16,20},{20,24},{24,28},{28,0},{1,5},{5... | collective-permute-start | bytes 884744 | tf_op jit(solution)/shard_map/ppermute | solution.py:229
  54.1 40.2 %copy-start.3 = (bf16[128,4096]{1,0:T(8,128)(2,1)S(1)}, bf16[128,4096]{1,0:T(8,128)(2,1)}, u32[]{:S(2)}) copy-start(bf16[128,4096]{1,0:T(8,128)(2,1)} %refs_1_.5) | copy-start | bytes 3145732
  56.2 23.6 %collective-permute-start.13 = (bf16[72,2048]{1,0:T(8,128)(2,1)S(1)}, bf16[72,2048]{1,0:T(8,128)(2,1)S(1)}, u32[]{:S(2)}, u32[]{:S(2)}) collective-permute-start(bf16[72,2048]{1,0:T(8,128)(2,1)S(1)} %get-tuple-element.50), channel_id=1, source_target_pairs={{0,16},{4,20},{8,24},{12,28},{16,0},{20,4},{24,8},{28,12},{1,17},{... | collective-permute-start | bytes 884744 | tf_op jit(solution)/shard_map/ppermute | solution.py:229
  62.5 31.1 %collective-permute-start.10 = (bf16[64,4096]{1,0:T(8,128)(2,1)S(1)}, bf16[64,4096]{1,0:T(8,128)(2,1)S(1)}, u32[]{:S(2)}, u32[]{:S(2)}) collective-permute-start(bf16[64,4096]{1,0:T(8,128)(2,1)S(1)} %get-tuple-element.47), channel_id=1, source_target_pairs={{0,3},{1,2},{2,1},{3,0},{4,7},{5,6},{6,5},{7,4},{8,11},{9,10},{10,... | collective-permute-start | bytes 1572872 | tf_op jit(solution)/shard_map/ppermute | solution.py:229
  64.8 28.8 %collective-permute-start.11 = (bf16[64,4096]{1,0:T(8,128)(2,1)S(1)}, bf16[64,4096]{1,0:T(8,128)(2,1)S(1)}, u32[]{:S(2)}, u32[]{:S(2)}) collective-permute-start(bf16[64,4096]{1,0:T(8,128)(2,1)S(1)} %get-tuple-element.48), channel_id=1, source_target_pairs={{0,2},{1,3},{2,0},{3,1},{4,6},{5,7},{6,4},{7,5},{8,10},{9,11},{10,... | collective-permute-start | bytes 1572872 | tf_op jit(solution)/shard_map/ppermute | solution.py:229
  65.0 17.9 %collective-permute-start.14 = (bf16[72,2048]{1,0:T(8,128)(2,1)S(1)}, bf16[72,2048]{1,0:T(8,128)(2,1)S(1)}, u32[]{:S(2)}, u32[]{:S(2)}) collective-permute-start(bf16[72,2048]{1,0:T(8,128)(2,1)S(1)} %get-tuple-element.51), channel_id=1, source_target_pairs={{0,12},{4,16},{8,20},{12,24},{16,28},{20,0},{24,4},{28,8},{1,13},{... | collective-permute-start | bytes 884744 | tf_op jit(solution)/shard_map/ppermute | solution.py:229
  71.3 20.6 %collective-permute-start.15 = (bf16[72,2048]{1,0:T(8,128)(2,1)S(1)}, bf16[72,2048]{1,0:T(8,128)(2,1)S(1)}, u32[]{:S(2)}, u32[]{:S(2)}) collective-permute-start(bf16[72,2048]{1,0:T(8,128)(2,1)S(1)} %get-tuple-element.52), channel_id=1, source_target_pairs={{0,20},{4,24},{8,28},{12,0},{16,4},{20,8},{24,12},{28,16},{1,21},{... | collective-permute-start | bytes 884744 | tf_op jit(solution)/shard_map/ppermute | solution.py:229
  79.8 16.7 %collective-permute-start.12 = (bf16[64,4096]{1,0:T(8,128)(2,1)S(1)}, bf16[64,4096]{1,0:T(8,128)(2,1)S(1)}, u32[]{:S(2)}, u32[]{:S(2)}) collective-permute-start(bf16[64,4096]{1,0:T(8,128)(2,1)S(1)} %get-tuple-element.49), channel_id=1, source_target_pairs={{0,1},{1,0},{2,3},{3,2},{4,5},{5,4},{6,7},{7,6},{8,9},{9,8},{10,11... | collective-permute-start | bytes 1572872 | tf_op jit(solution)/shard_map/ppermute | solution.py:229
  82.9 14.6 %collective-permute-start.16 = (bf16[72,2048]{1,0:T(8,128)(2,1)S(1)}, bf16[72,2048]{1,0:T(8,128)(2,1)S(1)}, u32[]{:S(2)}, u32[]{:S(2)}) collective-permute-start(bf16[72,2048]{1,0:T(8,128)(2,1)S(1)} %get-tuple-element.53), channel_id=1, source_target_pairs={{0,24},{4,28},{8,0},{12,4},{16,8},{20,12},{24,16},{28,20},{1,25},{... | collective-permute-start | bytes 884744 | tf_op jit(solution)/shard_map/ppermute | solution.py:229
  92.0 11.7 %collective-permute-start.17 = (bf16[72,2048]{1,0:T(8,128)(2,1)S(1)}, bf16[72,2048]{1,0:T(8,128)(2,1)S(1)}, u32[]{:S(2)}, u32[]{:S(2)}) collective-permute-start(bf16[72,2048]{1,0:T(8,128)(2,1)S(1)} %get-tuple-element.54), channel_id=1, source_target_pairs={{0,4},{4,8},{8,12},{12,16},{16,20},{20,24},{24,28},{28,0},{1,5},{5... | collective-permute-start | bytes 884744 | tf_op jit(solution)/shard_map/ppermute | solution.py:229
  93.6 16.3 %collective-permute-start.18 = (bf16[72,2048]{1,0:T(8,128)(2,1)S(1)}, bf16[72,2048]{1,0:T(8,128)(2,1)S(1)}, u32[]{:S(2)}, u32[]{:S(2)}) collective-permute-start(bf16[72,2048]{1,0:T(8,128)(2,1)S(1)} %get-tuple-element.55), channel_id=1, source_target_pairs={{0,8},{4,12},{8,16},{12,20},{16,24},{20,28},{24,0},{28,4},{1,9},{5... | collective-permute-start | bytes 884744 | tf_op jit(solution)/shard_map/ppermute | solution.py:229
  93.7 21.2 %collective-permute-start.19 = (bf16[72,2048]{1,0:T(8,128)(2,1)S(1)}, bf16[72,2048]{1,0:T(8,128)(2,1)S(1)}, u32[]{:S(2)}, u32[]{:S(2)}) collective-permute-start(bf16[72,2048]{1,0:T(8,128)(2,1)S(1)} %get-tuple-element.56), channel_id=1, source_target_pairs={{0,28},{4,0},{8,4},{12,8},{16,12},{20,16},{24,20},{28,24},{1,29},{... | collective-permute-start | bytes 884744 | tf_op jit(solution)/shard_map/ppermute | solution.py:229
  96.5 18.3 %copy-start.10 = (s32[1,8,128,1]{2,3,1,0:T(1,128)S(1)}, s32[1,8,128,1]{2,3,1,0:T(1,128)}, u32[]{:S(2)}) copy-start(s32[1,8,128,1]{2,3,1,0:T(1,128)} %param.13) | copy-start | bytes 12292
  (8 other events, 17.8 us)

commit v4 on v3

--- a/solution.py
+++ b/solution.py
@@ -9,8 +9,7 @@
 from jax.sharding import PartitionSpec as P
 
 COLUMNS = 4
-OUTER_ORDER = {8: (4, 5, 3, 2, 7, 6, 1)}
-INNER_ORDER = {4: (3, 2, 1)}
+ORDER = {("grp", 8): (4, 5, 3, 2, 7, 6, 1), ("dp", 4): (3, 2, 1)}
 SCALE = 3.0
 VMEM = pl.BlockSpec(memory_space=pltpu.VMEM)
 ANY = pl.BlockSpec(memory_space=pl.ANY)
@@ -202,31 +201,37 @@
         out[:, cols] = add_far(plan, far_w, far_ref, acc, cols).astype(bf16)
 
 
-def near_grad_kernel(plan, near_w, q_ref, owner_ref, row_ref, *refs):
-    *blocks, out, codes = refs
+def near_grad_kernel(plan, outer, near_w, q_ref, owner_ref, row_ref, outer_owner_ref, outer_row_ref, *refs):
+    blocks, (out, *selects, codes, outer_codes) = refs[: len(plan.shifts)], refs[len(plan.shifts) :]
+    slot_codes(outer.axis, outer_owner_ref, outer_codes)
+    select, chunk = slot_onehot(outer, outer_codes, outer_row_ref)
+    for c, select_out in enumerate(selects):
+        select_out[...] = jnp.where(chunk == c, select, 0.0).astype(bf16)
     slot_codes(plan.axis, owner_ref, codes)
     onehot, _ = slot_onehot(plan, codes, row_ref)
     block = jnp.concatenate([block[...] for block in blocks], axis=0)
     out[...] = dot(near_w[: q_ref.shape[0], :], q_ref[...]) + dot(onehot.astype(bf16), block, TN)
 
 
-def doc_grad_kernel(plan, near_ref, owner_ref, row_ref, *refs):
-    *blocks, out, codes = refs
-    slot_codes(plan.axis, owner_ref, codes)
-    onehot, _ = slot_onehot(plan, codes, row_ref)
+def doc_grad_kernel(near_ref, *refs):
+    *refs, out = refs
+    split = out.shape[1] // refs[-1].shape[1]
+    selects, blocks = refs[:split], refs[split:]
     block = jnp.concatenate([block[...] for block in blocks], axis=0)
-    width = out.shape[1] // COLUMNS
-    for c in range(COLUMNS):
-        cols = slice(c * width, (c + 1) * width)
-        out[:, cols] = add_far(plan, onehot, block, near_ref[:, cols], cols).astype(bf16)
-
-
-def exchange(plan, blocks, sign):
+    width = block.shape[1]
+    for c, select in enumerate(selects):
+        for half in range(2):
+            cols = slice(half * width // 2, (half + 1) * width // 2)
+            at = slice(c * width + cols.start, c * width + cols.stop)
+            out[:, at] = (near_ref[:, at] + dot(select[...], block[:, cols], TN)).astype(bf16)
+
+
+def exchange(plan, blocks, back=False):
     size = lax.axis_size(plan.axis)
     moved = []
     for shift, block in zip(plan.shifts, blocks):
-        pairs = [(g, (g + sign * shift) % size if plan.axis == "grp" else g ^ shift) for g in range(size)]
-        moved.append(lax.ppermute(block, plan.axis, pairs))
+        there = [(g, (g + shift) % size if plan.axis == "grp" else g ^ shift) for g in range(size)]
+        moved.append(lax.ppermute(block, plan.axis, [(b, a) for a, b in there] if back else there))
     return moved
 
 
@@ -235,8 +240,8 @@
     dp, grp = lax.axis_size("dp"), lax.axis_size("grp")
     cap_inner = -(-max(2, 2 * rows // dp) // 16) * 16
     cap_outer = -(-max(2, 2 * rows // (grp - 1)) // 4) * 4
-    inner = Blocks("dp", INNER_ORDER.get(dp, tuple(range(1, dp))), cap_inner, 1)
-    outer_shifts = OUTER_ORDER.get(grp, tuple(range(1, grp)))
+    inner = Blocks("dp", ORDER.get(("dp", dp), tuple(range(1, dp))), cap_inner, 1)
+    outer_shifts = ORDER.get(("grp", grp), tuple(range(1, grp)))
     outer = Blocks("grp", outer_shifts, cap_outer, 1 if cap_outer % 8 == 0 else 2)
     inner_owner, inner_row = inner_owner.reshape(dp, rows), inner_row.reshape(dp, rows)
     outer_owner, outer_row = outer_owner.reshape(grp, rows), outer_row.reshape(grp, rows)
@@ -247,19 +252,25 @@
     far_flops, inner_flops, own_flops = 2 * outer.total * rows * width, 2 * inner.total * rows * width, 2 * rows * rows * width
 
     send = call(
-        functools.partial(send_kernel, outer),
-        outer_blocks,
+        functools.partial(send_kernel, outer._replace(shifts=outer.shifts[:1])),
+        outer_blocks[:1],
         outer_owner, outer_row, documents,
         scratch=outer_codes, flops=far_flops,
     )
-    got = exchange(outer, send, 1)
+    send += call(
+        functools.partial(send_kernel, outer._replace(shifts=outer.shifts[1:])),
+        outer_blocks[1:],
+        outer_owner, outer_row, documents, send[0],
+        scratch=outer_codes, flops=far_flops, unread=1,
+    )
+    got = exchange(outer, send)
     send_inner = call(
         functools.partial(send_kernel, inner),
         inner_blocks,
         inner_owner, inner_row, documents,
-        scratch=inner_codes, flops=inner_flops, unread=0,
-    )
-    got_inner = exchange(inner, send_inner, 1)
+        scratch=inner_codes, flops=inner_flops,
+    )
+    got_inner = exchange(inner, send_inner)
     scores, times, inner_rows = call(
         functools.partial(near_kernel, inner),
         [shape((rows + inner.total, rows), f32)] * 2 + [shape((inner.total, width), bf16)],
@@ -278,7 +289,7 @@
         queries, scores, times, positives.reshape(1, rows), outer_owner, *got,
         flops=2 * far_flops,
     )
-    back = exchange(outer, grads, -1)
+    back = exchange(outer, grads, back=True)
     query_grads = call(
         functools.partial(query_grad_kernel, outer),
         shape((rows, width), bf16),
@@ -289,21 +300,16 @@
         functools.partial(inner_grad_kernel, inner),
         inner_blocks,
         near_w, queries,
-        flops=inner_flops, unread=0,
-    )
-    back_inner = exchange(inner, grads_inner, -1)
-    near_grads = call(
-        functools.partial(near_grad_kernel, inner),
-        shape((rows, width), f32),
-        near_w, queries, inner_owner, inner_row, *back_inner, back[0], back[1], back[2],
-        scratch=inner_codes, flops=inner_flops + own_flops, unread=3,
-    )
-    doc_grads = call(
-        functools.partial(doc_grad_kernel, outer),
-        shape((rows, width), bf16),
-        near_grads, outer_owner, outer_row, *back,
-        scratch=outer_codes, flops=far_flops,
-    )
+        flops=inner_flops,
+    )
+    back_inner = exchange(inner, grads_inner, back=True)
+    near_grads, *selects = call(
+        functools.partial(near_grad_kernel, inner, outer),
+        [shape((rows, width), f32)] + [shape((outer.total, rows), bf16)] * outer.split,
+        near_w, queries, inner_owner, inner_row, outer_owner, outer_row, *back_inner, back[0], back[1], back[2],
+        scratch=inner_codes + outer_codes, flops=inner_flops + own_flops, unread=3,
+    )
+    doc_grads = call(doc_grad_kernel, shape((rows, width), bf16), near_grads, *selects, *back, flops=far_flops)
     return losses.reshape(rows), query_grads, doc_grads
 
 

time: 117 us -> 116 us (level)
  local copies, waits for them, and re-layouts: 5.29 us -> 3.99 us
    unnamed x24, local copies, waits for them, and re-layouts: 5.29 us -> 3.99 us
    pallas_call x8 -> x9, Pallas kernels: 10.4 us -> 10.5 us  [call(): pl.pallas_call(body, out_shape=out_shape, in_specs=[VMEM] * read + [ANY]...]
where the time goes in v4:
time: 116 us
  starting transfers between devices  50.6 us (44%)
  waiting for transfers between devices  50.2 us (43%)
  Pallas kernels  10.5 us (9%)
  local copies, waits for them, and re-layouts  3.99 us (3%)
    ppermute x20, starting transfers between devices, exchange(): lax.ppermute(block, plan.axis, [(b, a) for a, b in there] if back else th...  50.6 us
    ppermute x20, waiting for transfers between devices, exchange(): lax.ppermute(block, plan.axis, [(b, a) for a, b in there] if back else th...  50.2 us
    pallas_call x9, Pallas kernels, call(): pl.pallas_call(body, out_shape=out_shape, in_specs=[VMEM] * read + [ANY]...  10.5 us
    unnamed x24, local copies, waits for them, and re-layouts  3.99 us
  transfers between devices with their start and end apart: 20, of which 10 were waited for; matrix products, arithmetic and copies ran while one was open for 0% of the time, Pallas kernels for 5%

profile of v4, /device:TPU:3, one launch (start us, length us, event | category | flops | bytes accessed | tf_op | source)
XLA Modules:
  0.0 116.0 jit_solution(9547199710199844042)
XLA Ops:
  0.7 1.2 %copy-done = bf16[128,4096]{1,0:T(8,128)(2,1)S(1)} copy-done((bf16[128,4096]{1,0:T(8,128)(2,1)S(1)}, bf16[128,4096]{1,0:T(8,128)(2,1)}, u32[]{:S(2)}) %copy-start) | copy-done | bytes 1048600
  3.7 2.4 %collective-permute-start.3 = (bf16[72,2048]{1,0:T(8,128)(2,1)S(1)}, bf16[72,2048]{1,0:T(8,128)(2,1)S(1)}, u32[]{:S(2)}, u32[]{:S(2)}) collective-permute-start(bf16[72,2048]{1,0:T(8,128)(2,1)S(1)} %shard_map.95.refs_3_), channel_id=1, source_target_pairs={{0,16},{4,20},{8,24},{12,28},{16,0},{20,4},{24,8},{28,12},{1,17},{... | collective-permute-start | bytes 884744 | tf_op jit(solution)/shard_map/ppermute | solution.py:234
  8.2 2.2 %collective-permute-start = (bf16[64,4096]{1,0:T(8,128)(2,1)S(1)}, bf16[64,4096]{1,0:T(8,128)(2,1)S(1)}, u32[]{:S(2)}, u32[]{:S(2)}) collective-permute-start(bf16[64,4096]{1,0:T(8,128)(2,1)S(1)} %get-tuple-element.32), channel_id=1, source_target_pairs={{0,3},{1,2},{2,1},{3,0},{4,7},{5,6},{6,5},{7,4},{8,11},{9,10},{10,... | collective-permute-start | bytes 1572872 | tf_op jit(solution)/shard_map/ppermute | solution.py:234
  11.5 1.4 %collective-permute-start.4 = (bf16[72,2048]{1,0:T(8,128)(2,1)S(1)}, bf16[72,2048]{1,0:T(8,128)(2,1)S(1)}, u32[]{:S(2)}, u32[]{:S(2)}) collective-permute-start(bf16[72,2048]{1,0:T(8,128)(2,1)S(1)} %get-tuple-element.35), channel_id=1, source_target_pairs={{0,20},{4,24},{8,28},{12,0},{16,4},{20,8},{24,12},{28,16},{1,21},{... | collective-permute-start | bytes 884744 | tf_op jit(solution)/shard_map/ppermute | solution.py:234
  12.9 1.9 %collective-permute-start.5 = (bf16[72,2048]{1,0:T(8,128)(2,1)S(1)}, bf16[72,2048]{1,0:T(8,128)(2,1)S(1)}, u32[]{:S(2)}, u32[]{:S(2)}) collective-permute-start(bf16[72,2048]{1,0:T(8,128)(2,1)S(1)} %get-tuple-element.36), channel_id=1, source_target_pairs={{0,12},{4,16},{8,20},{12,24},{16,28},{20,0},{24,4},{28,8},{1,13},{... | collective-permute-start | bytes 884744 | tf_op jit(solution)/shard_map/ppermute | solution.py:234
  14.8 4.2 %collective-permute-done.3.refs_7_.refs_5_ = bf16[72,2048]{1,0:T(8,128)(2,1)S(1)} collective-permute-done((bf16[72,2048]{1,0:T(8,128)(2,1)S(1)}, bf16[72,2048]{1,0:T(8,128)(2,1)S(1)}, u32[]{:S(2)}, u32[]{:S(2)}) %collective-permute-start.3) | collective-permute-done | bytes 294944 | tf_op jit(solution)/shard_map/ppermute | solution.py:234
  19.0 9.0 %collective-permute-start.2 = (bf16[64,4096]{1,0:T(8,128)(2,1)S(1)}, bf16[64,4096]{1,0:T(8,128)(2,1)S(1)}, u32[]{:S(2)}, u32[]{:S(2)}) collective-permute-start(bf16[64,4096]{1,0:T(8,128)(2,1)S(1)} %get-tuple-element.34), channel_id=1, source_target_pairs={{0,1},{1,0},{2,3},{3,2},{4,5},{5,4},{6,7},{7,6},{8,9},{9,8},{10,11... | collective-permute-start | bytes 1572872 | tf_op jit(solution)/shard_map/ppermute | solution.py:234
  27.9 10.2 %collective-permute-done.4.refs_8_.refs_6_ = bf16[72,2048]{1,0:T(8,128)(2,1)S(1)} collective-permute-done((bf16[72,2048]{1,0:T(8,128)(2,1)S(1)}, bf16[72,2048]{1,0:T(8,128)(2,1)S(1)}, u32[]{:S(2)}, u32[]{:S(2)}) %collective-permute-start.4) | collective-permute-done | bytes 294944 | tf_op jit(solution)/shard_map/ppermute | solution.py:234
  39.1 4.2 %collective-permute-start.8 = (bf16[72,2048]{1,0:T(8,128)(2,1)S(1)}, bf16[72,2048]{1,0:T(8,128)(2,1)S(1)}, u32[]{:S(2)}, u32[]{:S(2)}) collective-permute-start(bf16[72,2048]{1,0:T(8,128)(2,1)S(1)} %get-tuple-element.41), channel_id=1, source_target_pairs={{0,24},{4,28},{8,0},{12,4},{16,8},{20,12},{24,16},{28,20},{1,25},{... | collective-permute-start | bytes 884744 | tf_op jit(solution)/shard_map/ppermute | solution.py:234
  45.7 2.5 %collective-permute-done.7.refs_9_ = bf16[72,2048]{1,0:T(8,128)(2,1)S(1)} collective-permute-done((bf16[72,2048]{1,0:T(8,128)(2,1)S(1)}, bf16[72,2048]{1,0:T(8,128)(2,1)S(1)}, u32[]{:S(2)}, u32[]{:S(2)}) %collective-permute-start.7) | collective-permute-done | bytes 294944 | tf_op jit(solution)/shard_map/ppermute | solution.py:234
  48.2 5.4 %collective-permute-done.9.refs_11_ = bf16[72,2048]{1,0:T(8,128)(2,1)S(1)} collective-permute-done((bf16[72,2048]{1,0:T(8,128)(2,1)S(1)}, bf16[72,2048]{1,0:T(8,128)(2,1)S(1)}, u32[]{:S(2)}, u32[]{:S(2)}) %collective-permute-start.9) | collective-permute-done | bytes 294944 | tf_op jit(solution)/shard_map/ppermute | solution.py:234
  53.6 2.1 %shard_map.98 = (f32[1,128]{1,0:T(1,128)}, bf16[320,128]{1,0:T(8,128)(2,1)S(1)}, bf16[504,128]{1,0:T(8,128)(2,1)S(1)}, bf16[504,2048]{1,0:T(8,128)(2,1)S(1)}, bf...) custom-call(bf16[128,4096]{1,0:T(8,128)(2,1)S(1)} %copy-done.2, ...), custom_call_target="tpu_custom_call" | custom-call | flops 1056964608 | bytes 7785472 | tf_op jit(solution)/shard_map/pallas_call | solution.py:49
  55.7 5.7 %collective-permute-start.13 = (bf16[72,2048]{1,0:T(8,128)(2,1)S(1)}, bf16[72,2048]{1,0:T(8,128)(2,1)S(1)}, u32[]{:S(2)}, u32[]{:S(2)}) collective-permute-start(bf16[72,2048]{1,0:T(8,128)(2,1)S(1)} %get-tuple-element.51), channel_id=1, source_target_pairs={{16,0},{20,4},{24,8},{28,12},{0,16},{4,20},{8,24},{12,28},{17,1},{... | collective-permute-start | bytes 884744 | tf_op jit(solution)/shard_map/ppermute | solution.py:234
  62.0 2.3 %collective-permute-start.10 = (bf16[64,4096]{1,0:T(8,128)(2,1)S(1)}, bf16[64,4096]{1,0:T(8,128)(2,1)S(1)}, u32[]{:S(2)}, u32[]{:S(2)}) collective-permute-start(bf16[64,4096]{1,0:T(8,128)(2,1)S(1)} %get-tuple-element.48), channel_id=1, source_target_pairs={{3,0},{2,1},{1,2},{0,3},{7,4},{6,5},{5,6},{4,7},{11,8},{10,9},{9,1... | collective-permute-start | bytes 1572872 | tf_op jit(solution)/shard_map/ppermute | solution.py:234
  64.5 6.3 %collective-permute-start.14 = (bf16[72,2048]{1,0:T(8,128)(2,1)S(1)}, bf16[72,2048]{1,0:T(8,128)(2,1)S(1)}, u32[]{:S(2)}, u32[]{:S(2)}) collective-permute-start(bf16[72,2048]{1,0:T(8,128)(2,1)S(1)} %get-tuple-element.52), channel_id=1, source_target_pairs={{20,0},{24,4},{28,8},{0,12},{4,16},{8,20},{12,24},{16,28},{21,1},{... | collective-permute-start | bytes 884744 | tf_op jit(solution)/shard_map/ppermute | solution.py:234
  70.8 8.5 %collective-permute-done.13.refs_9_.refs_3_ = bf16[72,2048]{1,0:T(8,128)(2,1)S(1)} collective-permute-done((bf16[72,2048]{1,0:T(8,128)(2,1)S(1)}, bf16[72,2048]{1,0:T(8,128)(2,1)S(1)}, u32[]{:S(2)}, u32[]{:S(2)}) %collective-permute-start.13) | collective-permute-done | bytes 294944 | tf_op jit(solution)/shard_map/ppermute | solution.py:234
  79.3 3.1 %collective-permute-start.12 = (bf16[64,4096]{1,0:T(8,128)(2,1)S(1)}, bf16[64,4096]{1,0:T(8,128)(2,1)S(1)}, u32[]{:S(2)}, u32[]{:S(2)}) collective-permute-start(bf16[64,4096]{1,0:T(8,128)(2,1)S(1)} %get-tuple-element.50), channel_id=1, source_target_pairs={{1,0},{0,1},{3,2},{2,3},{5,4},{4,5},{7,6},{6,7},{9,8},{8,9},{11,10... | collective-permute-start | bytes 1572872 | tf_op jit(solution)/shard_map/ppermute | solution.py:234
  82.4 8.0 %collective-permute-start.16 = (bf16[72,2048]{1,0:T(8,128)(2,1)S(1)}, bf16[72,2048]{1,0:T(8,128)(2,1)S(1)}, u32[]{:S(2)}, u32[]{:S(2)}) collective-permute-start(bf16[72,2048]{1,0:T(8,128)(2,1)S(1)} %get-tuple-element.57), channel_id=1, source_target_pairs={{8,0},{12,4},{16,8},{20,12},{24,16},{28,20},{0,24},{4,28},{9,1},{1... | collective-permute-start | bytes 884744 | tf_op jit(solution)/shard_map/ppermute | solution.py:234
  91.4 1.7 %collective-permute-start.17 = (bf16[72,2048]{1,0:T(8,128)(2,1)S(1)}, bf16[72,2048]{1,0:T(8,128)(2,1)S(1)}, u32[]{:S(2)}, u32[]{:S(2)}) collective-permute-start(bf16[72,2048]{1,0:T(8,128)(2,1)S(1)} %get-tuple-element.58), channel_id=1, source_target_pairs={{28,0},{0,4},{4,8},{8,12},{12,16},{16,20},{20,24},{24,28},{29,1},{... | collective-permute-start | bytes 884744 | tf_op jit(solution)/shard_map/ppermute | solution.py:234
  93.7 2.2 %shard_map.99 = bf16[128,4096]{1,0:T(8,128)(2,1)} custom-call(bf16[320,128]{1,0:T(8,128)(2,1)S(1)} %get-tuple-element.44.refs_0_, bf16[128,4096]{1,0:T(8,128)(2,1)S(1)} %copy-done.1, bf16[192,4096]{1,0:T(8,128)(2,1)S(1)} %get-tuple-element.45.refs_2_, bf16[504,128]{1,0:T(8,128)(2,1)S(1)} %get-tuple-element.46.refs_3_, ...), custom_call_target="tpu_custom_call" | custom-call | flops 864026624 | bytes 5945344 | tf_op jit(solution)/shard_map/pallas_call | solution.py:49
  97.0 6.1 %collective-permute-done.17.refs_7_ = bf16[72,2048]{1,0:T(8,128)(2,1)S(1)} collective-permute-done((bf16[72,2048]{1,0:T(8,128)(2,1)S(1)}, bf16[72,2048]{1,0:T(8,128)(2,1)S(1)}, u32[]{:S(2)}, u32[]{:S(2)}) %collective-permute-start.17) | collective-permute-done | bytes 294944 | tf_op jit(solution)/shard_map/ppermute | solution.py:234
  103.1 6.3 %collective-permute-done.18.refs_8_ = bf16[72,2048]{1,0:T(8,128)(2,1)S(1)} collective-permute-done((bf16[72,2048]{1,0:T(8,128)(2,1)S(1)}, bf16[72,2048]{1,0:T(8,128)(2,1)S(1)}, u32[]{:S(2)}, u32[]{:S(2)}) %collective-permute-start.18) | collective-permute-done | bytes 294944 | tf_op jit(solution)/shard_map/ppermute | solution.py:234
  109.5 4.8 %collective-permute-done.19.refs_9_ = bf16[72,2048]{1,0:T(8,128)(2,1)S(1)} collective-permute-done((bf16[72,2048]{1,0:T(8,128)(2,1)S(1)}, bf16[72,2048]{1,0:T(8,128)(2,1)S(1)}, u32[]{:S(2)}, u32[]{:S(2)}) %collective-permute-start.19) | collective-permute-done | bytes 294944 | tf_op jit(solution)/shard_map/ppermute | solution.py:234
  114.3 1.7 %shard_map.102 = bf16[128,4096]{1,0:T(8,128)(2,1)} custom-call(f32[128,4096]{1,0:T(8,128)S(1)} %get-tuple-element.54.refs_0_, bf16[504,128]{1,0:T(8,128)(2,1)S(1)} %get-tuple-element.55.refs_1_, bf16[504,128]{1,0:T(8,128)(2,1)S(1)} %get-tuple-element.56.refs_2_, bf16[72,2048]{1,0:T(8,128)(2,1)S(1)} %collective-permute-done.13.refs_9_.refs_3_, ...), custom_call_target="tpu_custom_call" | custom-call | flops 528482304 | bytes 5468160 | tf_op jit(solution)/shard_map/pallas_call | solution.py:49
  (49 shorter events, 11.7 us)
Async XLA Ops:
  0.6 43.1 %copy-start.6 = (s32[1,512,1]{1,2,0:T(1,128)S(1)}, s32[1,512,1]{1,2,0:T(1,128)}, u32[]{:S(2)}) copy-start(s32[1,512,1]{1,2,0:T(1,128)} %param.11) | copy-start | bytes 6148
  3.3 40.5 %copy-start.2 = (bf16[128,4096]{1,0:T(8,128)(2,1)S(1)}, bf16[128,4096]{1,0:T(8,128)(2,1)}, u32[]{:S(2)}) copy-start(bf16[128,4096]{1,0:T(8,128)(2,1)} %refs_1_.7) | copy-start | bytes 3145732
  3.7 15.2 %collective-permute-start.3 = (bf16[72,2048]{1,0:T(8,128)(2,1)S(1)}, bf16[72,2048]{1,0:T(8,128)(2,1)S(1)}, u32[]{:S(2)}, u32[]{:S(2)}) collective-permute-start(bf16[72,2048]{1,0:T(8,128)(2,1)S(1)} %shard_map.95.refs_3_), channel_id=1, source_target_pairs={{0,16},{4,20},{8,24},{12,28},{16,0},{20,4},{24,8},{28,12},{1,17},{... | collective-permute-start | bytes 884744 | tf_op jit(solution)/shard_map/ppermute | solution.py:234
  8.2 30.9 %collective-permute-start = (bf16[64,4096]{1,0:T(8,128)(2,1)S(1)}, bf16[64,4096]{1,0:T(8,128)(2,1)S(1)}, u32[]{:S(2)}, u32[]{:S(2)}) collective-permute-start(bf16[64,4096]{1,0:T(8,128)(2,1)S(1)} %get-tuple-element.32), channel_id=1, source_target_pairs={{0,3},{1,2},{2,1},{3,0},{4,7},{5,6},{6,5},{7,4},{8,11},{9,10},{10,... | collective-permute-start | bytes 1572872 | tf_op jit(solution)/shard_map/ppermute | solution.py:234
  10.4 33.0 %collective-permute-start.1 = (bf16[64,4096]{1,0:T(8,128)(2,1)S(1)}, bf16[64,4096]{1,0:T(8,128)(2,1)S(1)}, u32[]{:S(2)}, u32[]{:S(2)}) collective-permute-start(bf16[64,4096]{1,0:T(8,128)(2,1)S(1)} %get-tuple-element.33), channel_id=1, source_target_pairs={{0,2},{1,3},{2,0},{3,1},{4,6},{5,7},{6,4},{7,5},{8,10},{9,11},{10,... | collective-permute-start | bytes 1572872 | tf_op jit(solution)/shard_map/ppermute | solution.py:234
  11.5 26.6 %collective-permute-start.4 = (bf16[72,2048]{1,0:T(8,128)(2,1)S(1)}, bf16[72,2048]{1,0:T(8,128)(2,1)S(1)}, u32[]{:S(2)}, u32[]{:S(2)}) collective-permute-start(bf16[72,2048]{1,0:T(8,128)(2,1)S(1)} %get-tuple-element.35), channel_id=1, source_target_pairs={{0,20},{4,24},{8,28},{12,0},{16,4},{20,8},{24,12},{28,16},{1,21},{... | collective-permute-start | bytes 884744 | tf_op jit(solution)/shard_map/ppermute | solution.py:234
  12.9 25.2 %collective-permute-start.5 = (bf16[72,2048]{1,0:T(8,128)(2,1)S(1)}, bf16[72,2048]{1,0:T(8,128)(2,1)S(1)}, u32[]{:S(2)}, u32[]{:S(2)}) collective-permute-start(bf16[72,2048]{1,0:T(8,128)(2,1)S(1)} %get-tuple-element.36), channel_id=1, source_target_pairs={{0,12},{4,16},{8,20},{12,24},{16,28},{20,0},{24,4},{28,8},{1,13},{... | collective-permute-start | bytes 884744 | tf_op jit(solution)/shard_map/ppermute | solution.py:234
  19.0 24.8 %collective-permute-start.2 = (bf16[64,4096]{1,0:T(8,128)(2,1)S(1)}, bf16[64,4096]{1,0:T(8,128)(2,1)S(1)}, u32[]{:S(2)}, u32[]{:S(2)}) collective-permute-start(bf16[64,4096]{1,0:T(8,128)(2,1)S(1)} %get-tuple-element.34), channel_id=1, source_target_pairs={{0,1},{1,0},{2,3},{3,2},{4,5},{5,4},{6,7},{7,6},{8,9},{9,8},{10,11... | collective-permute-start | bytes 1572872 | tf_op jit(solution)/shard_map/ppermute | solution.py:234
  38.1 7.6 %collective-permute-start.6 = (bf16[72,2048]{1,0:T(8,128)(2,1)S(1)}, bf16[72,2048]{1,0:T(8,128)(2,1)S(1)}, u32[]{:S(2)}, u32[]{:S(2)}) collective-permute-start(bf16[72,2048]{1,0:T(8,128)(2,1)S(1)} %get-tuple-element.39), channel_id=1, source_target_pairs={{0,8},{4,12},{8,16},{12,20},{16,24},{20,28},{24,0},{28,4},{1,9},{5... | collective-permute-start | bytes 884744 | tf_op jit(solution)/shard_map/ppermute | solution.py:234
  38.1 10.1 %collective-permute-start.7 = (bf16[72,2048]{1,0:T(8,128)(2,1)S(1)}, bf16[72,2048]{1,0:T(8,128)(2,1)S(1)}, u32[]{:S(2)}, u32[]{:S(2)}) collective-permute-start(bf16[72,2048]{1,0:T(8,128)(2,1)S(1)} %get-tuple-element.40), channel_id=1, source_target_pairs={{0,28},{4,0},{8,4},{12,8},{16,12},{20,16},{24,20},{28,24},{1,29},{... | collective-permute-start | bytes 884744 | tf_op jit(solution)/shard_map/ppermute | solution.py:234
  39.1 9.1 %collective-permute-start.8 = (bf16[72,2048]{1,0:T(8,128)(2,1)S(1)}, bf16[72,2048]{1,0:T(8,128)(2,1)S(1)}, u32[]{:S(2)}, u32[]{:S(2)}) collective-permute-start(bf16[72,2048]{1,0:T(8,128)(2,1)S(1)} %get-tuple-element.41), channel_id=1, source_target_pairs={{0,24},{4,28},{8,0},{12,4},{16,8},{20,12},{24,16},{28,20},{1,25},{... | collective-permute-start | bytes 884744 | tf_op jit(solution)/shard_map/ppermute | solution.py:234
  43.4 10.2 %copy-start.8 = (s32[1,8,128,1]{2,3,1,0:T(1,128)S(1)}, s32[1,8,128,1]{2,3,1,0:T(1,128)}, u32[]{:S(2)}) copy-start(s32[1,8,128,1]{2,3,1,0:T(1,128)} %param.12) | copy-start | bytes 12292
  43.4 10.2 %copy-start.11 = (s32[128]{0:T(128)S(1)}, s32[128]{0:T(128)}, u32[]{:S(2)}) copy-start(s32[128]{0:T(128)} %param.9) | copy-start | bytes 1540
  43.4 10.2 %collective-permute-start.9 = (bf16[72,2048]{1,0:T(8,128)(2,1)S(1)}, bf16[72,2048]{1,0:T(8,128)(2,1)S(1)}, u32[]{:S(2)}, u32[]{:S(2)}) collective-permute-start(bf16[72,2048]{1,0:T(8,128)(2,1)S(1)} %get-tuple-element.42), channel_id=1, source_target_pairs={{0,4},{4,8},{8,12},{12,16},{16,20},{20,24},{24,28},{28,0},{1,5},{5... | collective-permute-start | bytes 884744 | tf_op jit(solution)/shard_map/ppermute | solution.py:234
  55.7 23.6 %collective-permute-start.13 = (bf16[72,2048]{1,0:T(8,128)(2,1)S(1)}, bf16[72,2048]{1,0:T(8,128)(2,1)S(1)}, u32[]{:S(2)}, u32[]{:S(2)}) collective-permute-start(bf16[72,2048]{1,0:T(8,128)(2,1)S(1)} %get-tuple-element.51), channel_id=1, source_target_pairs={{16,0},{20,4},{24,8},{28,12},{0,16},{4,20},{8,24},{12,28},{17,1},{... | collective-permute-start | bytes 884744 | tf_op jit(solution)/shard_map/ppermute | solution.py:234
  62.0 31.2 %collective-permute-start.10 = (bf16[64,4096]{1,0:T(8,128)(2,1)S(1)}, bf16[64,4096]{1,0:T(8,128)(2,1)S(1)}, u32[]{:S(2)}, u32[]{:S(2)}) collective-permute-start(bf16[64,4096]{1,0:T(8,128)(2,1)S(1)} %get-tuple-element.48), channel_id=1, source_target_pairs={{3,0},{2,1},{1,2},{0,3},{7,4},{6,5},{5,6},{4,7},{11,8},{10,9},{9,1... | collective-permute-start | bytes 1572872 | tf_op jit(solution)/shard_map/ppermute | solution.py:234
  64.3 28.9 %collective-permute-start.11 = (bf16[64,4096]{1,0:T(8,128)(2,1)S(1)}, bf16[64,4096]{1,0:T(8,128)(2,1)S(1)}, u32[]{:S(2)}, u32[]{:S(2)}) collective-permute-start(bf16[64,4096]{1,0:T(8,128)(2,1)S(1)} %get-tuple-element.49), channel_id=1, source_target_pairs={{2,0},{3,1},{0,2},{1,3},{6,4},{7,5},{4,6},{5,7},{10,8},{11,9},{8,1... | collective-permute-start | bytes 1572872 | tf_op jit(solution)/shard_map/ppermute | solution.py:234
  64.5 17.9 %collective-permute-start.14 = (bf16[72,2048]{1,0:T(8,128)(2,1)S(1)}, bf16[72,2048]{1,0:T(8,128)(2,1)S(1)}, u32[]{:S(2)}, u32[]{:S(2)}) collective-permute-start(bf16[72,2048]{1,0:T(8,128)(2,1)S(1)} %get-tuple-element.52), channel_id=1, source_target_pairs={{20,0},{24,4},{28,8},{0,12},{4,16},{8,20},{12,24},{16,28},{21,1},{... | collective-permute-start | bytes 884744 | tf_op jit(solution)/shard_map/ppermute | solution.py:234
  70.8 20.7 %collective-permute-start.15 = (bf16[72,2048]{1,0:T(8,128)(2,1)S(1)}, bf16[72,2048]{1,0:T(8,128)(2,1)S(1)}, u32[]{:S(2)}, u32[]{:S(2)}) collective-permute-start(bf16[72,2048]{1,0:T(8,128)(2,1)S(1)} %get-tuple-element.53), channel_id=1, source_target_pairs={{12,0},{16,4},{20,8},{24,12},{28,16},{0,20},{4,24},{8,28},{13,1},{... | collective-permute-start | bytes 884744 | tf_op jit(solution)/shard_map/ppermute | solution.py:234
  79.3 16.7 %collective-permute-start.12 = (bf16[64,4096]{1,0:T(8,128)(2,1)S(1)}, bf16[64,4096]{1,0:T(8,128)(2,1)S(1)}, u32[]{:S(2)}, u32[]{:S(2)}) collective-permute-start(bf16[64,4096]{1,0:T(8,128)(2,1)S(1)} %get-tuple-element.50), channel_id=1, source_target_pairs={{1,0},{0,1},{3,2},{2,3},{5,4},{4,5},{7,6},{6,7},{9,8},{8,9},{11,10... | collective-permute-start | bytes 1572872 | tf_op jit(solution)/shard_map/ppermute | solution.py:234
  82.4 14.6 %collective-permute-start.16 = (bf16[72,2048]{1,0:T(8,128)(2,1)S(1)}, bf16[72,2048]{1,0:T(8,128)(2,1)S(1)}, u32[]{:S(2)}, u32[]{:S(2)}) collective-permute-start(bf16[72,2048]{1,0:T(8,128)(2,1)S(1)} %get-tuple-element.57), channel_id=1, source_target_pairs={{8,0},{12,4},{16,8},{20,12},{24,16},{28,20},{0,24},{4,28},{9,1},{1... | collective-permute-start | bytes 884744 | tf_op jit(solution)/shard_map/ppermute | solution.py:234
  91.4 11.7 %collective-permute-start.17 = (bf16[72,2048]{1,0:T(8,128)(2,1)S(1)}, bf16[72,2048]{1,0:T(8,128)(2,1)S(1)}, u32[]{:S(2)}, u32[]{:S(2)}) collective-permute-start(bf16[72,2048]{1,0:T(8,128)(2,1)S(1)} %get-tuple-element.58), channel_id=1, source_target_pairs={{28,0},{0,4},{4,8},{8,12},{12,16},{16,20},{20,24},{24,28},{29,1},{... | collective-permute-start | bytes 884744 | tf_op jit(solution)/shard_map/ppermute | solution.py:234
  93.2 16.3 %collective-permute-start.18 = (bf16[72,2048]{1,0:T(8,128)(2,1)S(1)}, bf16[72,2048]{1,0:T(8,128)(2,1)S(1)}, u32[]{:S(2)}, u32[]{:S(2)}) collective-permute-start(bf16[72,2048]{1,0:T(8,128)(2,1)S(1)} %get-tuple-element.59), channel_id=1, source_target_pairs={{24,0},{28,4},{0,8},{4,12},{8,16},{12,20},{16,24},{20,28},{25,1},{... | collective-permute-start | bytes 884744 | tf_op jit(solution)/shard_map/ppermute | solution.py:234
  93.2 21.1 %collective-permute-start.19 = (bf16[72,2048]{1,0:T(8,128)(2,1)S(1)}, bf16[72,2048]{1,0:T(8,128)(2,1)S(1)}, u32[]{:S(2)}, u32[]{:S(2)}) collective-permute-start(bf16[72,2048]{1,0:T(8,128)(2,1)S(1)} %get-tuple-element.60), channel_id=1, source_target_pairs={{4,0},{8,4},{12,8},{16,12},{20,16},{24,20},{28,24},{0,28},{5,1},{9... | collective-permute-start | bytes 884744 | tf_op jit(solution)/shard_map/ppermute | solution.py:234
  (8 other events, 11.4 us)

commit v5 on v4

--- a/solution.py
+++ b/solution.py
@@ -39,7 +39,7 @@
         return slice(n * self.rows, (n + 1) * self.rows)
 
 
-def call(kernel, out_shape, *args, scratch=(), flops=0, unread=0, vmem=24):
+def call(kernel, out_shape, *args, scratch=(), flops=0, unread=0, vmem=12):
     nbytes = sum(a.size * a.dtype.itemsize for a in (*args, *jax.tree.leaves(out_shape)))
     read = len(args) - unread
 

time: 116 us -> 116 us (level)
  no operation moved by 1% of the time
where the time goes in v5:
time: 116 us
  starting transfers between devices  50.6 us (44%)
  waiting for transfers between devices  50.2 us (43%)
  Pallas kernels  10.5 us (9%)
  local copies, waits for them, and re-layouts  3.99 us (3%)
    ppermute x20, starting transfers between devices, exchange(): lax.ppermute(block, plan.axis, [(b, a) for a, b in there] if back else th...  50.6 us
    ppermute x20, waiting for transfers between devices, exchange(): lax.ppermute(block, plan.axis, [(b, a) for a, b in there] if back else th...  50.2 us
    pallas_call x9, Pallas kernels, call(): pl.pallas_call(body, out_shape=out_shape, in_specs=[VMEM] * read + [ANY]...  10.5 us
    unnamed x24, local copies, waits for them, and re-layouts  3.99 us
  transfers between devices with their start and end apart: 20, of which 10 were waited for; matrix products, arithmetic and copies ran while one was open for 0% of the time, Pallas kernels for 5%

profile of v5, /device:TPU:3, one launch (start us, length us, event | category | flops | bytes accessed | tf_op | source)
XLA Modules:
  0.0 116.0 jit_solution(4768895532182609311)
XLA Ops:
  0.7 1.2 %copy-done = bf16[128,4096]{1,0:T(8,128)(2,1)S(1)} copy-done((bf16[128,4096]{1,0:T(8,128)(2,1)S(1)}, bf16[128,4096]{1,0:T(8,128)(2,1)}, u32[]{:S(2)}) %copy-start) | copy-done | bytes 1048600
  3.7 2.4 %collective-permute-start.3 = (bf16[72,2048]{1,0:T(8,128)(2,1)S(1)}, bf16[72,2048]{1,0:T(8,128)(2,1)S(1)}, u32[]{:S(2)}, u32[]{:S(2)}) collective-permute-start(bf16[72,2048]{1,0:T(8,128)(2,1)S(1)} %shard_map.95.refs_3_), channel_id=1, source_target_pairs={{0,16},{4,20},{8,24},{12,28},{16,0},{20,4},{24,8},{28,12},{1,17},{... | collective-permute-start | bytes 884744 | tf_op jit(solution)/shard_map/ppermute | solution.py:234
  8.2 2.2 %collective-permute-start = (bf16[64,4096]{1,0:T(8,128)(2,1)S(1)}, bf16[64,4096]{1,0:T(8,128)(2,1)S(1)}, u32[]{:S(2)}, u32[]{:S(2)}) collective-permute-start(bf16[64,4096]{1,0:T(8,128)(2,1)S(1)} %get-tuple-element.32), channel_id=1, source_target_pairs={{0,3},{1,2},{2,1},{3,0},{4,7},{5,6},{6,5},{7,4},{8,11},{9,10},{10,... | collective-permute-start | bytes 1572872 | tf_op jit(solution)/shard_map/ppermute | solution.py:234
  11.5 1.4 %collective-permute-start.4 = (bf16[72,2048]{1,0:T(8,128)(2,1)S(1)}, bf16[72,2048]{1,0:T(8,128)(2,1)S(1)}, u32[]{:S(2)}, u32[]{:S(2)}) collective-permute-start(bf16[72,2048]{1,0:T(8,128)(2,1)S(1)} %get-tuple-element.35), channel_id=1, source_target_pairs={{0,20},{4,24},{8,28},{12,0},{16,4},{20,8},{24,12},{28,16},{1,21},{... | collective-permute-start | bytes 884744 | tf_op jit(solution)/shard_map/ppermute | solution.py:234
  12.9 1.9 %collective-permute-start.5 = (bf16[72,2048]{1,0:T(8,128)(2,1)S(1)}, bf16[72,2048]{1,0:T(8,128)(2,1)S(1)}, u32[]{:S(2)}, u32[]{:S(2)}) collective-permute-start(bf16[72,2048]{1,0:T(8,128)(2,1)S(1)} %get-tuple-element.36), channel_id=1, source_target_pairs={{0,12},{4,16},{8,20},{12,24},{16,28},{20,0},{24,4},{28,8},{1,13},{... | collective-permute-start | bytes 884744 | tf_op jit(solution)/shard_map/ppermute | solution.py:234
  14.8 4.2 %collective-permute-done.3.refs_7_.refs_5_ = bf16[72,2048]{1,0:T(8,128)(2,1)S(1)} collective-permute-done((bf16[72,2048]{1,0:T(8,128)(2,1)S(1)}, bf16[72,2048]{1,0:T(8,128)(2,1)S(1)}, u32[]{:S(2)}, u32[]{:S(2)}) %collective-permute-start.3) | collective-permute-done | bytes 294944 | tf_op jit(solution)/shard_map/ppermute | solution.py:234
  19.0 9.0 %collective-permute-start.2 = (bf16[64,4096]{1,0:T(8,128)(2,1)S(1)}, bf16[64,4096]{1,0:T(8,128)(2,1)S(1)}, u32[]{:S(2)}, u32[]{:S(2)}) collective-permute-start(bf16[64,4096]{1,0:T(8,128)(2,1)S(1)} %get-tuple-element.34), channel_id=1, source_target_pairs={{0,1},{1,0},{2,3},{3,2},{4,5},{5,4},{6,7},{7,6},{8,9},{9,8},{10,11... | collective-permute-start | bytes 1572872 | tf_op jit(solution)/shard_map/ppermute | solution.py:234
  27.9 10.2 %collective-permute-done.4.refs_8_.refs_6_ = bf16[72,2048]{1,0:T(8,128)(2,1)S(1)} collective-permute-done((bf16[72,2048]{1,0:T(8,128)(2,1)S(1)}, bf16[72,2048]{1,0:T(8,128)(2,1)S(1)}, u32[]{:S(2)}, u32[]{:S(2)}) %collective-permute-start.4) | collective-permute-done | bytes 294944 | tf_op jit(solution)/shard_map/ppermute | solution.py:234
  39.1 4.2 %collective-permute-start.8 = (bf16[72,2048]{1,0:T(8,128)(2,1)S(1)}, bf16[72,2048]{1,0:T(8,128)(2,1)S(1)}, u32[]{:S(2)}, u32[]{:S(2)}) collective-permute-start(bf16[72,2048]{1,0:T(8,128)(2,1)S(1)} %get-tuple-element.41), channel_id=1, source_target_pairs={{0,24},{4,28},{8,0},{12,4},{16,8},{20,12},{24,16},{28,20},{1,25},{... | collective-permute-start | bytes 884744 | tf_op jit(solution)/shard_map/ppermute | solution.py:234
  45.7 2.5 %collective-permute-done.7.refs_9_ = bf16[72,2048]{1,0:T(8,128)(2,1)S(1)} collective-permute-done((bf16[72,2048]{1,0:T(8,128)(2,1)S(1)}, bf16[72,2048]{1,0:T(8,128)(2,1)S(1)}, u32[]{:S(2)}, u32[]{:S(2)}) %collective-permute-start.7) | collective-permute-done | bytes 294944 | tf_op jit(solution)/shard_map/ppermute | solution.py:234
  48.2 5.4 %collective-permute-done.9.refs_11_ = bf16[72,2048]{1,0:T(8,128)(2,1)S(1)} collective-permute-done((bf16[72,2048]{1,0:T(8,128)(2,1)S(1)}, bf16[72,2048]{1,0:T(8,128)(2,1)S(1)}, u32[]{:S(2)}, u32[]{:S(2)}) %collective-permute-start.9) | collective-permute-done | bytes 294944 | tf_op jit(solution)/shard_map/ppermute | solution.py:234
  53.6 2.1 %shard_map.98 = (f32[1,128]{1,0:T(1,128)}, bf16[320,128]{1,0:T(8,128)(2,1)S(1)}, bf16[504,128]{1,0:T(8,128)(2,1)S(1)}, bf16[504,2048]{1,0:T(8,128)(2,1)S(1)}, bf...) custom-call(bf16[128,4096]{1,0:T(8,128)(2,1)S(1)} %copy-done.2, ...), custom_call_target="tpu_custom_call" | custom-call | flops 1056964608 | bytes 7785472 | tf_op jit(solution)/shard_map/pallas_call | solution.py:49
  55.7 5.7 %collective-permute-start.13 = (bf16[72,2048]{1,0:T(8,128)(2,1)S(1)}, bf16[72,2048]{1,0:T(8,128)(2,1)S(1)}, u32[]{:S(2)}, u32[]{:S(2)}) collective-permute-start(bf16[72,2048]{1,0:T(8,128)(2,1)S(1)} %get-tuple-element.51), channel_id=1, source_target_pairs={{16,0},{20,4},{24,8},{28,12},{0,16},{4,20},{8,24},{12,28},{17,1},{... | collective-permute-start | bytes 884744 | tf_op jit(solution)/shard_map/ppermute | solution.py:234
  62.0 2.3 %collective-permute-start.10 = (bf16[64,4096]{1,0:T(8,128)(2,1)S(1)}, bf16[64,4096]{1,0:T(8,128)(2,1)S(1)}, u32[]{:S(2)}, u32[]{:S(2)}) collective-permute-start(bf16[64,4096]{1,0:T(8,128)(2,1)S(1)} %get-tuple-element.48), channel_id=1, source_target_pairs={{3,0},{2,1},{1,2},{0,3},{7,4},{6,5},{5,6},{4,7},{11,8},{10,9},{9,1... | collective-permute-start | bytes 1572872 | tf_op jit(solution)/shard_map/ppermute | solution.py:234
  64.5 6.3 %collective-permute-start.14 = (bf16[72,2048]{1,0:T(8,128)(2,1)S(1)}, bf16[72,2048]{1,0:T(8,128)(2,1)S(1)}, u32[]{:S(2)}, u32[]{:S(2)}) collective-permute-start(bf16[72,2048]{1,0:T(8,128)(2,1)S(1)} %get-tuple-element.52), channel_id=1, source_target_pairs={{20,0},{24,4},{28,8},{0,12},{4,16},{8,20},{12,24},{16,28},{21,1},{... | collective-permute-start | bytes 884744 | tf_op jit(solution)/shard_map/ppermute | solution.py:234
  70.8 8.5 %collective-permute-done.13.refs_9_.refs_3_ = bf16[72,2048]{1,0:T(8,128)(2,1)S(1)} collective-permute-done((bf16[72,2048]{1,0:T(8,128)(2,1)S(1)}, bf16[72,2048]{1,0:T(8,128)(2,1)S(1)}, u32[]{:S(2)}, u32[]{:S(2)}) %collective-permute-start.13) | collective-permute-done | bytes 294944 | tf_op jit(solution)/shard_map/ppermute | solution.py:234
  79.3 3.1 %collective-permute-start.12 = (bf16[64,4096]{1,0:T(8,128)(2,1)S(1)}, bf16[64,4096]{1,0:T(8,128)(2,1)S(1)}, u32[]{:S(2)}, u32[]{:S(2)}) collective-permute-start(bf16[64,4096]{1,0:T(8,128)(2,1)S(1)} %get-tuple-element.50), channel_id=1, source_target_pairs={{1,0},{0,1},{3,2},{2,3},{5,4},{4,5},{7,6},{6,7},{9,8},{8,9},{11,10... | collective-permute-start | bytes 1572872 | tf_op jit(solution)/shard_map/ppermute | solution.py:234
  82.4 8.0 %collective-permute-start.16 = (bf16[72,2048]{1,0:T(8,128)(2,1)S(1)}, bf16[72,2048]{1,0:T(8,128)(2,1)S(1)}, u32[]{:S(2)}, u32[]{:S(2)}) collective-permute-start(bf16[72,2048]{1,0:T(8,128)(2,1)S(1)} %get-tuple-element.57), channel_id=1, source_target_pairs={{8,0},{12,4},{16,8},{20,12},{24,16},{28,20},{0,24},{4,28},{9,1},{1... | collective-permute-start | bytes 884744 | tf_op jit(solution)/shard_map/ppermute | solution.py:234
  91.4 1.7 %collective-permute-start.17 = (bf16[72,2048]{1,0:T(8,128)(2,1)S(1)}, bf16[72,2048]{1,0:T(8,128)(2,1)S(1)}, u32[]{:S(2)}, u32[]{:S(2)}) collective-permute-start(bf16[72,2048]{1,0:T(8,128)(2,1)S(1)} %get-tuple-element.58), channel_id=1, source_target_pairs={{28,0},{0,4},{4,8},{8,12},{12,16},{16,20},{20,24},{24,28},{29,1},{... | collective-permute-start | bytes 884744 | tf_op jit(solution)/shard_map/ppermute | solution.py:234
  93.7 2.2 %shard_map.99 = bf16[128,4096]{1,0:T(8,128)(2,1)} custom-call(bf16[320,128]{1,0:T(8,128)(2,1)S(1)} %get-tuple-element.44.refs_0_, bf16[128,4096]{1,0:T(8,128)(2,1)S(1)} %copy-done.1, bf16[192,4096]{1,0:T(8,128)(2,1)S(1)} %get-tuple-element.45.refs_2_, bf16[504,128]{1,0:T(8,128)(2,1)S(1)} %get-tuple-element.46.refs_3_, ...), custom_call_target="tpu_custom_call" | custom-call | flops 864026624 | bytes 5945344 | tf_op jit(solution)/shard_map/pallas_call | solution.py:49
  97.0 6.1 %collective-permute-done.17.refs_7_ = bf16[72,2048]{1,0:T(8,128)(2,1)S(1)} collective-permute-done((bf16[72,2048]{1,0:T(8,128)(2,1)S(1)}, bf16[72,2048]{1,0:T(8,128)(2,1)S(1)}, u32[]{:S(2)}, u32[]{:S(2)}) %collective-permute-start.17) | collective-permute-done | bytes 294944 | tf_op jit(solution)/shard_map/ppermute | solution.py:234
  103.1 6.3 %collective-permute-done.18.refs_8_ = bf16[72,2048]{1,0:T(8,128)(2,1)S(1)} collective-permute-done((bf16[72,2048]{1,0:T(8,128)(2,1)S(1)}, bf16[72,2048]{1,0:T(8,128)(2,1)S(1)}, u32[]{:S(2)}, u32[]{:S(2)}) %collective-permute-start.18) | collective-permute-done | bytes 294944 | tf_op jit(solution)/shard_map/ppermute | solution.py:234
  109.5 4.8 %collective-permute-done.19.refs_9_ = bf16[72,2048]{1,0:T(8,128)(2,1)S(1)} collective-permute-done((bf16[72,2048]{1,0:T(8,128)(2,1)S(1)}, bf16[72,2048]{1,0:T(8,128)(2,1)S(1)}, u32[]{:S(2)}, u32[]{:S(2)}) %collective-permute-start.19) | collective-permute-done | bytes 294944 | tf_op jit(solution)/shard_map/ppermute | solution.py:234
  114.3 1.7 %shard_map.102 = bf16[128,4096]{1,0:T(8,128)(2,1)} custom-call(f32[128,4096]{1,0:T(8,128)S(1)} %get-tuple-element.54.refs_0_, bf16[504,128]{1,0:T(8,128)(2,1)S(1)} %get-tuple-element.55.refs_1_, bf16[504,128]{1,0:T(8,128)(2,1)S(1)} %get-tuple-element.56.refs_2_, bf16[72,2048]{1,0:T(8,128)(2,1)S(1)} %collective-permute-done.13.refs_9_.refs_3_, ...), custom_call_target="tpu_custom_call" | custom-call | flops 528482304 | bytes 5468160 | tf_op jit(solution)/shard_map/pallas_call | solution.py:49
  (49 shorter events, 11.7 us)
Async XLA Ops:
  0.6 43.1 %copy-start.6 = (s32[1,512,1]{1,2,0:T(1,128)S(1)}, s32[1,512,1]{1,2,0:T(1,128)}, u32[]{:S(2)}) copy-start(s32[1,512,1]{1,2,0:T(1,128)} %param.11) | copy-start | bytes 6148
  3.3 40.5 %copy-start.2 = (bf16[128,4096]{1,0:T(8,128)(2,1)S(1)}, bf16[128,4096]{1,0:T(8,128)(2,1)}, u32[]{:S(2)}) copy-start(bf16[128,4096]{1,0:T(8,128)(2,1)} %refs_1_.7) | copy-start | bytes 3145732
  3.7 15.2 %collective-permute-start.3 = (bf16[72,2048]{1,0:T(8,128)(2,1)S(1)}, bf16[72,2048]{1,0:T(8,128)(2,1)S(1)}, u32[]{:S(2)}, u32[]{:S(2)}) collective-permute-start(bf16[72,2048]{1,0:T(8,128)(2,1)S(1)} %shard_map.95.refs_3_), channel_id=1, source_target_pairs={{0,16},{4,20},{8,24},{12,28},{16,0},{20,4},{24,8},{28,12},{1,17},{... | collective-permute-start | bytes 884744 | tf_op jit(solution)/shard_map/ppermute | solution.py:234
  8.2 30.9 %collective-permute-start = (bf16[64,4096]{1,0:T(8,128)(2,1)S(1)}, bf16[64,4096]{1,0:T(8,128)(2,1)S(1)}, u32[]{:S(2)}, u32[]{:S(2)}) collective-permute-start(bf16[64,4096]{1,0:T(8,128)(2,1)S(1)} %get-tuple-element.32), channel_id=1, source_target_pairs={{0,3},{1,2},{2,1},{3,0},{4,7},{5,6},{6,5},{7,4},{8,11},{9,10},{10,... | collective-permute-start | bytes 1572872 | tf_op jit(solution)/shard_map/ppermute | solution.py:234
  10.4 33.0 %collective-permute-start.1 = (bf16[64,4096]{1,0:T(8,128)(2,1)S(1)}, bf16[64,4096]{1,0:T(8,128)(2,1)S(1)}, u32[]{:S(2)}, u32[]{:S(2)}) collective-permute-start(bf16[64,4096]{1,0:T(8,128)(2,1)S(1)} %get-tuple-element.33), channel_id=1, source_target_pairs={{0,2},{1,3},{2,0},{3,1},{4,6},{5,7},{6,4},{7,5},{8,10},{9,11},{10,... | collective-permute-start | bytes 1572872 | tf_op jit(solution)/shard_map/ppermute | solution.py:234
  11.5 26.6 %collective-permute-start.4 = (bf16[72,2048]{1,0:T(8,128)(2,1)S(1)}, bf16[72,2048]{1,0:T(8,128)(2,1)S(1)}, u32[]{:S(2)}, u32[]{:S(2)}) collective-permute-start(bf16[72,2048]{1,0:T(8,128)(2,1)S(1)} %get-tuple-element.35), channel_id=1, source_target_pairs={{0,20},{4,24},{8,28},{12,0},{16,4},{20,8},{24,12},{28,16},{1,21},{... | collective-permute-start | bytes 884744 | tf_op jit(solution)/shard_map/ppermute | solution.py:234
  12.9 25.2 %collective-permute-start.5 = (bf16[72,2048]{1,0:T(8,128)(2,1)S(1)}, bf16[72,2048]{1,0:T(8,128)(2,1)S(1)}, u32[]{:S(2)}, u32[]{:S(2)}) collective-permute-start(bf16[72,2048]{1,0:T(8,128)(2,1)S(1)} %get-tuple-element.36), channel_id=1, source_target_pairs={{0,12},{4,16},{8,20},{12,24},{16,28},{20,0},{24,4},{28,8},{1,13},{... | collective-permute-start | bytes 884744 | tf_op jit(solution)/shard_map/ppermute | solution.py:234
  19.0 24.8 %collective-permute-start.2 = (bf16[64,4096]{1,0:T(8,128)(2,1)S(1)}, bf16[64,4096]{1,0:T(8,128)(2,1)S(1)}, u32[]{:S(2)}, u32[]{:S(2)}) collective-permute-start(bf16[64,4096]{1,0:T(8,128)(2,1)S(1)} %get-tuple-element.34), channel_id=1, source_target_pairs={{0,1},{1,0},{2,3},{3,2},{4,5},{5,4},{6,7},{7,6},{8,9},{9,8},{10,11... | collective-permute-start | bytes 1572872 | tf_op jit(solution)/shard_map/ppermute | solution.py:234
  38.1 7.6 %collective-permute-start.6 = (bf16[72,2048]{1,0:T(8,128)(2,1)S(1)}, bf16[72,2048]{1,0:T(8,128)(2,1)S(1)}, u32[]{:S(2)}, u32[]{:S(2)}) collective-permute-start(bf16[72,2048]{1,0:T(8,128)(2,1)S(1)} %get-tuple-element.39), channel_id=1, source_target_pairs={{0,8},{4,12},{8,16},{12,20},{16,24},{20,28},{24,0},{28,4},{1,9},{5... | collective-permute-start | bytes 884744 | tf_op jit(solution)/shard_map/ppermute | solution.py:234
  38.1 10.1 %collective-permute-start.7 = (bf16[72,2048]{1,0:T(8,128)(2,1)S(1)}, bf16[72,2048]{1,0:T(8,128)(2,1)S(1)}, u32[]{:S(2)}, u32[]{:S(2)}) collective-permute-start(bf16[72,2048]{1,0:T(8,128)(2,1)S(1)} %get-tuple-element.40), channel_id=1, source_target_pairs={{0,28},{4,0},{8,4},{12,8},{16,12},{20,16},{24,20},{28,24},{1,29},{... | collective-permute-start | bytes 884744 | tf_op jit(solution)/shard_map/ppermute | solution.py:234
  39.1 9.1 %collective-permute-start.8 = (bf16[72,2048]{1,0:T(8,128)(2,1)S(1)}, bf16[72,2048]{1,0:T(8,128)(2,1)S(1)}, u32[]{:S(2)}, u32[]{:S(2)}) collective-permute-start(bf16[72,2048]{1,0:T(8,128)(2,1)S(1)} %get-tuple-element.41), channel_id=1, source_target_pairs={{0,24},{4,28},{8,0},{12,4},{16,8},{20,12},{24,16},{28,20},{1,25},{... | collective-permute-start | bytes 884744 | tf_op jit(solution)/shard_map/ppermute | solution.py:234
  43.4 10.2 %copy-start.8 = (s32[1,8,128,1]{2,3,1,0:T(1,128)S(1)}, s32[1,8,128,1]{2,3,1,0:T(1,128)}, u32[]{:S(2)}) copy-start(s32[1,8,128,1]{2,3,1,0:T(1,128)} %param.12) | copy-start | bytes 12292
  43.4 10.2 %copy-start.11 = (s32[128]{0:T(128)S(1)}, s32[128]{0:T(128)}, u32[]{:S(2)}) copy-start(s32[128]{0:T(128)} %param.9) | copy-start | bytes 1540
  43.4 10.2 %collective-permute-start.9 = (bf16[72,2048]{1,0:T(8,128)(2,1)S(1)}, bf16[72,2048]{1,0:T(8,128)(2,1)S(1)}, u32[]{:S(2)}, u32[]{:S(2)}) collective-permute-start(bf16[72,2048]{1,0:T(8,128)(2,1)S(1)} %get-tuple-element.42), channel_id=1, source_target_pairs={{0,4},{4,8},{8,12},{12,16},{16,20},{20,24},{24,28},{28,0},{1,5},{5... | collective-permute-start | bytes 884744 | tf_op jit(solution)/shard_map/ppermute | solution.py:234
  55.7 23.6 %collective-permute-start.13 = (bf16[72,2048]{1,0:T(8,128)(2,1)S(1)}, bf16[72,2048]{1,0:T(8,128)(2,1)S(1)}, u32[]{:S(2)}, u32[]{:S(2)}) collective-permute-start(bf16[72,2048]{1,0:T(8,128)(2,1)S(1)} %get-tuple-element.51), channel_id=1, source_target_pairs={{16,0},{20,4},{24,8},{28,12},{0,16},{4,20},{8,24},{12,28},{17,1},{... | collective-permute-start | bytes 884744 | tf_op jit(solution)/shard_map/ppermute | solution.py:234
  62.0 31.2 %collective-permute-start.10 = (bf16[64,4096]{1,0:T(8,128)(2,1)S(1)}, bf16[64,4096]{1,0:T(8,128)(2,1)S(1)}, u32[]{:S(2)}, u32[]{:S(2)}) collective-permute-start(bf16[64,4096]{1,0:T(8,128)(2,1)S(1)} %get-tuple-element.48), channel_id=1, source_target_pairs={{3,0},{2,1},{1,2},{0,3},{7,4},{6,5},{5,6},{4,7},{11,8},{10,9},{9,1... | collective-permute-start | bytes 1572872 | tf_op jit(solution)/shard_map/ppermute | solution.py:234
  64.3 28.9 %collective-permute-start.11 = (bf16[64,4096]{1,0:T(8,128)(2,1)S(1)}, bf16[64,4096]{1,0:T(8,128)(2,1)S(1)}, u32[]{:S(2)}, u32[]{:S(2)}) collective-permute-start(bf16[64,4096]{1,0:T(8,128)(2,1)S(1)} %get-tuple-element.49), channel_id=1, source_target_pairs={{2,0},{3,1},{0,2},{1,3},{6,4},{7,5},{4,6},{5,7},{10,8},{11,9},{8,1... | collective-permute-start | bytes 1572872 | tf_op jit(solution)/shard_map/ppermute | solution.py:234
  64.5 17.9 %collective-permute-start.14 = (bf16[72,2048]{1,0:T(8,128)(2,1)S(1)}, bf16[72,2048]{1,0:T(8,128)(2,1)S(1)}, u32[]{:S(2)}, u32[]{:S(2)}) collective-permute-start(bf16[72,2048]{1,0:T(8,128)(2,1)S(1)} %get-tuple-element.52), channel_id=1, source_target_pairs={{20,0},{24,4},{28,8},{0,12},{4,16},{8,20},{12,24},{16,28},{21,1},{... | collective-permute-start | bytes 884744 | tf_op jit(solution)/shard_map/ppermute | solution.py:234
  70.8 20.7 %collective-permute-start.15 = (bf16[72,2048]{1,0:T(8,128)(2,1)S(1)}, bf16[72,2048]{1,0:T(8,128)(2,1)S(1)}, u32[]{:S(2)}, u32[]{:S(2)}) collective-permute-start(bf16[72,2048]{1,0:T(8,128)(2,1)S(1)} %get-tuple-element.53), channel_id=1, source_target_pairs={{12,0},{16,4},{20,8},{24,12},{28,16},{0,20},{4,24},{8,28},{13,1},{... | collective-permute-start | bytes 884744 | tf_op jit(solution)/shard_map/ppermute | solution.py:234
  79.3 16.7 %collective-permute-start.12 = (bf16[64,4096]{1,0:T(8,128)(2,1)S(1)}, bf16[64,4096]{1,0:T(8,128)(2,1)S(1)}, u32[]{:S(2)}, u32[]{:S(2)}) collective-permute-start(bf16[64,4096]{1,0:T(8,128)(2,1)S(1)} %get-tuple-element.50), channel_id=1, source_target_pairs={{1,0},{0,1},{3,2},{2,3},{5,4},{4,5},{7,6},{6,7},{9,8},{8,9},{11,10... | collective-permute-start | bytes 1572872 | tf_op jit(solution)/shard_map/ppermute | solution.py:234
  82.4 14.6 %collective-permute-start.16 = (bf16[72,2048]{1,0:T(8,128)(2,1)S(1)}, bf16[72,2048]{1,0:T(8,128)(2,1)S(1)}, u32[]{:S(2)}, u32[]{:S(2)}) collective-permute-start(bf16[72,2048]{1,0:T(8,128)(2,1)S(1)} %get-tuple-element.57), channel_id=1, source_target_pairs={{8,0},{12,4},{16,8},{20,12},{24,16},{28,20},{0,24},{4,28},{9,1},{1... | collective-permute-start | bytes 884744 | tf_op jit(solution)/shard_map/ppermute | solution.py:234
  91.4 11.7 %collective-permute-start.17 = (bf16[72,2048]{1,0:T(8,128)(2,1)S(1)}, bf16[72,2048]{1,0:T(8,128)(2,1)S(1)}, u32[]{:S(2)}, u32[]{:S(2)}) collective-permute-start(bf16[72,2048]{1,0:T(8,128)(2,1)S(1)} %get-tuple-element.58), channel_id=1, source_target_pairs={{28,0},{0,4},{4,8},{8,12},{12,16},{16,20},{20,24},{24,28},{29,1},{... | collective-permute-start | bytes 884744 | tf_op jit(solution)/shard_map/ppermute | solution.py:234
  93.2 16.3 %collective-permute-start.18 = (bf16[72,2048]{1,0:T(8,128)(2,1)S(1)}, bf16[72,2048]{1,0:T(8,128)(2,1)S(1)}, u32[]{:S(2)}, u32[]{:S(2)}) collective-permute-start(bf16[72,2048]{1,0:T(8,128)(2,1)S(1)} %get-tuple-element.59), channel_id=1, source_target_pairs={{24,0},{28,4},{0,8},{4,12},{8,16},{12,20},{16,24},{20,28},{25,1},{... | collective-permute-start | bytes 884744 | tf_op jit(solution)/shard_map/ppermute | solution.py:234
  93.2 21.1 %collective-permute-start.19 = (bf16[72,2048]{1,0:T(8,128)(2,1)S(1)}, bf16[72,2048]{1,0:T(8,128)(2,1)S(1)}, u32[]{:S(2)}, u32[]{:S(2)}) collective-permute-start(bf16[72,2048]{1,0:T(8,128)(2,1)S(1)} %get-tuple-element.60), channel_id=1, source_target_pairs={{4,0},{8,4},{12,8},{16,12},{20,16},{24,20},{28,24},{0,28},{5,1},{9... | collective-permute-start | bytes 884744 | tf_op jit(solution)/shard_map/ppermute | solution.py:234
  (8 other events, 11.4 us)

commit v6 on v5

--- a/solution.py
+++ b/solution.py
@@ -135,8 +135,7 @@
     rows = q_ref.shape[0]
     named = (owner_ref[pl.ds(me, 1), :] == me) & (row_ref[pl.ds(me, 1), :] == lax.broadcasted_iota(i32, (rows, rows), 0))
     times = 1.0 + jnp.sum(named.astype(f32), axis=1, keepdims=True)
-    times_out[:rows, :] = jnp.broadcast_to(times, (rows, rows))
-    times_out[rows:, :] = jnp.ones((plan.total, rows), f32)
+    times_out[...] = jnp.broadcast_to(times, (rows, rows))
     scores_out[:rows, :] = SCALE * dot(docs_ref[...], q_ref[...], NT)
     inner_out[...] = jnp.concatenate([block[...] for block in blocks], axis=0)
     scores = SCALE * dot(inner_out[...], q_ref[...], NT)
@@ -162,7 +161,9 @@
     scores = jnp.where(live_slots(plan, owner_ref), SCALE * jnp.concatenate(scores, axis=0), -jnp.inf)
     near = near_ref[...]
     top = jnp.maximum(jnp.max(near, axis=0, keepdims=True), jnp.max(scores, axis=0, keepdims=True))
-    near_e = times_ref[...] * jnp.exp(near - top)
+    near_e = jnp.exp(near - top)
+    own = times_ref.shape[0]
+    near_e = jnp.concatenate([times_ref[...] * near_e[:own], near_e[own:]], axis=0)
     far_e = jnp.exp(scores - top)
     total = jnp.sum(near_e, axis=0, keepdims=True)
     total = total + jnp.sum(jnp.where(chunk == 0, far_e, 0.0), axis=0, keepdims=True)
@@ -273,7 +274,7 @@
     got_inner = exchange(inner, send_inner)
     scores, times, inner_rows = call(
         functools.partial(near_kernel, inner),
-        [shape((rows + inner.total, rows), f32)] * 2 + [shape((inner.total, width), bf16)],
+        [shape((rows + inner.total, rows), f32), shape((rows, rows), f32)] + [shape((inner.total, width), bf16)],
         queries, documents, inner_owner, inner_row, *got_inner, got[0], got[1], got[2],
         flops=inner_flops + own_flops, unread=3,
     )

time: 116 us -> 116 us (level)
  no operation moved by 1% of the time
where the time goes in v6:
time: 116 us
  starting transfers between devices  50.6 us (44%)
  waiting for transfers between devices  50.2 us (43%)
  Pallas kernels  10.5 us (9%)
  local copies, waits for them, and re-layouts  3.99 us (3%)
    ppermute x20, starting transfers between devices, exchange(): lax.ppermute(block, plan.axis, [(b, a) for a, b in there] if back else th...  50.6 us
    ppermute x20, waiting for transfers between devices, exchange(): lax.ppermute(block, plan.axis, [(b, a) for a, b in there] if back else th...  50.2 us
    pallas_call x9, Pallas kernels, call(): pl.pallas_call(body, out_shape=out_shape, in_specs=[VMEM] * read + [ANY]...  10.5 us
    unnamed x24, local copies, waits for them, and re-layouts  3.99 us
  transfers between devices with their start and end apart: 20, of which 10 were waited for; matrix products, arithmetic and copies ran while one was open for 0% of the time, Pallas kernels for 5%

profile of v6, /device:TPU:3, one launch (start us, length us, event | category | flops | bytes accessed | tf_op | source)
XLA Modules:
  0.0 116.0 jit_solution(15492439157535363805)
XLA Ops:
  0.7 1.2 %copy-done = bf16[128,4096]{1,0:T(8,128)(2,1)S(1)} copy-done((bf16[128,4096]{1,0:T(8,128)(2,1)S(1)}, bf16[128,4096]{1,0:T(8,128)(2,1)}, u32[]{:S(2)}) %copy-start) | copy-done | bytes 1048600
  3.7 2.4 %collective-permute-start.3 = (bf16[72,2048]{1,0:T(8,128)(2,1)S(1)}, bf16[72,2048]{1,0:T(8,128)(2,1)S(1)}, u32[]{:S(2)}, u32[]{:S(2)}) collective-permute-start(bf16[72,2048]{1,0:T(8,128)(2,1)S(1)} %shard_map.95.refs_3_), channel_id=1, source_target_pairs={{0,16},{4,20},{8,24},{12,28},{16,0},{20,4},{24,8},{28,12},{1,17},{... | collective-permute-start | bytes 884744 | tf_op jit(solution)/shard_map/ppermute | solution.py:235
  8.2 2.2 %collective-permute-start = (bf16[64,4096]{1,0:T(8,128)(2,1)S(1)}, bf16[64,4096]{1,0:T(8,128)(2,1)S(1)}, u32[]{:S(2)}, u32[]{:S(2)}) collective-permute-start(bf16[64,4096]{1,0:T(8,128)(2,1)S(1)} %get-tuple-element.32), channel_id=1, source_target_pairs={{0,3},{1,2},{2,1},{3,0},{4,7},{5,6},{6,5},{7,4},{8,11},{9,10},{10,... | collective-permute-start | bytes 1572872 | tf_op jit(solution)/shard_map/ppermute | solution.py:235
  11.5 1.4 %collective-permute-start.4 = (bf16[72,2048]{1,0:T(8,128)(2,1)S(1)}, bf16[72,2048]{1,0:T(8,128)(2,1)S(1)}, u32[]{:S(2)}, u32[]{:S(2)}) collective-permute-start(bf16[72,2048]{1,0:T(8,128)(2,1)S(1)} %get-tuple-element.35), channel_id=1, source_target_pairs={{0,20},{4,24},{8,28},{12,0},{16,4},{20,8},{24,12},{28,16},{1,21},{... | collective-permute-start | bytes 884744 | tf_op jit(solution)/shard_map/ppermute | solution.py:235
  12.9 1.9 %collective-permute-start.5 = (bf16[72,2048]{1,0:T(8,128)(2,1)S(1)}, bf16[72,2048]{1,0:T(8,128)(2,1)S(1)}, u32[]{:S(2)}, u32[]{:S(2)}) collective-permute-start(bf16[72,2048]{1,0:T(8,128)(2,1)S(1)} %get-tuple-element.36), channel_id=1, source_target_pairs={{0,12},{4,16},{8,20},{12,24},{16,28},{20,0},{24,4},{28,8},{1,13},{... | collective-permute-start | bytes 884744 | tf_op jit(solution)/shard_map/ppermute | solution.py:235
  14.8 4.2 %collective-permute-done.3.refs_7_.refs_5_ = bf16[72,2048]{1,0:T(8,128)(2,1)S(1)} collective-permute-done((bf16[72,2048]{1,0:T(8,128)(2,1)S(1)}, bf16[72,2048]{1,0:T(8,128)(2,1)S(1)}, u32[]{:S(2)}, u32[]{:S(2)}) %collective-permute-start.3) | collective-permute-done | bytes 294944 | tf_op jit(solution)/shard_map/ppermute | solution.py:235
  19.0 9.0 %collective-permute-start.2 = (bf16[64,4096]{1,0:T(8,128)(2,1)S(1)}, bf16[64,4096]{1,0:T(8,128)(2,1)S(1)}, u32[]{:S(2)}, u32[]{:S(2)}) collective-permute-start(bf16[64,4096]{1,0:T(8,128)(2,1)S(1)} %get-tuple-element.34), channel_id=1, source_target_pairs={{0,1},{1,0},{2,3},{3,2},{4,5},{5,4},{6,7},{7,6},{8,9},{9,8},{10,11... | collective-permute-start | bytes 1572872 | tf_op jit(solution)/shard_map/ppermute | solution.py:235
  27.9 10.2 %collective-permute-done.4.refs_8_.refs_6_ = bf16[72,2048]{1,0:T(8,128)(2,1)S(1)} collective-permute-done((bf16[72,2048]{1,0:T(8,128)(2,1)S(1)}, bf16[72,2048]{1,0:T(8,128)(2,1)S(1)}, u32[]{:S(2)}, u32[]{:S(2)}) %collective-permute-start.4) | collective-permute-done | bytes 294944 | tf_op jit(solution)/shard_map/ppermute | solution.py:235
  39.1 4.2 %collective-permute-start.8 = (bf16[72,2048]{1,0:T(8,128)(2,1)S(1)}, bf16[72,2048]{1,0:T(8,128)(2,1)S(1)}, u32[]{:S(2)}, u32[]{:S(2)}) collective-permute-start(bf16[72,2048]{1,0:T(8,128)(2,1)S(1)} %get-tuple-element.41), channel_id=1, source_target_pairs={{0,24},{4,28},{8,0},{12,4},{16,8},{20,12},{24,16},{28,20},{1,25},{... | collective-permute-start | bytes 884744 | tf_op jit(solution)/shard_map/ppermute | solution.py:235
  45.7 2.5 %collective-permute-done.7.refs_9_ = bf16[72,2048]{1,0:T(8,128)(2,1)S(1)} collective-permute-done((bf16[72,2048]{1,0:T(8,128)(2,1)S(1)}, bf16[72,2048]{1,0:T(8,128)(2,1)S(1)}, u32[]{:S(2)}, u32[]{:S(2)}) %collective-permute-start.7) | collective-permute-done | bytes 294944 | tf_op jit(solution)/shard_map/ppermute | solution.py:235
  48.2 5.4 %collective-permute-done.9.refs_11_ = bf16[72,2048]{1,0:T(8,128)(2,1)S(1)} collective-permute-done((bf16[72,2048]{1,0:T(8,128)(2,1)S(1)}, bf16[72,2048]{1,0:T(8,128)(2,1)S(1)}, u32[]{:S(2)}, u32[]{:S(2)}) %collective-permute-start.9) | collective-permute-done | bytes 294944 | tf_op jit(solution)/shard_map/ppermute | solution.py:235
  53.6 2.1 %shard_map.98 = (f32[1,128]{1,0:T(1,128)}, bf16[320,128]{1,0:T(8,128)(2,1)S(1)}, bf16[504,128]{1,0:T(8,128)(2,1)S(1)}, bf16[504,2048]{1,0:T(8,128)(2,1)S(1)}, bf...) custom-call(bf16[128,4096]{1,0:T(8,128)(2,1)S(1)} %copy-done.2, ...), custom_call_target="tpu_custom_call" | custom-call | flops 1056964608 | bytes 7687168 | tf_op jit(solution)/shard_map/pallas_call | solution.py:49
  55.7 5.7 %collective-permute-start.13 = (bf16[72,2048]{1,0:T(8,128)(2,1)S(1)}, bf16[72,2048]{1,0:T(8,128)(2,1)S(1)}, u32[]{:S(2)}, u32[]{:S(2)}) collective-permute-start(bf16[72,2048]{1,0:T(8,128)(2,1)S(1)} %get-tuple-element.51), channel_id=1, source_target_pairs={{16,0},{20,4},{24,8},{28,12},{0,16},{4,20},{8,24},{12,28},{17,1},{... | collective-permute-start | bytes 884744 | tf_op jit(solution)/shard_map/ppermute | solution.py:235
  62.0 2.3 %collective-permute-start.10 = (bf16[64,4096]{1,0:T(8,128)(2,1)S(1)}, bf16[64,4096]{1,0:T(8,128)(2,1)S(1)}, u32[]{:S(2)}, u32[]{:S(2)}) collective-permute-start(bf16[64,4096]{1,0:T(8,128)(2,1)S(1)} %get-tuple-element.48), channel_id=1, source_target_pairs={{3,0},{2,1},{1,2},{0,3},{7,4},{6,5},{5,6},{4,7},{11,8},{10,9},{9,1... | collective-permute-start | bytes 1572872 | tf_op jit(solution)/shard_map/ppermute | solution.py:235
  64.5 6.3 %collective-permute-start.14 = (bf16[72,2048]{1,0:T(8,128)(2,1)S(1)}, bf16[72,2048]{1,0:T(8,128)(2,1)S(1)}, u32[]{:S(2)}, u32[]{:S(2)}) collective-permute-start(bf16[72,2048]{1,0:T(8,128)(2,1)S(1)} %get-tuple-element.52), channel_id=1, source_target_pairs={{20,0},{24,4},{28,8},{0,12},{4,16},{8,20},{12,24},{16,28},{21,1},{... | collective-permute-start | bytes 884744 | tf_op jit(solution)/shard_map/ppermute | solution.py:235
  70.8 8.5 %collective-permute-done.13.refs_9_.refs_3_ = bf16[72,2048]{1,0:T(8,128)(2,1)S(1)} collective-permute-done((bf16[72,2048]{1,0:T(8,128)(2,1)S(1)}, bf16[72,2048]{1,0:T(8,128)(2,1)S(1)}, u32[]{:S(2)}, u32[]{:S(2)}) %collective-permute-start.13) | collective-permute-done | bytes 294944 | tf_op jit(solution)/shard_map/ppermute | solution.py:235
  79.3 3.1 %collective-permute-start.12 = (bf16[64,4096]{1,0:T(8,128)(2,1)S(1)}, bf16[64,4096]{1,0:T(8,128)(2,1)S(1)}, u32[]{:S(2)}, u32[]{:S(2)}) collective-permute-start(bf16[64,4096]{1,0:T(8,128)(2,1)S(1)} %get-tuple-element.50), channel_id=1, source_target_pairs={{1,0},{0,1},{3,2},{2,3},{5,4},{4,5},{7,6},{6,7},{9,8},{8,9},{11,10... | collective-permute-start | bytes 1572872 | tf_op jit(solution)/shard_map/ppermute | solution.py:235
  82.4 8.0 %collective-permute-start.16 = (bf16[72,2048]{1,0:T(8,128)(2,1)S(1)}, bf16[72,2048]{1,0:T(8,128)(2,1)S(1)}, u32[]{:S(2)}, u32[]{:S(2)}) collective-permute-start(bf16[72,2048]{1,0:T(8,128)(2,1)S(1)} %get-tuple-element.57), channel_id=1, source_target_pairs={{8,0},{12,4},{16,8},{20,12},{24,16},{28,20},{0,24},{4,28},{9,1},{1... | collective-permute-start | bytes 884744 | tf_op jit(solution)/shard_map/ppermute | solution.py:235
  91.4 1.7 %collective-permute-start.17 = (bf16[72,2048]{1,0:T(8,128)(2,1)S(1)}, bf16[72,2048]{1,0:T(8,128)(2,1)S(1)}, u32[]{:S(2)}, u32[]{:S(2)}) collective-permute-start(bf16[72,2048]{1,0:T(8,128)(2,1)S(1)} %get-tuple-element.58), channel_id=1, source_target_pairs={{28,0},{0,4},{4,8},{8,12},{12,16},{16,20},{20,24},{24,28},{29,1},{... | collective-permute-start | bytes 884744 | tf_op jit(solution)/shard_map/ppermute | solution.py:235
  93.7 2.2 %shard_map.99 = bf16[128,4096]{1,0:T(8,128)(2,1)} custom-call(bf16[320,128]{1,0:T(8,128)(2,1)S(1)} %get-tuple-element.44.refs_0_, bf16[128,4096]{1,0:T(8,128)(2,1)S(1)} %copy-done.1, bf16[192,4096]{1,0:T(8,128)(2,1)S(1)} %get-tuple-element.45.refs_2_, bf16[504,128]{1,0:T(8,128)(2,1)S(1)} %get-tuple-element.46.refs_3_, ...), custom_call_target="tpu_custom_call" | custom-call | flops 864026624 | bytes 5945344 | tf_op jit(solution)/shard_map/pallas_call | solution.py:49
  97.0 6.1 %collective-permute-done.17.refs_7_ = bf16[72,2048]{1,0:T(8,128)(2,1)S(1)} collective-permute-done((bf16[72,2048]{1,0:T(8,128)(2,1)S(1)}, bf16[72,2048]{1,0:T(8,128)(2,1)S(1)}, u32[]{:S(2)}, u32[]{:S(2)}) %collective-permute-start.17) | collective-permute-done | bytes 294944 | tf_op jit(solution)/shard_map/ppermute | solution.py:235
  103.1 6.3 %collective-permute-done.18.refs_8_ = bf16[72,2048]{1,0:T(8,128)(2,1)S(1)} collective-permute-done((bf16[72,2048]{1,0:T(8,128)(2,1)S(1)}, bf16[72,2048]{1,0:T(8,128)(2,1)S(1)}, u32[]{:S(2)}, u32[]{:S(2)}) %collective-permute-start.18) | collective-permute-done | bytes 294944 | tf_op jit(solution)/shard_map/ppermute | solution.py:235
  109.5 4.8 %collective-permute-done.19.refs_9_ = bf16[72,2048]{1,0:T(8,128)(2,1)S(1)} collective-permute-done((bf16[72,2048]{1,0:T(8,128)(2,1)S(1)}, bf16[72,2048]{1,0:T(8,128)(2,1)S(1)}, u32[]{:S(2)}, u32[]{:S(2)}) %collective-permute-start.19) | collective-permute-done | bytes 294944 | tf_op jit(solution)/shard_map/ppermute | solution.py:235
  114.3 1.7 %shard_map.102 = bf16[128,4096]{1,0:T(8,128)(2,1)} custom-call(f32[128,4096]{1,0:T(8,128)S(1)} %get-tuple-element.54.refs_0_, bf16[504,128]{1,0:T(8,128)(2,1)S(1)} %get-tuple-element.55.refs_1_, bf16[504,128]{1,0:T(8,128)(2,1)S(1)} %get-tuple-element.56.refs_2_, bf16[72,2048]{1,0:T(8,128)(2,1)S(1)} %collective-permute-done.13.refs_9_.refs_3_, ...), custom_call_target="tpu_custom_call" | custom-call | flops 528482304 | bytes 5468160 | tf_op jit(solution)/shard_map/pallas_call | solution.py:49
  (49 shorter events, 11.8 us)
Async XLA Ops:
  0.6 43.1 %copy-start.6 = (s32[1,512,1]{1,2,0:T(1,128)S(1)}, s32[1,512,1]{1,2,0:T(1,128)}, u32[]{:S(2)}) copy-start(s32[1,512,1]{1,2,0:T(1,128)} %param.11) | copy-start | bytes 6148
  3.3 40.5 %copy-start.2 = (bf16[128,4096]{1,0:T(8,128)(2,1)S(1)}, bf16[128,4096]{1,0:T(8,128)(2,1)}, u32[]{:S(2)}) copy-start(bf16[128,4096]{1,0:T(8,128)(2,1)} %refs_1_.7) | copy-start | bytes 3145732
  3.7 15.2 %collective-permute-start.3 = (bf16[72,2048]{1,0:T(8,128)(2,1)S(1)}, bf16[72,2048]{1,0:T(8,128)(2,1)S(1)}, u32[]{:S(2)}, u32[]{:S(2)}) collective-permute-start(bf16[72,2048]{1,0:T(8,128)(2,1)S(1)} %shard_map.95.refs_3_), channel_id=1, source_target_pairs={{0,16},{4,20},{8,24},{12,28},{16,0},{20,4},{24,8},{28,12},{1,17},{... | collective-permute-start | bytes 884744 | tf_op jit(solution)/shard_map/ppermute | solution.py:235
  8.2 30.9 %collective-permute-start = (bf16[64,4096]{1,0:T(8,128)(2,1)S(1)}, bf16[64,4096]{1,0:T(8,128)(2,1)S(1)}, u32[]{:S(2)}, u32[]{:S(2)}) collective-permute-start(bf16[64,4096]{1,0:T(8,128)(2,1)S(1)} %get-tuple-element.32), channel_id=1, source_target_pairs={{0,3},{1,2},{2,1},{3,0},{4,7},{5,6},{6,5},{7,4},{8,11},{9,10},{10,... | collective-permute-start | bytes 1572872 | tf_op jit(solution)/shard_map/ppermute | solution.py:235
  10.4 33.0 %collective-permute-start.1 = (bf16[64,4096]{1,0:T(8,128)(2,1)S(1)}, bf16[64,4096]{1,0:T(8,128)(2,1)S(1)}, u32[]{:S(2)}, u32[]{:S(2)}) collective-permute-start(bf16[64,4096]{1,0:T(8,128)(2,1)S(1)} %get-tuple-element.33), channel_id=1, source_target_pairs={{0,2},{1,3},{2,0},{3,1},{4,6},{5,7},{6,4},{7,5},{8,10},{9,11},{10,... | collective-permute-start | bytes 1572872 | tf_op jit(solution)/shard_map/ppermute | solution.py:235
  11.5 26.6 %collective-permute-start.4 = (bf16[72,2048]{1,0:T(8,128)(2,1)S(1)}, bf16[72,2048]{1,0:T(8,128)(2,1)S(1)}, u32[]{:S(2)}, u32[]{:S(2)}) collective-permute-start(bf16[72,2048]{1,0:T(8,128)(2,1)S(1)} %get-tuple-element.35), channel_id=1, source_target_pairs={{0,20},{4,24},{8,28},{12,0},{16,4},{20,8},{24,12},{28,16},{1,21},{... | collective-permute-start | bytes 884744 | tf_op jit(solution)/shard_map/ppermute | solution.py:235
  12.9 25.2 %collective-permute-start.5 = (bf16[72,2048]{1,0:T(8,128)(2,1)S(1)}, bf16[72,2048]{1,0:T(8,128)(2,1)S(1)}, u32[]{:S(2)}, u32[]{:S(2)}) collective-permute-start(bf16[72,2048]{1,0:T(8,128)(2,1)S(1)} %get-tuple-element.36), channel_id=1, source_target_pairs={{0,12},{4,16},{8,20},{12,24},{16,28},{20,0},{24,4},{28,8},{1,13},{... | collective-permute-start | bytes 884744 | tf_op jit(solution)/shard_map/ppermute | solution.py:235
  19.0 24.8 %collective-permute-start.2 = (bf16[64,4096]{1,0:T(8,128)(2,1)S(1)}, bf16[64,4096]{1,0:T(8,128)(2,1)S(1)}, u32[]{:S(2)}, u32[]{:S(2)}) collective-permute-start(bf16[64,4096]{1,0:T(8,128)(2,1)S(1)} %get-tuple-element.34), channel_id=1, source_target_pairs={{0,1},{1,0},{2,3},{3,2},{4,5},{5,4},{6,7},{7,6},{8,9},{9,8},{10,11... | collective-permute-start | bytes 1572872 | tf_op jit(solution)/shard_map/ppermute | solution.py:235
  38.1 7.6 %collective-permute-start.6 = (bf16[72,2048]{1,0:T(8,128)(2,1)S(1)}, bf16[72,2048]{1,0:T(8,128)(2,1)S(1)}, u32[]{:S(2)}, u32[]{:S(2)}) collective-permute-start(bf16[72,2048]{1,0:T(8,128)(2,1)S(1)} %get-tuple-element.39), channel_id=1, source_target_pairs={{0,8},{4,12},{8,16},{12,20},{16,24},{20,28},{24,0},{28,4},{1,9},{5... | collective-permute-start | bytes 884744 | tf_op jit(solution)/shard_map/ppermute | solution.py:235
  38.1 10.1 %collective-permute-start.7 = (bf16[72,2048]{1,0:T(8,128)(2,1)S(1)}, bf16[72,2048]{1,0:T(8,128)(2,1)S(1)}, u32[]{:S(2)}, u32[]{:S(2)}) collective-permute-start(bf16[72,2048]{1,0:T(8,128)(2,1)S(1)} %get-tuple-element.40), channel_id=1, source_target_pairs={{0,28},{4,0},{8,4},{12,8},{16,12},{20,16},{24,20},{28,24},{1,29},{... | collective-permute-start | bytes 884744 | tf_op jit(solution)/shard_map/ppermute | solution.py:235
  39.1 9.1 %collective-permute-start.8 = (bf16[72,2048]{1,0:T(8,128)(2,1)S(1)}, bf16[72,2048]{1,0:T(8,128)(2,1)S(1)}, u32[]{:S(2)}, u32[]{:S(2)}) collective-permute-start(bf16[72,2048]{1,0:T(8,128)(2,1)S(1)} %get-tuple-element.41), channel_id=1, source_target_pairs={{0,24},{4,28},{8,0},{12,4},{16,8},{20,12},{24,16},{28,20},{1,25},{... | collective-permute-start | bytes 884744 | tf_op jit(solution)/shard_map/ppermute | solution.py:235
  43.4 10.2 %copy-start.8 = (s32[1,8,128,1]{2,3,1,0:T(1,128)S(1)}, s32[1,8,128,1]{2,3,1,0:T(1,128)}, u32[]{:S(2)}) copy-start(s32[1,8,128,1]{2,3,1,0:T(1,128)} %param.12) | copy-start | bytes 12292
  43.4 10.2 %copy-start.11 = (s32[128]{0:T(128)S(1)}, s32[128]{0:T(128)}, u32[]{:S(2)}) copy-start(s32[128]{0:T(128)} %param.9) | copy-start | bytes 1540
  43.4 10.2 %collective-permute-start.9 = (bf16[72,2048]{1,0:T(8,128)(2,1)S(1)}, bf16[72,2048]{1,0:T(8,128)(2,1)S(1)}, u32[]{:S(2)}, u32[]{:S(2)}) collective-permute-start(bf16[72,2048]{1,0:T(8,128)(2,1)S(1)} %get-tuple-element.42), channel_id=1, source_target_pairs={{0,4},{4,8},{8,12},{12,16},{16,20},{20,24},{24,28},{28,0},{1,5},{5... | collective-permute-start | bytes 884744 | tf_op jit(solution)/shard_map/ppermute | solution.py:235
  55.7 23.6 %collective-permute-start.13 = (bf16[72,2048]{1,0:T(8,128)(2,1)S(1)}, bf16[72,2048]{1,0:T(8,128)(2,1)S(1)}, u32[]{:S(2)}, u32[]{:S(2)}) collective-permute-start(bf16[72,2048]{1,0:T(8,128)(2,1)S(1)} %get-tuple-element.51), channel_id=1, source_target_pairs={{16,0},{20,4},{24,8},{28,12},{0,16},{4,20},{8,24},{12,28},{17,1},{... | collective-permute-start | bytes 884744 | tf_op jit(solution)/shard_map/ppermute | solution.py:235
  62.0 31.1 %collective-permute-start.10 = (bf16[64,4096]{1,0:T(8,128)(2,1)S(1)}, bf16[64,4096]{1,0:T(8,128)(2,1)S(1)}, u32[]{:S(2)}, u32[]{:S(2)}) collective-permute-start(bf16[64,4096]{1,0:T(8,128)(2,1)S(1)} %get-tuple-element.48), channel_id=1, source_target_pairs={{3,0},{2,1},{1,2},{0,3},{7,4},{6,5},{5,6},{4,7},{11,8},{10,9},{9,1... | collective-permute-start | bytes 1572872 | tf_op jit(solution)/shard_map/ppermute | solution.py:235
  64.3 28.8 %collective-permute-start.11 = (bf16[64,4096]{1,0:T(8,128)(2,1)S(1)}, bf16[64,4096]{1,0:T(8,128)(2,1)S(1)}, u32[]{:S(2)}, u32[]{:S(2)}) collective-permute-start(bf16[64,4096]{1,0:T(8,128)(2,1)S(1)} %get-tuple-element.49), channel_id=1, source_target_pairs={{2,0},{3,1},{0,2},{1,3},{6,4},{7,5},{4,6},{5,7},{10,8},{11,9},{8,1... | collective-permute-start | bytes 1572872 | tf_op jit(solution)/shard_map/ppermute | solution.py:235
  64.5 17.9 %collective-permute-start.14 = (bf16[72,2048]{1,0:T(8,128)(2,1)S(1)}, bf16[72,2048]{1,0:T(8,128)(2,1)S(1)}, u32[]{:S(2)}, u32[]{:S(2)}) collective-permute-start(bf16[72,2048]{1,0:T(8,128)(2,1)S(1)} %get-tuple-element.52), channel_id=1, source_target_pairs={{20,0},{24,4},{28,8},{0,12},{4,16},{8,20},{12,24},{16,28},{21,1},{... | collective-permute-start | bytes 884744 | tf_op jit(solution)/shard_map/ppermute | solution.py:235
  70.8 20.6 %collective-permute-start.15 = (bf16[72,2048]{1,0:T(8,128)(2,1)S(1)}, bf16[72,2048]{1,0:T(8,128)(2,1)S(1)}, u32[]{:S(2)}, u32[]{:S(2)}) collective-permute-start(bf16[72,2048]{1,0:T(8,128)(2,1)S(1)} %get-tuple-element.53), channel_id=1, source_target_pairs={{12,0},{16,4},{20,8},{24,12},{28,16},{0,20},{4,24},{8,28},{13,1},{... | collective-permute-start | bytes 884744 | tf_op jit(solution)/shard_map/ppermute | solution.py:235
  79.3 16.7 %collective-permute-start.12 = (bf16[64,4096]{1,0:T(8,128)(2,1)S(1)}, bf16[64,4096]{1,0:T(8,128)(2,1)S(1)}, u32[]{:S(2)}, u32[]{:S(2)}) collective-permute-start(bf16[64,4096]{1,0:T(8,128)(2,1)S(1)} %get-tuple-element.50), channel_id=1, source_target_pairs={{1,0},{0,1},{3,2},{2,3},{5,4},{4,5},{7,6},{6,7},{9,8},{8,9},{11,10... | collective-permute-start | bytes 1572872 | tf_op jit(solution)/shard_map/ppermute | solution.py:235
  82.4 14.6 %collective-permute-start.16 = (bf16[72,2048]{1,0:T(8,128)(2,1)S(1)}, bf16[72,2048]{1,0:T(8,128)(2,1)S(1)}, u32[]{:S(2)}, u32[]{:S(2)}) collective-permute-start(bf16[72,2048]{1,0:T(8,128)(2,1)S(1)} %get-tuple-element.57), channel_id=1, source_target_pairs={{8,0},{12,4},{16,8},{20,12},{24,16},{28,20},{0,24},{4,28},{9,1},{1... | collective-permute-start | bytes 884744 | tf_op jit(solution)/shard_map/ppermute | solution.py:235
  91.4 11.7 %collective-permute-start.17 = (bf16[72,2048]{1,0:T(8,128)(2,1)S(1)}, bf16[72,2048]{1,0:T(8,128)(2,1)S(1)}, u32[]{:S(2)}, u32[]{:S(2)}) collective-permute-start(bf16[72,2048]{1,0:T(8,128)(2,1)S(1)} %get-tuple-element.58), channel_id=1, source_target_pairs={{28,0},{0,4},{4,8},{8,12},{12,16},{16,20},{20,24},{24,28},{29,1},{... | collective-permute-start | bytes 884744 | tf_op jit(solution)/shard_map/ppermute | solution.py:235
  93.1 16.3 %collective-permute-start.18 = (bf16[72,2048]{1,0:T(8,128)(2,1)S(1)}, bf16[72,2048]{1,0:T(8,128)(2,1)S(1)}, u32[]{:S(2)}, u32[]{:S(2)}) collective-permute-start(bf16[72,2048]{1,0:T(8,128)(2,1)S(1)} %get-tuple-element.59), channel_id=1, source_target_pairs={{24,0},{28,4},{0,8},{4,12},{8,16},{12,20},{16,24},{20,28},{25,1},{... | collective-permute-start | bytes 884744 | tf_op jit(solution)/shard_map/ppermute | solution.py:235
  93.2 21.1 %collective-permute-start.19 = (bf16[72,2048]{1,0:T(8,128)(2,1)S(1)}, bf16[72,2048]{1,0:T(8,128)(2,1)S(1)}, u32[]{:S(2)}, u32[]{:S(2)}) collective-permute-start(bf16[72,2048]{1,0:T(8,128)(2,1)S(1)} %get-tuple-element.60), channel_id=1, source_target_pairs={{4,0},{8,4},{12,8},{16,12},{20,16},{24,20},{28,24},{0,28},{5,1},{9... | collective-permute-start | bytes 884744 | tf_op jit(solution)/shard_map/ppermute | solution.py:235
  (8 other events, 11.4 us)
